TPU v7x, 768 devices: a whole 4x8x12 slice. The times are simulated.
768 devices in a mesh: seq: 96 (over y, z), vocab: 8 (over x, core).
Axes of the slice: x: 4, y: 8, z: 12, core: 2. Of those that a mesh axis runs over, the one named last changes fastest.
Arguments:
- neighbour_ids: int32 [24576], P('seq'), may hold values from 0 to 122879, as said below
- table_cols: bfloat16 [896, 122880], P('vocab', 'seq')
- gain: float32 [896], replicated, may hold values from 0.1 to 1.9
- w_in: bfloat16 [896, 3584], P(None, 'vocab'), may hold values from -0.1875 to 0.1875
- w_out: bfloat16 [3584, 896], P('vocab'), may hold values from -0.09375 to 0.09375
Outputs:
- encoded: bfloat16 [896, 24576], P('vocab', 'seq')
Inputs may be any that keep to these rules, and one draw needn't show every extreme that they name: `neighbour_ids`: in each aligned block of 256 entries, at most 6 ids lie in any one range [r * 1280, (r + 1) * 1280); one range, the same for all blocks, holds exactly 6 ids of every block.
All inputs are finite; a program needn't handle non-finite values.
Results may differ from a plain program's by a relative error of at most 0.0052.
Values may be sent and summed in bfloat16 or wider, within the bound.
No kernel may reach another device: no remote copies, remote signals or barrier semaphores. Data moves between devices by JAX's collectives and lax.ppermute only.
A program may use at most 32 MiB of HBM per device.

v0:
```python
import jax
import jax.numpy as jnp
from jax import lax
from jax.sharding import PartitionSpec as P

E = 896


norm_eps = 1e-05


def on_device(neighbour_ids, table_cols, gain, w_in, w_out):
    seq_count = lax.axis_size("seq")
    tok_count = neighbour_ids.shape[0]
    feat_local = table_cols.shape[0]
    vocab_rows = table_cols.shape[1]
    capacity = max(2, 9 * tok_count // (4 * seq_count))
    owners = neighbour_ids // vocab_rows
    same_owner = owners[:, None] == owners[None, :]
    positions = jnp.arange(tok_count, dtype=jnp.int32)
    earlier = positions[None, :] < positions[:, None]
    slot_rank = jnp.sum(jnp.logical_and(same_owner, earlier), axis=1)
    slot_index = owners * capacity + slot_rank
    outgoing = jnp.full((seq_count * capacity,), -1, jnp.int32).at[slot_index].set(neighbour_ids)
    outgoing = outgoing.reshape(seq_count, capacity)
    id_block = lax.all_to_all(outgoing, "seq", split_axis=0, concat_axis=0, tiled=True)
    sources = id_block.shape[0]
    items = id_block.shape[1]
    row_base = lax.axis_index("seq") * vocab_rows
    local_rows = (id_block - row_base).reshape(-1)
    valid = id_block.reshape(-1) >= 0
    picked = jnp.take(table_cols, jnp.clip(local_rows, 0, vocab_rows - 1), axis=1)
    fetched = jnp.where(valid[None, :], picked, jnp.zeros_like(picked))
    fetched = fetched.reshape(feat_local, sources, items)
    returned = lax.all_to_all(fetched, "seq", split_axis=1, concat_axis=1, tiled=True)
    gathered = jnp.take(returned.reshape(feat_local, seq_count * capacity), slot_index, axis=1)
    widened = lax.all_gather(gathered, "vocab", axis=0, tiled=True).astype(jnp.float32)
    squares = jnp.sum(widened * widened, axis=0, keepdims=True)
    scaled = (gain[:, None] * widened).astype(jnp.bfloat16)
    accumulated = lax.dot_general(
        w_in, scaled, (((0,), (0,)), ((), ())), preferred_element_type=jnp.float32
    )
    accumulated, squares = (accumulated, squares)
    pre = accumulated * lax.rsqrt(squares / E + norm_eps)
    hidden = jax.nn.gelu(pre, approximate=True).astype(jnp.bfloat16)
    summed = lax.psum_scatter(
        lax.dot_general(
            w_out, hidden, (((0,), (0,)), ((), ())), preferred_element_type=jnp.float32
        ),
        "vocab",
        scatter_dimension=0,
        tiled=True,
    )
    return (gathered.astype(jnp.float32) + summed).astype(jnp.bfloat16)


def solution(mesh):
    in_specs = (P("seq"), P("vocab", "seq"), P(), P(None, "vocab"), P("vocab", None))
    out_specs = P("vocab", "seq")
    return jax.shard_map(
        on_device, mesh=mesh, in_specs=in_specs, out_specs=out_specs, check_vma=False
    )
```

profile of v0, /device:TPU:7, one launch (start us, length us, event | category | flops | bytes accessed | tf_op | source)
XLA Modules:
  0.0 127.9 jit_solution(14435690333468673803)
XLA Ops:
  6.5 0.8 and_select_fusion
  7.3 0.2 convert_reduce_fusion
  7.5 0.5 copy-done.1
  8.0 1.4 %scatter_custom_fusion = s32[576]{0:T(1024)S(1)} fusion(s32[256]{0:T(256)S(1)} %get-tuple-element.6, s32[256]{0:T(256)S(1)} %copy-done.1, s32[]{:T(128)} %constant.23.clone.1), kind=kCustom, calls=%fused_computation.40 | custom fusion | bytes 2308 | tf_op jit(solution)/shard_map/scatter | solution.py:24
  9.4 0.8 all_to_all.9
  10.2 21.7 %all-to-all-start = ((s32[96,1,6]{2,1,0:T(1,128)}), s32[96,1,6]{2,1,0:T(1,128)S(1)}, u32[]{:S(2)}, u32[]{:S(2)}) async-start(s32[96,1,6]{2,1,0:T(1,128)} %bitcast), calls=%async_computation | async-start | bytes 98304 | tf_op jit(solution)/shard_map/all_to_all | solution.py:26
  31.9 1.2 copy.29
  33.1 11.8 %all-to-all-done = s32[96,1,6]{2,1,0:T(1,128)S(1)} async-done(((s32[96,1,6]{2,1,0:T(1,128)}), s32[96,1,6]{2,1,0:T(1,128)S(1)}, u32[]{:S(2)}, u32[]{:S(2)}) %all-to-all-start) | async-done | bytes 2336 | tf_op jit(solution)/shard_map/all_to_all | solution.py:26
  44.9 0.1 copy.24
  45.0 0.1 copy.27
  45.1 0.1 copy.25
  45.2 0.1 copy.28
  45.3 0.1 min.18
  45.5 1.9 %gather_fusion = bf16[576,112]{1,0:T(8,128)(2,1)S(1)} fusion(bf16[112,1280]{0,1:T(8,128)(2,1)S(1)} %copy.29, s32[1024]{0:T(1024)S(1)} %pad_clamp_fusion.1), kind=kCustom, calls=%fused_computation | custom fusion | bytes 260352 | tf_op jit(solution)/shard_map/jit(_take)/gather | solution.py:32
  47.5 0.1 gather.11
  47.5 0.9 select_select_fusion
  48.5 5.9 %all-to-all-start.1 = ((bf16[112,96,6]{0,2,1:T(8,128)(2,1)}), bf16[112,96,6]{0,2,1:T(8,128)(2,1)S(1)}, u32[]{:S(2)}, u32[]{:S(2)}) async-start(bf16[112,96,6]{0,2,1:T(8,128)(2,1)} %select_select_fusion), calls=%async_computation.1 | async-start | bytes 393216 | tf_op jit(solution)/shard_map/all_to_all | solution.py:35
  54.4 0.0 reduce-scatter.4.cloned.1.call-start
  54.5 14.1 %all-to-all-done.1 = bf16[112,96,6]{0,2,1:T(8,128)(2,1)S(1)} async-done(((bf16[112,96,6]{0,2,1:T(8,128)(2,1)}), bf16[112,96,6]{0,2,1:T(8,128)(2,1)S(1)}, u32[]{:S(2)}, u32[]{:S(2)}) %all-to-all-start.1) | async-done | bytes 129056 | tf_op jit(solution)/shard_map/all_to_all | solution.py:35
  68.6 0.1 reshape.84
  68.7 0.9 gather_fusion.1
  69.6 0.1 select_bitcast_fusion
  69.7 0.1 copy.30
  69.8 16.7 %all_gather.3 = bf16[896,256]{1,0:T(8,128)(2,1)S(1)} all-gather(bf16[112,256]{1,0:T(8,128)(2,1)S(1)} %copy.30), channel_id=1, replica_groups=mesh['seq'=96,'vocab'=8] {'vocab'}, dimensions={0}, use_global_device_ids=true | all-gather | bytes 516096 | tf_op jit(solution)/shard_map/all_gather | solution.py:37
  86.5 0.2 fusion.2
  86.6 0.5 copy-done.3
  87.1 1.3 %convolution_bitcast_fusion = f32[896,256]{0,1:T(8,128)S(1)} fusion(bf16[448,896]{1,0:T(8,128)(2,1)S(1)} %copy-done, bf16[896,448]{0,1:T(8,128)(2,1)S(1)} %copy-done.2, bf16[896,256]{1,0:T(8,128)(2,1)S(1)} %all_gather.3, f32[896]{0:T(1024)S(1)} %copy-done.3, f32[256]{0:T(256)S(1)} %add_rsqrt_fusion), kind=kOutput, calls=%fused_computation.3 | convolution fusion | flops 412876800 | bytes 2986496 | tf_op jit(solution)/shard_map/dot_general | solution.py:47
  88.5 1.2 copy.32
  89.7 29.5 %reduce-scatter.4.cloned.1.call-done = f32[112,256]{1,0:T(8,128)} async-done(((f32[896,256]{1,0:T(8,128)}), f32[112,256]{1,0:T(8,128)}) %reduce-scatter.4.cloned.1.call-update) | async-done | bytes 114704
  119.2 1.0 copy.33
  120.2 0.1 add_convert_fusion
  120.3 0.7 copy.31
  (14 shorter events, 0.1 us)
Async XLA Ops:
  6.5 80.1 %copy-start = (bf16[448,896]{1,0:T(8,128)(2,1)S(1)}, bf16[448,896]{1,0:T(8,128)(2,1)}, u32[]{:S(2)}) copy-start(bf16[448,896]{1,0:T(8,128)(2,1)} %param.9) | copy-start | bytes 2408452
  7.3 0.7 copy-start.1
  10.2 34.7 %all-to-all-start = ((s32[96,1,6]{2,1,0:T(1,128)}), s32[96,1,6]{2,1,0:T(1,128)S(1)}, u32[]{:S(2)}, u32[]{:S(2)}) async-start(s32[96,1,6]{2,1,0:T(1,128)} %bitcast), calls=%async_computation | async-start | bytes 98304 | tf_op jit(solution)/shard_map/all_to_all | solution.py:26
  48.5 20.1 %all-to-all-start.1 = ((bf16[112,96,6]{0,2,1:T(8,128)(2,1)}), bf16[112,96,6]{0,2,1:T(8,128)(2,1)S(1)}, u32[]{:S(2)}, u32[]{:S(2)}) async-start(bf16[112,96,6]{0,2,1:T(8,128)(2,1)} %select_select_fusion), calls=%async_computation.1 | async-start | bytes 393216 | tf_op jit(solution)/shard_map/all_to_all | solution.py:35
  54.4 64.8 %reduce-scatter.4.cloned.1.call-start = ((), (), s32[]{:S(2)}) async-start(), calls=%async_computation.3 | async-start | bytes 1032192
  68.7 17.9 %copy-start.2 = (bf16[896,448]{0,1:T(8,128)(2,1)S(1)}, bf16[896,448]{0,1:T(8,128)(2,1)}, u32[]{:S(2)}) copy-start(bf16[896,448]{0,1:T(8,128)(2,1)} %param.8) | copy-start | bytes 2408452
  86.5 0.7 copy-start.3
Sparse Core Ops, SparseCore 0:
  89.8 29.3 reduce-scatter.3
where the time goes:
time: 128 us
  waiting for transfers between devices  55.5 us (43%)
  starting transfers between devices  27.7 us (22%)
  blocking collectives  16.7 us (13%)
  between operations  13.5 us (11%)
  local copies, waits for them, and re-layouts  10.9 us (9%)
  other arithmetic  2.33 us (2%)
  matrix products  1.31 us (1%)
    unnamed x2, waiting for transfers between devices  29.5 us
    all_to_all x1, starting transfers between devices, on_device(): lax.all_to_all(outgoing, 'seq', split_axis=0, concat_axis=0, tiled=True)  21.7 us
    all_gather x1, blocking collectives, on_device(): lax.all_gather(gathered, 'vocab', axis=0, tiled=True).astype(jnp.float32)  16.7 us
    all_to_all x1, waiting for transfers between devices, on_device(): lax.all_to_all(fetched, 'seq', split_axis=1, concat_axis=1, tiled=True)  14.1 us
    all_to_all x1, waiting for transfers between devices, on_device(): lax.all_to_all(outgoing, 'seq', split_axis=0, concat_axis=0, tiled=True)  11.8 us
    all_to_all x1, starting transfers between devices, on_device(): lax.all_to_all(fetched, 'seq', split_axis=1, concat_axis=1, tiled=True)  5.94 us
    unnamed x11, local copies, waits for them, and re-layouts  4.41 us
  transfers between devices with their start and end apart: 3, of which 3 were waited for; matrix products, arithmetic and copies ran while one was open for 1% of the time, Pallas kernels for 0%

commit v1 on v0

v1 whole, which is shorter than its diff:
```python
import functools

import jax
import jax.numpy as jnp
from jax import lax
from jax.experimental import pallas as pl
from jax.experimental.pallas import tpu as pltpu
from jax.sharding import Mesh, PartitionSpec as P

CAP = 6
SLOTS = 8
SPLIT = 64
NORM_EPS = 1e-05
F32 = jnp.float32
BF16 = jnp.bfloat16
I32 = jnp.int32


def iota(shape, dim):
    return lax.broadcasted_iota(I32, shape, dim)


def hot(mask):
    return jnp.where(mask, 1.0, 0.0).astype(BF16)


def dot(a, b, ca, cb):
    return lax.dot_general(a, b, (((ca,), (cb,)), ((), ())), preferred_element_type=F32)


def request_kernel(rows, ids_ref, out_ref, slot_ref):
    owners, toks = out_ref.shape[0], ids_ref.shape[1]
    ids = ids_ref[...]
    owner = ids // rows
    code = ids - owner * rows + 1
    mine = iota((owners, toks), 0) == owner
    mine_hot = hot(mine)
    earlier = hot(iota((toks, toks), 0) < iota((toks, toks), 1))
    count = dot(mine_hot, earlier, 1, 0)
    rank = jnp.sum(jnp.where(mine, count, 0.0), axis=0, keepdims=True).astype(I32)
    at = iota((SLOTS, toks), 0) == rank
    high = jnp.where(at, code // SPLIT, 0).astype(F32).astype(BF16)
    low = jnp.where(at, code % SPLIT, 0).astype(F32).astype(BF16)
    out = dot(mine_hot, high, 1, 1) * SPLIT + dot(mine_hot, low, 1, 1)
    out_ref[:, 0, :] = out.astype(I32)
    slot_ref[...] = owner * SLOTS + rank


def layer_kernel(block_ref, table_ref, own_ref, gain_ref, in_a, in_b, out_a, out_b,
                 part_ref, emb_ref, pick, scaled, hidden):
    sources = block_ref.shape[0]
    feats, rows = table_ref.shape
    cols = sources * CAP
    code = block_ref[:, 0, :]
    spread = hot(iota((sources, cols), 1) // CAP == iota((sources, cols), 0))
    high = (code // SPLIT).astype(F32).astype(BF16)
    low = (code % SPLIT).astype(F32).astype(BF16)
    wide = dot(high, spread, 0, 0) * SPLIT + dot(low, spread, 0, 0)
    lane = iota((SLOTS, cols), 1)
    local = jnp.sum(jnp.where(lane - (lane // CAP) * CAP == iota((SLOTS, cols), 0), wide, 0.0), axis=0, keepdims=True)
    local = local.astype(I32) - 1
    pick[...] = hot(iota((rows, cols), 0) == local)
    emb_ref[...] = dot(own_ref[...], pick[...], 1, 0).astype(BF16)
    squares = jnp.zeros((1, cols), F32)
    step = feats // 2
    for i in range(2):
        at = pl.ds(i * step, step)
        x = dot(table_ref[at, :], pick[...], 1, 0)
        squares += jnp.sum(x * x, axis=0, keepdims=True)
        scaled[at, :] = (gain_ref[at, :] * x).astype(BF16)
    scale = lax.rsqrt(squares / feats + NORM_EPS)
    half = in_a.shape[0]
    for i, w in enumerate((in_a, in_b)):
        pre = dot(w[...], scaled[...], 1, 0) * scale
        hidden[pl.ds(i * half, half), :] = jax.nn.gelu(pre, approximate=True).astype(BF16)
    total = dot(out_a[...], hidden[:half, :], 0, 0) + dot(out_b[...], hidden[half:, :], 0, 0)
    part_ref[...] = total.astype(BF16).reshape(part_ref.shape)


def finish_kernel(parts_ref, emb_ref, out_ref):
    total = emb_ref[...].astype(F32)
    for i in range(parts_ref.shape[0]):
        total += parts_ref[i].astype(F32)
    encoded = total.astype(BF16)
    cols = encoded.shape[1]
    sources = out_ref.shape[0]
    n = sources * SLOTS
    row, col = iota((n, cols), 0), iota((n, cols), 1)
    place = hot((row // SLOTS) * CAP + row % SLOTS == col)
    place = jnp.where(row % SLOTS < CAP, place, jnp.zeros_like(place))
    out_ref[...] = dot(place, encoded, 1, 1).astype(BF16).reshape(out_ref.shape)


def place_kernel(back_ref, slot_ref, out_ref):
    back = back_ref[...].reshape(-1, back_ref.shape[2])
    n, toks = back.shape[0], slot_ref.shape[1]
    pick = hot(iota((n, toks), 0) == slot_ref[...])
    out_ref[...] = dot(back, pick, 0, 0).astype(BF16)


def call(kernel, out_shape, scratch=(), vmem=32 * 1024 * 1024):
    return pl.pallas_call(
        kernel,
        out_shape=out_shape,
        scratch_shapes=list(scratch),
        compiler_params=pltpu.CompilerParams(vmem_limit_bytes=vmem),
    )


def on_device(neighbour_ids, table_cols, gain, w_in, w_out):
    seq = ("y", "z")
    owners = lax.axis_size(seq)
    chips = lax.axis_size("x")
    feat_local, rows = table_cols.shape
    feats, half = w_in.shape
    toks = neighbour_ids.shape[0]
    cols = owners * CAP
    shape = jax.ShapeDtypeStruct

    ids = neighbour_ids.reshape(1, toks)
    outgoing, slot = call(
        functools.partial(request_kernel, rows),
        (shape((owners, 1, SLOTS), I32), shape((1, toks), I32)),
    )(ids)
    table = lax.all_gather(table_cols, ("x", "core"), axis=0, tiled=True)
    block = lax.all_to_all(outgoing, seq, split_axis=0, concat_axis=0, tiled=True)

    core = lax.axis_index("core")
    swap = [(0, 1), (1, 0)]
    w_in_t = w_in.T
    by_core = w_out.reshape(half, chips, 2, feat_local)
    out_mine = lax.dynamic_index_in_dim(by_core, core, 2, False).reshape(half, chips * feat_local)
    out_send = lax.dynamic_index_in_dim(by_core, 1 - core, 2, False).reshape(half, chips * feat_local)
    in_other = lax.ppermute(w_in_t, "core", swap)
    out_other = lax.ppermute(out_send, "core", swap)

    parts, emb = call(
        layer_kernel,
        (shape((chips, feat_local, cols), BF16), shape((feat_local, cols), BF16)),
        (pltpu.VMEM((rows, cols), BF16), pltpu.VMEM((feats, cols), BF16), pltpu.VMEM((2 * half, cols), BF16)),
    )(block, table, table_cols, gain.reshape(feats, 1), w_in_t, in_other, out_mine, out_other)
    parts = lax.all_to_all(parts, "x", split_axis=0, concat_axis=0, tiled=True)
    encoded = call(finish_kernel, shape((owners, SLOTS, feat_local), BF16))(parts, emb)
    back = lax.all_to_all(encoded, seq, split_axis=0, concat_axis=0, tiled=True)
    return call(place_kernel, shape((feat_local, toks), BF16))(back, slot)


def solution(mesh):
    fine = Mesh(mesh.devices.reshape(8, 12, 4, 2), ("y", "z", "x", "core"))
    seq, vocab = ("y", "z"), ("x", "core")
    in_specs = (P(seq), P(vocab, seq), P(), P(None, vocab), P(vocab, None))
    return jax.shard_map(
        on_device, mesh=fine, in_specs=in_specs, out_specs=P(vocab, seq), check_vma=False
    )
```

time: 128 us -> 112 us (0.88)
  the two profiles are of different devices: /device:TPU:7 before, /device:TPU:8 now
where the time goes in v1:
time: 112 us
  blocking collectives  34.6 us (31%)
  starting transfers between devices  26.1 us (23%)
  local copies, waits for them, and re-layouts  16.7 us (15%)
  between operations  13.5 us (12%)
  waiting for transfers between devices  12.7 us (11%)
  Pallas kernels  7.88 us (7%)
    all_to_all x1, starting transfers between devices, on_device(): lax.all_to_all(outgoing, seq, split_axis=0, concat_axis=0, tiled=True)  21.8 us
    all_to_all x1, blocking collectives, on_device(): back = lax.all_to_all(encoded, seq, split_axis=0, concat_axis=0, tiled=True)  21.8 us
    all_to_all x1, blocking collectives, on_device(): parts = lax.all_to_all(parts, 'x', split_axis=0, concat_axis=0, tiled=True)  12.8 us
    all_to_all x1, waiting for transfers between devices, on_device(): lax.all_to_all(outgoing, seq, split_axis=0, concat_axis=0, tiled=True)  11.9 us
    dynamic_slice x1, local copies, waits for them, and re-layouts, on_device(): lax.dynamic_index_in_dim(by_core, 1 - core, 2, False)  7.22 us
    pallas_call x1, Pallas kernels, on_device(): call(layer_kernel, (shape((chips, feat_local, cols), BF16), shape((feat_l...  5.47 us
    reshape x1, local copies, waits for them, and re-layouts, on_device(): by_core = w_out.reshape(half, chips, 2, feat_local)  5.21 us
    ppermute x1, starting transfers between devices, on_device(): out_other = lax.ppermute(out_send, 'core', swap)  2.39 us
  transfers between devices with their start and end apart: 4, of which 1 were waited for; matrix products, arithmetic and copies ran while one was open for 14% of the time, Pallas kernels for 1%

profile of v1, /device:TPU:8, one launch (start us, length us, event | category | flops | bytes accessed | tf_op | source)
XLA Modules:
  0.0 111.5 jit_solution(18411264107342956670)
XLA Ops:
  6.5 0.0 all-gather.2.cloned.1.call-start
  6.5 0.7 all-gather.2.cloned.1.call-update
  7.3 1.9 %collective-permute-start = (bf16[448,896]{1,0:T(8,128)(2,1)}, bf16[448,896]{1,0:T(8,128)(2,1)S(1)}, u32[]{:S(2)}, u32[]{:S(2)}) collective-permute-start(bf16[448,896]{1,0:T(8,128)(2,1)} %bitcast.2), channel_id=1, source_target_pairs={{0,1},{1,0},{2,3},{3,2},{4,5},{5,4},{6,7},{7,6},{8,9},{9,8},{10,11... | collective-permute-start | bytes 2408456 | tf_op jit(solution)/shard_map/ppermute | solution.py:134
  9.2 0.0 copy-start.3
  9.2 5.2 %reshape.19 = bf16[448,4,2,112]{3,2,1,0:T(2,128)(2,1)S(1)} reshape(bf16[448,896]{1,0:T(8,128)(2,1)} %param.9) | data formatting | bytes 1605632 | tf_op jit(solution)/shard_map/reshape | solution.py:131
  14.4 0.0 copy-start.4
  14.4 0.0 copy-start.1
  14.4 0.0 copy-start.2
  14.5 7.2 %dynamic-slice_reduce_fusion = (bf16[448,4,112]{2,1,0:T(4,128)(2,1)S(1)}, bf16[448,4,112]{2,1,0:T(4,128)(2,1)}) fusion(bf16[448,4,2,112]{3,2,1,0:T(2,128)(2,1)S(1)} %reshape.19, s32[]{:T(128)S(6)} %select_n.8, s32[]{:T(128)S(6)} %select_n.7), kind=kLoop, calls=%fused_computation | loop fusion | bytes 1605640 | tf_op jit(solution)/shard_map/jit(dynamic_index_in_dim)/dynamic_slice | solution.py:133
  21.7 1.1 reshape.21
  22.8 2.4 %collective-permute-start.1 = (bf16[448,448]{1,0:T(8,128)(2,1)}, bf16[448,448]{1,0:T(8,128)(2,1)S(1)}, u32[]{:S(2)}, u32[]{:S(2)}) collective-permute-start(bf16[448,448]{1,0:T(8,128)(2,1)} %reshape.21), channel_id=1, source_target_pairs={{0,1},{1,0},{2,3},{3,2},{4,5},{5,4},{6,7},{7,6},{8,9},{9,8},{10,11... | collective-permute-start | bytes 1204232 | tf_op jit(solution)/shard_map/ppermute | solution.py:135
  25.2 0.0 copy-done.3
  25.2 1.0 shard_map.55
  26.1 21.8 %all-to-all-start = ((s32[96,1,8]{2,1,0:T(1,128)}), s32[96,1,8]{2,1,0:T(1,128)S(1)}, u32[]{:S(2)}, u32[]{:S(2)}) async-start(s32[96,1,8]{2,1,0:T(1,128)} %get-tuple-element.9), calls=%async_computation | async-start | bytes 98304 | tf_op jit(solution)/shard_map/all_to_all | solution.py:126
  47.9 1.4 %reshape.20.out_a = bf16[448,448]{1,0:T(8,128)(2,1)S(1)} reshape(bf16[448,4,112]{2,1,0:T(4,128)(2,1)} %get-tuple-element.14) | data formatting | bytes 802816 | tf_op jit(solution)/shard_map/reshape | solution.py:132
  49.3 0.0 copy-done.4
  49.3 0.2 reshape.22.gain_ref
  49.5 11.9 %all-to-all-done.block_ref = s32[96,1,8]{2,1,0:T(1,128)S(1)} async-done(((s32[96,1,8]{2,1,0:T(1,128)}), s32[96,1,8]{2,1,0:T(1,128)S(1)}, u32[]{:S(2)}, u32[]{:S(2)}) %all-to-all-start) | async-done | bytes 3104 | tf_op jit(solution)/shard_map/all_to_all | solution.py:126
  61.4 0.0 collective-permute-done.1.out_b
  61.4 0.0 collective-permute-done.in_b
  61.4 0.0 all-gather.2.cloned.1.call-done.table_ref
  61.5 0.0 copy-done.1
  61.5 0.0 copy-done.2
  61.5 0.0 copy-start
  61.5 1.6 %copy-done = bf16[896,1280]{1,0:T(8,128)(2,1)S(1)} copy-done((bf16[896,1280]{1,0:T(8,128)(2,1)S(1)}, bf16[896,1280]{1,0:T(8,128)(2,1)}, u32[]{:S(2)}) %copy-start) | copy-done | bytes 2293784
  63.1 5.5 %shard_map.56 = (bf16[4,112,576]{2,1,0:T(8,128)(2,1)S(1)}, bf16[112,576]{1,0:T(8,128)(2,1)S(1)}) custom-call(s32[96,1,8]{2,1,0:T(1,128)S(1)} %all-to-all-done.block_ref, bf16[896,1280]{1,0:T(8,128)(2,1)S(1)} %copy-done, bf16[112,1280]{1,0:T(8,128)(2,1)S(1)} %copy-done.1, f32[896,1]{1,0:T(8,128)S(1)} %reshape.22.gain_ref, bf16[448,896]{1,0:T(8,128)(2,1)S(1)} %bitcast.3, ...), custom_call_target="tpu_custom_call" | custom-call | tf_op jit(solution)/shard_map/pallas_call | solution.py:137
  68.6 12.8 %all_to_all.15.parts_ref = bf16[4,112,576]{2,1,0:T(8,128)(2,1)S(1)} all-to-all(bf16[4,112,576]{2,1,0:T(8,128)(2,1)S(1)} %get-tuple-element.10), channel_id=1, replica_groups=mesh['y'=8,'z'=12,'x'=4,'core'=2] {'x'}, dimensions={0} | all-to-all | bytes 1032192 | tf_op jit(solution)/shard_map/all_to_all | solution.py:142
  81.4 0.6 shard_map.57
  82.0 21.8 %all_to_all.16.back_ref = bf16[96,8,112]{2,1,0:T(8,128)(2,1)S(1)} all-to-all(bf16[96,8,112]{2,1,0:T(8,128)(2,1)S(1)} %shard_map.57), channel_id=1, replica_groups=mesh['y'=8,'z'=12,'x'=4,'core'=2] {'y','z'}, dimensions={0} | all-to-all | bytes 344064 | tf_op jit(solution)/shard_map/all_to_all | solution.py:144
  103.8 0.9 shard_map.58
Async XLA Ops:
  6.5 54.9 %all-gather.2.cloned.1.call-start = ((), (), s32[]{:S(2)}) async-start(), calls=%async_computation.3 | async-start | bytes 2580480 | tf_op jit(solution)/shard_map/all_gather | solution.py:125
  7.3 54.2 %collective-permute-start = (bf16[448,896]{1,0:T(8,128)(2,1)}, bf16[448,896]{1,0:T(8,128)(2,1)S(1)}, u32[]{:S(2)}, u32[]{:S(2)}) collective-permute-start(bf16[448,896]{1,0:T(8,128)(2,1)} %bitcast.2), channel_id=1, source_target_pairs={{0,1},{1,0},{2,3},{3,2},{4,5},{5,4},{6,7},{7,6},{8,9},{9,8},{10,11... | collective-permute-start | bytes 2408456 | tf_op jit(solution)/shard_map/ppermute | solution.py:134
  9.2 16.0 %copy-start.3 = (s32[256]{0:T(256)S(1)}, s32[256]{0:T(256)}, u32[]{:S(2)}) copy-start(s32[256]{0:T(256)} %param.5) | copy-start | bytes 3076
  14.4 34.9 %copy-start.4 = (f32[896]{0:T(1024)S(1)}, f32[896]{0:T(1024)}, u32[]{:S(2)}) copy-start(f32[896]{0:T(1024)} %param.7) | copy-start | bytes 10756
  14.4 47.0 %copy-start.1 = (bf16[112,1280]{1,0:T(8,128)(2,1)S(1)}, bf16[112,1280]{1,0:T(8,128)(2,1)}, u32[]{:S(2)}) copy-start(bf16[112,1280]{1,0:T(8,128)(2,1)} %own_ref.1) | copy-start | bytes 860164
  14.4 47.0 %copy-start.2 = (bf16[896,448]{0,1:T(8,128)(2,1)S(1)}, bf16[896,448]{0,1:T(8,128)(2,1)}, u32[]{:S(2)}) copy-start(bf16[896,448]{0,1:T(8,128)(2,1)} %param.8) | copy-start | bytes 2408452
  22.8 38.7 %collective-permute-start.1 = (bf16[448,448]{1,0:T(8,128)(2,1)}, bf16[448,448]{1,0:T(8,128)(2,1)S(1)}, u32[]{:S(2)}, u32[]{:S(2)}) collective-permute-start(bf16[448,448]{1,0:T(8,128)(2,1)} %reshape.21), channel_id=1, source_target_pairs={{0,1},{1,0},{2,3},{3,2},{4,5},{5,4},{6,7},{7,6},{8,9},{9,8},{10,11... | collective-permute-start | bytes 1204232 | tf_op jit(solution)/shard_map/ppermute | solution.py:135
  26.1 35.3 %all-to-all-start = ((s32[96,1,8]{2,1,0:T(1,128)}), s32[96,1,8]{2,1,0:T(1,128)S(1)}, u32[]{:S(2)}, u32[]{:S(2)}) async-start(s32[96,1,8]{2,1,0:T(1,128)} %get-tuple-element.9), calls=%async_computation | async-start | bytes 98304 | tf_op jit(solution)/shard_map/all_to_all | solution.py:126
  61.5 1.6 %copy-start = (bf16[896,1280]{1,0:T(8,128)(2,1)S(1)}, bf16[896,1280]{1,0:T(8,128)(2,1)}, u32[]{:S(2)}) copy-start(bf16[896,1280]{1,0:T(8,128)(2,1)} %all-gather.2.cloned.1.call-done.table_ref) | copy-start | bytes 6881284
Sparse Core Ops, SparseCore 0:
  9.8 40.1 all-gather.1

commit v2 on v1

--- a/solution.py
+++ b/solution.py
@@ -46,10 +46,35 @@
     slot_ref[...] = owner * SLOTS + rank
 
 
-def layer_kernel(block_ref, table_ref, own_ref, gain_ref, in_a, in_b, out_a, out_b,
-                 part_ref, emb_ref, pick, scaled, hidden):
+def third(r, block, count):
+    return sum((r >= k * block).astype(I32) for k in range(1, count))
+
+
+def blocks_kernel(w_ref, mine_ref, send_ref):
+    core = lax.axis_index("core")
+    n, m = mine_ref.shape[0], w_ref.shape[1]
+    row, lane = iota((n, m), 0), iota((n, m), 1)
+    block = n // lax.axis_size("x")
+    base = row + third(row, block, n // block) * block
+    w = w_ref[...]
+    mine_ref[...] = dot(hot(lane == base + core * block), w, 1, 1).astype(BF16)
+    send_ref[...] = dot(hot(lane == base + (1 - core) * block), w, 1, 1).astype(BF16)
+
+
+def order_kernel(*refs):
+    out_ref = refs[-1]
+    chips = out_ref.shape[0]
+    me = lax.axis_index("x")
+    for k, ref in enumerate(refs[:-1]):
+        out_ref[lax.rem(me - k + chips, chips)] = ref[...]
+
+
+def layer_kernel(block_ref, mine_ref, other_ref, gain_ref, in_a, in_b, out_a, out_b,
+                 part_ref, emb_ref, pick, scaled, hidden, own):
+    core, chip = lax.axis_index("core"), lax.axis_index("x")
     sources = block_ref.shape[0]
-    feats, rows = table_ref.shape
+    chips, step, rows = mine_ref.shape
+    feats = 2 * chips * step
     cols = sources * CAP
     code = block_ref[:, 0, :]
     spread = hot(iota((sources, cols), 1) // CAP == iota((sources, cols), 0))
@@ -60,20 +85,23 @@
     local = jnp.sum(jnp.where(lane - (lane // CAP) * CAP == iota((SLOTS, cols), 0), wide, 0.0), axis=0, keepdims=True)
     local = local.astype(I32) - 1
     pick[...] = hot(iota((rows, cols), 0) == local)
-    emb_ref[...] = dot(own_ref[...], pick[...], 1, 0).astype(BF16)
     squares = jnp.zeros((1, cols), F32)
-    step = feats // 2
-    for i in range(2):
-        at = pl.ds(i * step, step)
-        x = dot(table_ref[at, :], pick[...], 1, 0)
+    for ref, side in ((mine_ref, core), (other_ref, 1 - core)):
+        x = dot(ref[...].reshape(chips * step, rows), pick[...], 1, 0)
         squares += jnp.sum(x * x, axis=0, keepdims=True)
-        scaled[at, :] = (gain_ref[at, :] * x).astype(BF16)
+        for i in range(chips):
+            part = x[i * step:(i + 1) * step]
+            at = pl.ds(pl.multiple_of((2 * i + side) * step, 16), step)
+            scaled[at, :] = (gain_ref[at, :] * part).astype(BF16)
+            if ref is mine_ref:
+                own[i] = part.astype(BF16)
+    emb_ref[...] = own[chip]
     scale = lax.rsqrt(squares / feats + NORM_EPS)
     half = in_a.shape[0]
     for i, w in enumerate((in_a, in_b)):
         pre = dot(w[...], scaled[...], 1, 0) * scale
         hidden[pl.ds(i * half, half), :] = jax.nn.gelu(pre, approximate=True).astype(BF16)
-    total = dot(out_a[...], hidden[:half, :], 0, 0) + dot(out_b[...], hidden[half:, :], 0, 0)
+    total = dot(out_a[...], hidden[:half, :], 1, 0) + dot(out_b[...], hidden[half:, :], 1, 0)
     part_ref[...] = total.astype(BF16).reshape(part_ref.shape)
 
 
@@ -118,27 +146,37 @@
     shape = jax.ShapeDtypeStruct
 
     ids = neighbour_ids.reshape(1, toks)
+    behind = [
+        lax.ppermute(table_cols, "x", [(i, (i + k) % chips) for i in range(chips)])
+        for k in range(1, chips)
+    ]
     outgoing, slot = call(
         functools.partial(request_kernel, rows),
         (shape((owners, 1, SLOTS), I32), shape((1, toks), I32)),
     )(ids)
-    table = lax.all_gather(table_cols, ("x", "core"), axis=0, tiled=True)
     block = lax.all_to_all(outgoing, seq, split_axis=0, concat_axis=0, tiled=True)
 
-    core = lax.axis_index("core")
     swap = [(0, 1), (1, 0)]
     w_in_t = w_in.T
-    by_core = w_out.reshape(half, chips, 2, feat_local)
-    out_mine = lax.dynamic_index_in_dim(by_core, core, 2, False).reshape(half, chips * feat_local)
-    out_send = lax.dynamic_index_in_dim(by_core, 1 - core, 2, False).reshape(half, chips * feat_local)
-    in_other = lax.ppermute(w_in_t, "core", swap)
+    w_out, _ = lax.optimization_barrier((w_out, slot))
+    w_swap, _ = lax.optimization_barrier((w_in_t, slot))
+    out_mine, out_send = call(blocks_kernel, (shape((chips * feat_local, half), BF16),) * 2)(w_out)
+    in_other = lax.ppermute(w_swap, "core", swap)
     out_other = lax.ppermute(out_send, "core", swap)
+    own_table, _ = lax.optimization_barrier((table_cols, slot))
+    mine = call(order_kernel, shape((chips, feat_local, rows), BF16))(own_table, *behind)
+    other = lax.ppermute(mine, "core", swap)
 
     parts, emb = call(
         layer_kernel,
         (shape((chips, feat_local, cols), BF16), shape((feat_local, cols), BF16)),
-        (pltpu.VMEM((rows, cols), BF16), pltpu.VMEM((feats, cols), BF16), pltpu.VMEM((2 * half, cols), BF16)),
-    )(block, table, table_cols, gain.reshape(feats, 1), w_in_t, in_other, out_mine, out_other)
+        (
+            pltpu.VMEM((rows, cols), BF16),
+            pltpu.VMEM((feats, cols), BF16),
+            pltpu.VMEM((2 * half, cols), BF16),
+            pltpu.VMEM((chips, feat_local, cols), BF16),
+        ),
+    )(block, mine, other, gain.reshape(feats, 1), w_in_t, in_other, out_mine, out_other)
     parts = lax.all_to_all(parts, "x", split_axis=0, concat_axis=0, tiled=True)
     encoded = call(finish_kernel, shape((owners, SLOTS, feat_local), BF16))(parts, emb)
     back = lax.all_to_all(encoded, seq, split_axis=0, concat_axis=0, tiled=True)

time: 112 us -> 110 us (0.982)
  between operations: 13.5 us -> 0.14 us
  starting transfers between devices: 26.1 us -> 39.1 us
  local copies, waits for them, and re-layouts: 16.7 us -> 4.84 us
  waiting for transfers between devices: 12.7 us -> 18.9 us
  Pallas kernels: 7.88 us -> 11.1 us
    ppermute x1 -> x5, starting transfers between devices: 1.92 us -> 15.1 us  [the longest x3 10.8 us: on_device(): lax.ppermute(table_cols, 'x', [(i, (i + k) % chips) for i in range(chips)])]
    reshape x3 -> x0, local copies, waits for them, and re-layouts: 7.67 us -> none  [the longest x1 5.21 us: on_device(): by_core = w_out.reshape(half, chips, 2, feat_local)]
    dynamic_slice x1 -> x0, local copies, waits for them, and re-layouts: 7.22 us -> none  [on_device(): lax.dynamic_index_in_dim(by_core, 1 - core, 2, False)]
    ppermute x1 -> x5, waiting for transfers between devices: 0.01 us -> 6.35 us  [the longest x3 6.34 us: on_device(): lax.ppermute(table_cols, 'x', [(i, (i + k) % chips) for i in range(chips)])]
    unnamed x10 -> x16, local copies, waits for them, and re-layouts: 1.66 us -> 3.98 us
    pallas_call x0 -> x2, Pallas kernels: none -> 2.01 us  [the longest x1 1.91 us: on_device(): call(blocks_kernel, (shape((chips * feat_local, half), BF16),) * 2)(w_out)]
    pallas_call x1, Pallas kernels: 5.47 us -> 6.68 us  [on_device(): call(layer_kernel, (shape((chips, feat_local, cols), BF16), shape((feat_l...]
  transfers between devices with their start and end apart: 4 -> 7, of which waited for: 1 -> 2; matrix products, arithmetic and copies ran while one was open for 14% -> 1% of each run, Pallas kernels for 1% -> 3%
where the time goes in v2:
time: 110 us; the launch traced here: 109 us
  starting transfers between devices  39.1 us (36%)
  blocking collectives  35.3 us (32%)
  waiting for transfers between devices  18.9 us (17%)
  Pallas kernels  11.1 us (10%)
  local copies, waits for them, and re-layouts  4.84 us (4%)
    all_to_all x1, starting transfers between devices, on_device(): lax.all_to_all(outgoing, seq, split_axis=0, concat_axis=0, tiled=True)  22.1 us
    all_to_all x1, blocking collectives, on_device(): back = lax.all_to_all(encoded, seq, split_axis=0, concat_axis=0, tiled=True)  21.5 us
    all_to_all x1, blocking collectives, on_device(): parts = lax.all_to_all(parts, 'x', split_axis=0, concat_axis=0, tiled=True)  13.8 us
    all_to_all x1, waiting for transfers between devices, on_device(): lax.all_to_all(outgoing, seq, split_axis=0, concat_axis=0, tiled=True)  12.6 us
    ppermute x3, starting transfers between devices, on_device(): lax.ppermute(table_cols, 'x', [(i, (i + k) % chips) for i in range(chips)])  10.8 us
    pallas_call x1, Pallas kernels, on_device(): call(layer_kernel, (shape((chips, feat_local, cols), BF16), shape((feat_l...  6.68 us
    ppermute x3, waiting for transfers between devices, on_device(): lax.ppermute(table_cols, 'x', [(i, (i + k) % chips) for i in range(chips)])  6.34 us
    unnamed x16, local copies, waits for them, and re-layouts  3.98 us
  transfers between devices with their start and end apart: 7, of which 2 were waited for; matrix products, arithmetic and copies ran while one was open for 1% of the time, Pallas kernels for 3%

profile of v2, /device:TPU:8, one launch (start us, length us, event | category | flops | bytes accessed | tf_op | source)
XLA Modules:
  0.0 109.5 jit_solution(3035069414899865242)
XLA Ops:
  0.0 3.4 %collective-permute-start = (bf16[112,1280]{1,0:T(8,128)(2,1)}, bf16[112,1280]{1,0:T(8,128)(2,1)S(1)}, u32[]{:S(2)}, u32[]{:S(2)}) collective-permute-start(bf16[112,1280]{1,0:T(8,128)(2,1)} %refs_0_), channel_id=1, source_target_pairs={{0,2},{2,4},{4,6},{6,0},{1,3},{3,5},{5,7},{7,1},{8,10},{10,12},{12... | collective-permute-start | bytes 860168 | tf_op jit(solution)/shard_map/ppermute | solution.py:150
  3.4 3.7 %collective-permute-start.2 = (bf16[112,1280]{1,0:T(8,128)(2,1)}, bf16[112,1280]{1,0:T(8,128)(2,1)S(1)}, u32[]{:S(2)}, u32[]{:S(2)}) collective-permute-start(bf16[112,1280]{1,0:T(8,128)(2,1)} %refs_0_), channel_id=1, source_target_pairs={{0,6},{2,0},{4,2},{6,4},{1,7},{3,1},{5,3},{7,5},{8,14},{10,8},{12,... | collective-permute-start | bytes 860168 | tf_op jit(solution)/shard_map/ppermute | solution.py:150
  7.1 3.7 %collective-permute-start.1 = (bf16[112,1280]{1,0:T(8,128)(2,1)}, bf16[112,1280]{1,0:T(8,128)(2,1)S(1)}, u32[]{:S(2)}, u32[]{:S(2)}) collective-permute-start(bf16[112,1280]{1,0:T(8,128)(2,1)} %refs_0_), channel_id=1, source_target_pairs={{0,4},{2,6},{4,0},{6,2},{1,5},{3,7},{5,1},{7,3},{8,12},{10,14},{12... | collective-permute-start | bytes 860168 | tf_op jit(solution)/shard_map/ppermute | solution.py:150
  10.8 0.0 copy-start.7
  10.8 0.7 copy-done.7
  11.5 1.0 shard_map.55
  12.5 0.5 copy-done.5
  13.0 0.0 collective-permute-done.refs_1_
  13.0 6.3 %collective-permute-done.2.refs_3_ = bf16[112,1280]{1,0:T(8,128)(2,1)S(1)} collective-permute-done((bf16[112,1280]{1,0:T(8,128)(2,1)}, bf16[112,1280]{1,0:T(8,128)(2,1)S(1)}, u32[]{:S(2)}, u32[]{:S(2)}) %collective-permute-start.2) | collective-permute-done | bytes 286752 | tf_op jit(solution)/shard_map/ppermute | solution.py:150
  19.3 0.0 collective-permute-done.1.refs_2_
  19.3 1.0 copy-done.4
  20.3 0.1 shard_map.56.mine_ref
  20.4 1.9 %collective-permute-start.3 = (bf16[4,112,1280]{2,1,0:T(8,128)(2,1)S(1)}, bf16[4,112,1280]{2,1,0:T(8,128)(2,1)S(1)}, u32[]{:S(2)}, u32[]{:S(2)}) collective-permute-start(bf16[4,112,1280]{2,1,0:T(8,128)(2,1)S(1)} %shard_map.56.mine_ref), channel_id=1, source_target_pairs={{0,1},{1,0},{2,3},{3,2},{4,5},{5,4},{6,7},{7,6},{8,9},{9,8},{10,11... | collective-permute-start | bytes 3440648 | tf_op jit(solution)/shard_map/ppermute | solution.py:168
  22.3 0.0 copy-done.1
  22.3 2.4 %collective-permute-start.4 = (bf16[448,896]{1,0:T(8,128)(2,1)S(1)}, bf16[448,896]{1,0:T(8,128)(2,1)}, u32[]{:S(2)}, u32[]{:S(2)}) collective-permute-start(bf16[448,896]{1,0:T(8,128)(2,1)S(1)} %bitcast.2), channel_id=1, source_target_pairs={{0,1},{1,0},{2,3},{3,2},{4,5},{5,4},{6,7},{7,6},{8,9},{9,8},{10,11... | collective-permute-start | bytes 2408456 | tf_op jit(solution)/shard_map/ppermute | solution.py:164
  24.8 0.0 copy-done
  24.8 1.9 %shard_map.57 = (bf16[448,448]{1,0:T(8,128)(2,1)S(1)}, bf16[448,448]{1,0:T(8,128)(2,1)}) custom-call(bf16[448,896]{1,0:T(8,128)(2,1)S(1)} %copy-done), custom_call_target="tpu_custom_call" | custom-call | tf_op jit(solution)/shard_map/pallas_call | solution.py:163
  26.7 0.8 copy-done.2
  27.5 1.9 %collective-permute-start.5 = (bf16[448,448]{1,0:T(8,128)(2,1)}, bf16[448,448]{1,0:T(8,128)(2,1)}, u32[]{:S(2)}, u32[]{:S(2)}) collective-permute-start(bf16[448,448]{1,0:T(8,128)(2,1)} %get-tuple-element.20), channel_id=1, source_target_pairs={{0,1},{1,0},{2,3},{3,2},{4,5},{5,4},{6,7},{7,6},{8,9},{9,8},{10,11... | collective-permute-start | bytes 1204232 | tf_op jit(solution)/shard_map/ppermute | solution.py:165
  29.4 22.1 %all-to-all-start = ((s32[96,1,8]{2,1,0:T(1,128)}), s32[96,1,8]{2,1,0:T(1,128)}, u32[]{:S(2)}, u32[]{:S(2)}) async-start(s32[96,1,8]{2,1,0:T(1,128)} %get-tuple-element.14), calls=%async_computation | async-start | bytes 98304 | tf_op jit(solution)/shard_map/all_to_all | solution.py:157
  51.5 0.9 reshape.8.gain_ref
  52.4 12.6 %all-to-all-done.block_ref = s32[96,1,8]{2,1,0:T(1,128)} async-done(((s32[96,1,8]{2,1,0:T(1,128)}), s32[96,1,8]{2,1,0:T(1,128)}, u32[]{:S(2)}, u32[]{:S(2)}) %all-to-all-start) | async-done | bytes 3104 | tf_op jit(solution)/shard_map/all_to_all | solution.py:157
  65.0 0.0 collective-permute-done.5.out_b
  65.0 0.0 collective-permute-done.4.in_b
  65.0 0.0 collective-permute-done.3.other_ref
  65.0 1.0 copy-done.3
  66.0 6.7 %shard_map.58 = (bf16[4,112,576]{2,1,0:T(8,128)(2,1)S(1)}, bf16[112,576]{1,0:T(8,128)(2,1)S(1)}) custom-call(s32[96,1,8]{2,1,0:T(1,128)} %all-to-all-done.block_ref, bf16[4,112,1280]{2,1,0:T(8,128)(2,1)S(1)} %shard_map.56.mine_ref, bf16[4,112,1280]{2,1,0:T(8,128)(2,1)S(1)} %collective-permute-done.3.other_ref, f32[896,1]{1,0:T(8,128)S(1)} %reshape.8.gain_ref, ...), custom_call_target="tpu_custom_call" | custom-call | tf_op jit(solution)/shard_map/pallas_call | solution.py:170
  72.7 13.8 %all_to_all.15.parts_ref = bf16[4,112,576]{2,1,0:T(8,128)(2,1)S(1)} all-to-all(bf16[4,112,576]{2,1,0:T(8,128)(2,1)S(1)} %get-tuple-element.21), channel_id=1, replica_groups=mesh['y'=8,'z'=12,'x'=4,'core'=2] {'x'}, dimensions={0} | all-to-all | bytes 1032192 | tf_op jit(solution)/shard_map/all_to_all | solution.py:180
  86.5 0.6 shard_map.59
  87.1 21.5 %all_to_all.16.back_ref = bf16[96,8,112]{2,1,0:T(8,128)(2,1)S(1)} all-to-all(bf16[96,8,112]{2,1,0:T(8,128)(2,1)S(1)} %shard_map.59), channel_id=1, replica_groups=mesh['y'=8,'z'=12,'x'=4,'core'=2] {'y','z'}, dimensions={0} | all-to-all | bytes 344064 | tf_op jit(solution)/shard_map/all_to_all | solution.py:182
  108.6 0.0 copy-done.6
  108.6 0.9 shard_map.60
  (7 shorter events, 0.0 us)
Async XLA Ops:
  0.0 13.0 %collective-permute-start = (bf16[112,1280]{1,0:T(8,128)(2,1)}, bf16[112,1280]{1,0:T(8,128)(2,1)S(1)}, u32[]{:S(2)}, u32[]{:S(2)}) collective-permute-start(bf16[112,1280]{1,0:T(8,128)(2,1)} %refs_0_), channel_id=1, source_target_pairs={{0,2},{2,4},{4,6},{6,0},{1,3},{3,5},{5,7},{7,1},{8,10},{10,12},{12... | collective-permute-start | bytes 860168 | tf_op jit(solution)/shard_map/ppermute | solution.py:150
  3.4 15.9 %collective-permute-start.2 = (bf16[112,1280]{1,0:T(8,128)(2,1)}, bf16[112,1280]{1,0:T(8,128)(2,1)S(1)}, u32[]{:S(2)}, u32[]{:S(2)}) collective-permute-start(bf16[112,1280]{1,0:T(8,128)(2,1)} %refs_0_), channel_id=1, source_target_pairs={{0,6},{2,0},{4,2},{6,4},{1,7},{3,1},{5,3},{7,5},{8,14},{10,8},{12,... | collective-permute-start | bytes 860168 | tf_op jit(solution)/shard_map/ppermute | solution.py:150
  7.1 12.3 %collective-permute-start.1 = (bf16[112,1280]{1,0:T(8,128)(2,1)}, bf16[112,1280]{1,0:T(8,128)(2,1)S(1)}, u32[]{:S(2)}, u32[]{:S(2)}) collective-permute-start(bf16[112,1280]{1,0:T(8,128)(2,1)} %refs_0_), channel_id=1, source_target_pairs={{0,4},{2,6},{4,0},{6,2},{1,5},{3,7},{5,1},{7,3},{8,12},{10,14},{12... | collective-permute-start | bytes 860168 | tf_op jit(solution)/shard_map/ppermute | solution.py:150
  10.8 0.7 copy-start.7
  12.5 0.5 copy-start.5
  13.0 9.3 %copy-start.1 = (bf16[896,448]{0,1:T(8,128)(2,1)S(1)}, bf16[896,448]{0,1:T(8,128)(2,1)}, u32[]{:S(2)}) copy-start(bf16[896,448]{0,1:T(8,128)(2,1)} %param.8) | copy-start | bytes 2408452
  13.0 11.8 %copy-start = (bf16[448,896]{1,0:T(8,128)(2,1)S(1)}, bf16[448,896]{1,0:T(8,128)(2,1)}, u32[]{:S(2)}) copy-start(bf16[448,896]{1,0:T(8,128)(2,1)} %w_ref) | copy-start | bytes 2408452
  19.3 1.0 copy-start.4
  20.4 44.6 %collective-permute-start.3 = (bf16[4,112,1280]{2,1,0:T(8,128)(2,1)S(1)}, bf16[4,112,1280]{2,1,0:T(8,128)(2,1)S(1)}, u32[]{:S(2)}, u32[]{:S(2)}) collective-permute-start(bf16[4,112,1280]{2,1,0:T(8,128)(2,1)S(1)} %shard_map.56.mine_ref), channel_id=1, source_target_pairs={{0,1},{1,0},{2,3},{3,2},{4,5},{5,4},{6,7},{7,6},{8,9},{9,8},{10,11... | collective-permute-start | bytes 3440648 | tf_op jit(solution)/shard_map/ppermute | solution.py:168
  22.3 42.6 %collective-permute-start.4 = (bf16[448,896]{1,0:T(8,128)(2,1)S(1)}, bf16[448,896]{1,0:T(8,128)(2,1)}, u32[]{:S(2)}, u32[]{:S(2)}) collective-permute-start(bf16[448,896]{1,0:T(8,128)(2,1)S(1)} %bitcast.2), channel_id=1, source_target_pairs={{0,1},{1,0},{2,3},{3,2},{4,5},{5,4},{6,7},{7,6},{8,9},{9,8},{10,11... | collective-permute-start | bytes 2408456 | tf_op jit(solution)/shard_map/ppermute | solution.py:164
  26.7 0.8 copy-start.2
  27.5 37.5 %collective-permute-start.5 = (bf16[448,448]{1,0:T(8,128)(2,1)}, bf16[448,448]{1,0:T(8,128)(2,1)}, u32[]{:S(2)}, u32[]{:S(2)}) collective-permute-start(bf16[448,448]{1,0:T(8,128)(2,1)} %get-tuple-element.20), channel_id=1, source_target_pairs={{0,1},{1,0},{2,3},{3,2},{4,5},{5,4},{6,7},{7,6},{8,9},{9,8},{10,11... | collective-permute-start | bytes 1204232 | tf_op jit(solution)/shard_map/ppermute | solution.py:165
  29.4 35.6 %all-to-all-start = ((s32[96,1,8]{2,1,0:T(1,128)}), s32[96,1,8]{2,1,0:T(1,128)}, u32[]{:S(2)}, u32[]{:S(2)}) async-start(s32[96,1,8]{2,1,0:T(1,128)} %get-tuple-element.14), calls=%async_computation | async-start | bytes 98304 | tf_op jit(solution)/shard_map/all_to_all | solution.py:157
  65.0 1.0 copy-start.3
  72.7 35.9 %copy-start.6 = (s32[1,256]{1,0:T(1,128)S(1)}, s32[1,256]{1,0:T(1,128)}, u32[]{:S(2)}) copy-start(s32[1,256]{1,0:T(1,128)} %copy-done.5) | copy-start | bytes 3076

commit v3 on v2

--- a/solution.py
+++ b/solution.py
@@ -28,29 +28,33 @@
     return lax.dot_general(a, b, (((ca,), (cb,)), ((), ())), preferred_element_type=F32)
 
 
-def request_kernel(rows, ids_ref, out_ref, slot_ref):
-    owners, toks = out_ref.shape[0], ids_ref.shape[1]
-    ids = ids_ref[...]
+def ranked(ids, owners, rows):
+    toks = ids.shape[1]
     owner = ids // rows
-    code = ids - owner * rows + 1
     mine = iota((owners, toks), 0) == owner
     mine_hot = hot(mine)
     earlier = hot(iota((toks, toks), 0) < iota((toks, toks), 1))
     count = dot(mine_hot, earlier, 1, 0)
     rank = jnp.sum(jnp.where(mine, count, 0.0), axis=0, keepdims=True).astype(I32)
-    at = iota((SLOTS, toks), 0) == rank
+    return owner, ids - owner * rows + 1, rank, mine_hot
+
+
+def request_kernel(rows, ids_ref, out_ref):
+    owner, code, rank, mine_hot = ranked(ids_ref[...], out_ref.shape[0], rows)
+    at = iota((SLOTS, ids_ref.shape[1]), 0) == rank
     high = jnp.where(at, code // SPLIT, 0).astype(F32).astype(BF16)
     low = jnp.where(at, code % SPLIT, 0).astype(F32).astype(BF16)
     out = dot(mine_hot, high, 1, 1) * SPLIT + dot(mine_hot, low, 1, 1)
     out_ref[:, 0, :] = out.astype(I32)
-    slot_ref[...] = owner * SLOTS + rank
 
 
 def third(r, block, count):
     return sum((r >= k * block).astype(I32) for k in range(1, count))
 
 
-def blocks_kernel(w_ref, mine_ref, send_ref):
+def blocks_kernel(owners, rows, w_ref, ids_ref, mine_ref, send_ref, slot_ref):
+    owner, _, rank, _ = ranked(ids_ref[...], owners, rows)
+    slot_ref[...] = owner * SLOTS + rank
     core = lax.axis_index("core")
     n, m = mine_ref.shape[0], w_ref.shape[1]
     row, lane = iota((n, m), 0), iota((n, m), 1)
@@ -69,13 +73,9 @@
         out_ref[lax.rem(me - k + chips, chips)] = ref[...]
 
 
-def layer_kernel(block_ref, mine_ref, other_ref, gain_ref, in_a, in_b, out_a, out_b,
-                 part_ref, emb_ref, pick, scaled, hidden, own):
-    core, chip = lax.axis_index("core"), lax.axis_index("x")
+def pick_kernel(block_ref, pick_ref):
     sources = block_ref.shape[0]
-    chips, step, rows = mine_ref.shape
-    feats = 2 * chips * step
-    cols = sources * CAP
+    rows, cols = pick_ref.shape
     code = block_ref[:, 0, :]
     spread = hot(iota((sources, cols), 1) // CAP == iota((sources, cols), 0))
     high = (code // SPLIT).astype(F32).astype(BF16)
@@ -84,7 +84,15 @@
     lane = iota((SLOTS, cols), 1)
     local = jnp.sum(jnp.where(lane - (lane // CAP) * CAP == iota((SLOTS, cols), 0), wide, 0.0), axis=0, keepdims=True)
     local = local.astype(I32) - 1
-    pick[...] = hot(iota((rows, cols), 0) == local)
+    pick_ref[...] = hot(iota((rows, cols), 0) == local)
+
+
+def layer_kernel(pick, mine_ref, other_ref, gain_ref, in_a, in_b, out_a, out_b,
+                 part_ref, emb_ref, scaled, hidden, own):
+    core, chip = lax.axis_index("core"), lax.axis_index("x")
+    chips, step, rows = mine_ref.shape
+    feats = 2 * chips * step
+    cols = pick.shape[1]
     squares = jnp.zeros((1, cols), F32)
     for ref, side in ((mine_ref, core), (other_ref, 1 - core)):
         x = dot(ref[...].reshape(chips * step, rows), pick[...], 1, 0)
@@ -126,11 +134,12 @@
     out_ref[...] = dot(back, pick, 0, 0).astype(BF16)
 
 
-def call(kernel, out_shape, scratch=(), vmem=32 * 1024 * 1024):
+def call(kernel, out_shape, scratch=(), vmem=32 * 1024 * 1024, flops=None):
     return pl.pallas_call(
         kernel,
         out_shape=out_shape,
         scratch_shapes=list(scratch),
+        cost_estimate=flops and pl.CostEstimate(flops=flops, bytes_accessed=0, transcendentals=0),
         compiler_params=pltpu.CompilerParams(vmem_limit_bytes=vmem),
     )
 
@@ -150,33 +159,30 @@
         lax.ppermute(table_cols, "x", [(i, (i + k) % chips) for i in range(chips)])
         for k in range(1, chips)
     ]
-    outgoing, slot = call(
-        functools.partial(request_kernel, rows),
-        (shape((owners, 1, SLOTS), I32), shape((1, toks), I32)),
-    )(ids)
+    outgoing = call(functools.partial(request_kernel, rows), shape((owners, 1, SLOTS), I32))(ids)
     block = lax.all_to_all(outgoing, seq, split_axis=0, concat_axis=0, tiled=True)
 
     swap = [(0, 1), (1, 0)]
     w_in_t = w_in.T
-    w_out, _ = lax.optimization_barrier((w_out, slot))
-    w_swap, _ = lax.optimization_barrier((w_in_t, slot))
-    out_mine, out_send = call(blocks_kernel, (shape((chips * feat_local, half), BF16),) * 2)(w_out)
-    in_other = lax.ppermute(w_swap, "core", swap)
+    out_mine, out_send, slot = call(
+        functools.partial(blocks_kernel, owners, rows),
+        (shape((chips * feat_local, half), BF16),) * 2 + (shape((1, toks), I32),),
+    )(w_out, ids)
+    in_other = lax.ppermute(w_in_t, "core", swap)
     out_other = lax.ppermute(out_send, "core", swap)
-    own_table, _ = lax.optimization_barrier((table_cols, slot))
-    mine = call(order_kernel, shape((chips, feat_local, rows), BF16))(own_table, *behind)
+    mine = call(order_kernel, shape((chips, feat_local, rows), BF16))(table_cols, *behind)
     other = lax.ppermute(mine, "core", swap)
 
+    pick = call(pick_kernel, shape((rows, cols), BF16), flops=30_000_000_000)(block)
     parts, emb = call(
         layer_kernel,
         (shape((chips, feat_local, cols), BF16), shape((feat_local, cols), BF16)),
         (
-            pltpu.VMEM((rows, cols), BF16),
             pltpu.VMEM((feats, cols), BF16),
             pltpu.VMEM((2 * half, cols), BF16),
             pltpu.VMEM((chips, feat_local, cols), BF16),
         ),
-    )(block, mine, other, gain.reshape(feats, 1), w_in_t, in_other, out_mine, out_other)
+    )(pick, mine, other, gain.reshape(feats, 1), w_in_t, in_other, out_mine, out_other)
     parts = lax.all_to_all(parts, "x", split_axis=0, concat_axis=0, tiled=True)
     encoded = call(finish_kernel, shape((owners, SLOTS, feat_local), BF16))(parts, emb)
     back = lax.all_to_all(encoded, seq, split_axis=0, concat_axis=0, tiled=True)

time: 110 us -> 102 us (0.927)
  waiting for transfers between devices: 18.9 us -> 2.2 us
  blocking collectives: 35.3 us -> 42.8 us
  local copies, waits for them, and re-layouts: 4.84 us -> 3.37 us
  Pallas kernels: 11.1 us -> 12.5 us
  starting transfers between devices: 39.1 us -> 40.5 us
    all_to_all x1, waiting for transfers between devices: 12.6 us -> 2.19 us  [on_device(): lax.all_to_all(outgoing, seq, split_axis=0, concat_axis=0, tiled=True)]
    all_to_all x1, blocking collectives: 21.5 us -> 31.5 us  [on_device(): back = lax.all_to_all(encoded, seq, split_axis=0, concat_axis=0, tiled=True)]
    ppermute x3, waiting for transfers between devices: 6.34 us -> 0.01 us  [on_device(): lax.ppermute(table_cols, 'x', [(i, (i + k) % chips) for i in range(chips)])]
    all_to_all x1, blocking collectives: 13.8 us -> 11.3 us  [on_device(): parts = lax.all_to_all(parts, 'x', split_axis=0, concat_axis=0, tiled=True)]
    pallas_call x2 -> x3, Pallas kernels: 2.9 us -> 5.16 us  [the longest x1 2.23 us: on_device(): call(pick_kernel, shape((rows, cols), BF16), flops=30000000000)(block)]
    unnamed x16 -> x18, local copies, waits for them, and re-layouts: 3.98 us -> 2.51 us
    ppermute x3, starting transfers between devices: 10.8 us -> 12 us  [on_device(): lax.ppermute(table_cols, 'x', [(i, (i + k) % chips) for i in range(chips)])]
  transfers between devices with their start and end apart: 7 -> 7, of which waited for: 2 -> 1; matrix products, arithmetic and copies ran while one was open for 1% -> 1% of each run, Pallas kernels for 3% -> 5%
where the time goes in v3:
time: 102 us; the launch traced here: 101 us
  blocking collectives  42.8 us (42%)
  starting transfers between devices  40.5 us (40%)
  Pallas kernels  12.5 us (12%)
  local copies, waits for them, and re-layouts  3.37 us (3%)
  waiting for transfers between devices  2.2 us (2%)
    all_to_all x1, blocking collectives, on_device(): back = lax.all_to_all(encoded, seq, split_axis=0, concat_axis=0, tiled=True)  31.5 us
    all_to_all x1, starting transfers between devices, on_device(): lax.all_to_all(outgoing, seq, split_axis=0, concat_axis=0, tiled=True)  22.1 us
    ppermute x3, starting transfers between devices, on_device(): lax.ppermute(table_cols, 'x', [(i, (i + k) % chips) for i in range(chips)])  12 us
    all_to_all x1, blocking collectives, on_device(): parts = lax.all_to_all(parts, 'x', split_axis=0, concat_axis=0, tiled=True)  11.3 us
    pallas_call x1, Pallas kernels, on_device(): call(layer_kernel, (shape((chips, feat_local, cols), BF16), shape((feat_l...  5.8 us
    unnamed x18, local copies, waits for them, and re-layouts  2.51 us
    ppermute x1, starting transfers between devices, on_device(): out_other = lax.ppermute(out_send, 'core', swap)  2.4 us
    pallas_call x1, Pallas kernels, on_device(): call(pick_kernel, shape((rows, cols), BF16), flops=30000000000)(block)  2.23 us
  transfers between devices with their start and end apart: 7, of which 1 were waited for; matrix products, arithmetic and copies ran while one was open for 1% of the time, Pallas kernels for 5%

profile of v3, /device:TPU:8, one launch (start us, length us, event | category | flops | bytes accessed | tf_op | source)
XLA Modules:
  0.0 101.5 jit_solution(5481407797918550022)
XLA Ops:
  0.0 4.9 %collective-permute-start.1 = (bf16[112,1280]{1,0:T(8,128)(2,1)}, bf16[112,1280]{1,0:T(8,128)(2,1)S(1)}, u32[]{:S(2)}, u32[]{:S(2)}) collective-permute-start(bf16[112,1280]{1,0:T(8,128)(2,1)} %refs_0_.1), channel_id=1, source_target_pairs={{0,4},{2,6},{4,0},{6,2},{1,5},{3,7},{5,1},{7,3},{8,12},{10,14},{12... | collective-permute-start | bytes 860168 | tf_op jit(solution)/shard_map/ppermute | solution.py:159
  4.9 2.5 %collective-permute-start = (bf16[112,1280]{1,0:T(8,128)(2,1)}, bf16[112,1280]{1,0:T(8,128)(2,1)S(1)}, u32[]{:S(2)}, u32[]{:S(2)}) collective-permute-start(bf16[112,1280]{1,0:T(8,128)(2,1)} %refs_0_.1), channel_id=1, source_target_pairs={{0,2},{2,4},{4,6},{6,0},{1,3},{3,5},{5,7},{7,1},{8,10},{10,12},{12... | collective-permute-start | bytes 860168 | tf_op jit(solution)/shard_map/ppermute | solution.py:159
  7.4 4.6 %collective-permute-start.2 = (bf16[112,1280]{1,0:T(8,128)(2,1)}, bf16[112,1280]{1,0:T(8,128)(2,1)S(1)}, u32[]{:S(2)}, u32[]{:S(2)}) collective-permute-start(bf16[112,1280]{1,0:T(8,128)(2,1)} %refs_0_.1), channel_id=1, source_target_pairs={{0,6},{2,0},{4,2},{6,4},{1,7},{3,1},{5,3},{7,5},{8,14},{10,8},{12,... | collective-permute-start | bytes 860168 | tf_op jit(solution)/shard_map/ppermute | solution.py:159
  12.0 0.0 copy-start.5
  12.0 0.7 copy-done.5
  12.7 1.0 shard_map.55
  13.7 22.1 %all-to-all-start = ((s32[96,1,8]{2,1,0:T(1,128)}), s32[96,1,8]{2,1,0:T(1,128)}, u32[]{:S(2)}, u32[]{:S(2)}) async-start(s32[96,1,8]{2,1,0:T(1,128)} %shard_map.55), calls=%async_computation | async-start | bytes 98304 | tf_op jit(solution)/shard_map/all_to_all | solution.py:163
  35.8 1.9 %collective-permute-start.4 = (bf16[448,896]{1,0:T(8,128)(2,1)}, bf16[448,896]{1,0:T(8,128)(2,1)}, u32[]{:S(2)}, u32[]{:S(2)}) collective-permute-start(bf16[448,896]{1,0:T(8,128)(2,1)} %bitcast.2), channel_id=1, source_target_pairs={{0,1},{1,0},{2,3},{3,2},{4,5},{5,4},{6,7},{7,6},{8,9},{9,8},{10,11... | collective-permute-start | bytes 2408456 | tf_op jit(solution)/shard_map/ppermute | solution.py:171
  37.7 0.0 copy-start
  37.7 1.1 %copy-done = bf16[448,896]{1,0:T(8,128)(2,1)S(1)} copy-done((bf16[448,896]{1,0:T(8,128)(2,1)S(1)}, bf16[448,896]{1,0:T(8,128)(2,1)}, u32[]{:S(2)}) %copy-start) | copy-done | bytes 802840
  38.9 0.7 copy-done.6
  39.5 1.9 %shard_map.58 = (bf16[448,448]{1,0:T(8,128)(2,1)S(1)}, bf16[448,448]{1,0:T(8,128)(2,1)}, s32[1,256]{1,0:T(1,128)S(1)}) custom-call(bf16[448,896]{1,0:T(8,128)(2,1)S(1)} %copy-done, s32[1,256]{1,0:T(1,128)S(1)} %bitcast.5), custom_call_target="tpu_custom_call" | custom-call | tf_op jit(solution)/shard_map/pallas_call | solution.py:167
  41.5 2.4 %collective-permute-start.5 = (bf16[448,448]{1,0:T(8,128)(2,1)}, bf16[448,448]{1,0:T(8,128)(2,1)}, u32[]{:S(2)}, u32[]{:S(2)}) collective-permute-start(bf16[448,448]{1,0:T(8,128)(2,1)} %get-tuple-element.11), channel_id=1, source_target_pairs={{0,1},{1,0},{2,3},{3,2},{4,5},{5,4},{6,7},{7,6},{8,9},{9,8},{10,11... | collective-permute-start | bytes 1204232 | tf_op jit(solution)/shard_map/ppermute | solution.py:172
  43.9 0.9 reshape.8.gain_ref
  44.8 0.0 collective-permute-done.1.refs_2_
  44.8 0.0 collective-permute-done.refs_1_
  44.8 0.0 copy-done.2
  44.8 0.0 collective-permute-done.2.refs_3_
  44.8 0.0 copy-done.4
  44.8 0.1 shard_map.57.mine_ref
  44.9 0.0 copy-start.1
  44.9 2.1 %collective-permute-start.3 = (bf16[4,112,1280]{2,1,0:T(8,128)(2,1)S(1)}, bf16[4,112,1280]{2,1,0:T(8,128)(2,1)S(1)}, u32[]{:S(2)}, u32[]{:S(2)}) collective-permute-start(bf16[4,112,1280]{2,1,0:T(8,128)(2,1)S(1)} %shard_map.57.mine_ref), channel_id=1, source_target_pairs={{0,1},{1,0},{2,3},{3,2},{4,5},{5,4},{6,7},{7,6},{8,9},{9,8},{10,11... | collective-permute-start | bytes 3440648 | tf_op jit(solution)/shard_map/ppermute | solution.py:174
  47.0 2.2 %all-to-all-done.block_ref = s32[96,1,8]{2,1,0:T(1,128)} async-done(((s32[96,1,8]{2,1,0:T(1,128)}), s32[96,1,8]{2,1,0:T(1,128)}, u32[]{:S(2)}, u32[]{:S(2)}) %all-to-all-start) | async-done | bytes 3104 | tf_op jit(solution)/shard_map/all_to_all | solution.py:163
  49.2 2.2 %shard_map.56.pick = bf16[1280,576]{1,0:T(8,128)(2,1)S(1)} custom-call(s32[96,1,8]{2,1,0:T(1,128)} %all-to-all-done.block_ref), custom_call_target="tpu_custom_call" | custom-call | flops 30000001024 | tf_op jit(solution)/shard_map/pallas_call | solution.py:176
  51.4 0.0 collective-permute-done.5.out_b
  51.4 0.0 collective-permute-done.4.in_b
  51.4 0.0 collective-permute-done.3.other_ref
  51.5 5.8 %shard_map.59 = (bf16[4,112,576]{2,1,0:T(8,128)(2,1)S(1)}, bf16[112,576]{1,0:T(8,128)(2,1)S(1)}) custom-call(bf16[1280,576]{1,0:T(8,128)(2,1)S(1)} %shard_map.56.pick, bf16[4,112,1280]{2,1,0:T(8,128)(2,1)S(1)} %shard_map.57.mine_ref, bf16[4,112,1280]{2,1,0:T(8,128)(2,1)S(1)} %collective-permute-done.3.other_ref, f32[896,1]{1,0:T(8,128)S(1)} %reshape.8.gain_ref, ...), custom_call_target="tpu_custom_call" | custom-call | tf_op jit(solution)/shard_map/pallas_call | solution.py:177
  57.3 11.3 %all_to_all.15.parts_ref = bf16[4,112,576]{2,1,0:T(8,128)(2,1)S(1)} all-to-all(bf16[4,112,576]{2,1,0:T(8,128)(2,1)S(1)} %get-tuple-element.12), channel_id=1, replica_groups=mesh['y'=8,'z'=12,'x'=4,'core'=2] {'x'}, dimensions={0} | all-to-all | bytes 1032192 | tf_op jit(solution)/shard_map/all_to_all | solution.py:186
  68.6 0.6 shard_map.60
  69.1 31.5 %all_to_all.16.back_ref = bf16[96,8,112]{2,1,0:T(8,128)(2,1)S(1)} all-to-all(bf16[96,8,112]{2,1,0:T(8,128)(2,1)S(1)} %shard_map.60), channel_id=1, replica_groups=mesh['y'=8,'z'=12,'x'=4,'core'=2] {'y','z'}, dimensions={0} | all-to-all | bytes 344064 | tf_op jit(solution)/shard_map/all_to_all | solution.py:188
  100.6 0.9 shard_map.61
  (10 shorter events, 0.0 us)
Async XLA Ops:
  0.0 44.8 %collective-permute-start.1 = (bf16[112,1280]{1,0:T(8,128)(2,1)}, bf16[112,1280]{1,0:T(8,128)(2,1)S(1)}, u32[]{:S(2)}, u32[]{:S(2)}) collective-permute-start(bf16[112,1280]{1,0:T(8,128)(2,1)} %refs_0_.1), channel_id=1, source_target_pairs={{0,4},{2,6},{4,0},{6,2},{1,5},{3,7},{5,1},{7,3},{8,12},{10,14},{12... | collective-permute-start | bytes 860168 | tf_op jit(solution)/shard_map/ppermute | solution.py:159
  4.9 39.8 %collective-permute-start = (bf16[112,1280]{1,0:T(8,128)(2,1)}, bf16[112,1280]{1,0:T(8,128)(2,1)S(1)}, u32[]{:S(2)}, u32[]{:S(2)}) collective-permute-start(bf16[112,1280]{1,0:T(8,128)(2,1)} %refs_0_.1), channel_id=1, source_target_pairs={{0,2},{2,4},{4,6},{6,0},{1,3},{3,5},{5,7},{7,1},{8,10},{10,12},{12... | collective-permute-start | bytes 860168 | tf_op jit(solution)/shard_map/ppermute | solution.py:159
  7.4 37.4 %collective-permute-start.2 = (bf16[112,1280]{1,0:T(8,128)(2,1)}, bf16[112,1280]{1,0:T(8,128)(2,1)S(1)}, u32[]{:S(2)}, u32[]{:S(2)}) collective-permute-start(bf16[112,1280]{1,0:T(8,128)(2,1)} %refs_0_.1), channel_id=1, source_target_pairs={{0,6},{2,0},{4,2},{6,4},{1,7},{3,1},{5,3},{7,5},{8,14},{10,8},{12,... | collective-permute-start | bytes 860168 | tf_op jit(solution)/shard_map/ppermute | solution.py:159
  12.0 0.7 copy-start.5
  13.7 35.5 %all-to-all-start = ((s32[96,1,8]{2,1,0:T(1,128)}), s32[96,1,8]{2,1,0:T(1,128)}, u32[]{:S(2)}, u32[]{:S(2)}) async-start(s32[96,1,8]{2,1,0:T(1,128)} %shard_map.55), calls=%async_computation | async-start | bytes 98304 | tf_op jit(solution)/shard_map/all_to_all | solution.py:163
  35.8 15.7 %collective-permute-start.4 = (bf16[448,896]{1,0:T(8,128)(2,1)}, bf16[448,896]{1,0:T(8,128)(2,1)}, u32[]{:S(2)}, u32[]{:S(2)}) collective-permute-start(bf16[448,896]{1,0:T(8,128)(2,1)} %bitcast.2), channel_id=1, source_target_pairs={{0,1},{1,0},{2,3},{3,2},{4,5},{5,4},{6,7},{7,6},{8,9},{9,8},{10,11... | collective-permute-start | bytes 2408456 | tf_op jit(solution)/shard_map/ppermute | solution.py:171
  37.7 1.1 %copy-start = (bf16[448,896]{1,0:T(8,128)(2,1)S(1)}, bf16[448,896]{1,0:T(8,128)(2,1)}, u32[]{:S(2)}) copy-start(bf16[448,896]{1,0:T(8,128)(2,1)} %w_ref.1) | copy-start | bytes 2408452
  38.9 0.7 copy-start.6
  39.5 5.3 %copy-start.4 = (bf16[112,1280]{1,0:T(8,128)(2,1)S(1)}, bf16[112,1280]{1,0:T(8,128)(2,1)}, u32[]{:S(2)}) copy-start(bf16[112,1280]{1,0:T(8,128)(2,1)} %refs_0_.1) | copy-start | bytes 860164
  41.5 3.3 %copy-start.2 = (bf16[448,448]{1,0:T(8,128)(2,1)}, bf16[448,448]{1,0:T(8,128)(2,1)S(1)}, u32[]{:S(2)}) copy-start(bf16[448,448]{1,0:T(8,128)(2,1)S(1)} %get-tuple-element.10.out_a) | copy-start | bytes 1204228
  41.5 3.4 %copy-start.7 = (s32[1,256]{1,0:T(1,128)}, s32[1,256]{1,0:T(1,128)S(1)}, u32[]{:S(2)}) copy-start(s32[1,256]{1,0:T(1,128)S(1)} %get-tuple-element.14.slot_ref) | copy-start | bytes 3076
  41.5 9.9 %collective-permute-start.5 = (bf16[448,448]{1,0:T(8,128)(2,1)}, bf16[448,448]{1,0:T(8,128)(2,1)}, u32[]{:S(2)}, u32[]{:S(2)}) collective-permute-start(bf16[448,448]{1,0:T(8,128)(2,1)} %get-tuple-element.11), channel_id=1, source_target_pairs={{0,1},{1,0},{2,3},{3,2},{4,5},{5,4},{6,7},{7,6},{8,9},{9,8},{10,11... | collective-permute-start | bytes 1204232 | tf_op jit(solution)/shard_map/ppermute | solution.py:172
  44.9 6.5 %copy-start.1 = (bf16[896,448]{0,1:T(8,128)(2,1)S(1)}, bf16[896,448]{0,1:T(8,128)(2,1)}, u32[]{:S(2)}) copy-start(bf16[896,448]{0,1:T(8,128)(2,1)} %param.8) | copy-start | bytes 2408452
  44.9 6.5 %collective-permute-start.3 = (bf16[4,112,1280]{2,1,0:T(8,128)(2,1)S(1)}, bf16[4,112,1280]{2,1,0:T(8,128)(2,1)S(1)}, u32[]{:S(2)}, u32[]{:S(2)}) collective-permute-start(bf16[4,112,1280]{2,1,0:T(8,128)(2,1)S(1)} %shard_map.57.mine_ref), channel_id=1, source_target_pairs={{0,1},{1,0},{2,3},{3,2},{4,5},{5,4},{6,7},{7,6},{8,9},{9,8},{10,11... | collective-permute-start | bytes 3440648 | tf_op jit(solution)/shard_map/ppermute | solution.py:174
  49.2 2.3 %copy-start.3 = (bf16[448,448]{1,0:T(8,128)(2,1)S(1)}, bf16[448,448]{1,0:T(8,128)(2,1)}, u32[]{:S(2)}) copy-start(bf16[448,448]{1,0:T(8,128)(2,1)} %copy-done.2) | copy-start | bytes 1204228
  57.3 43.3 %copy-start.8 = (s32[1,256]{1,0:T(1,128)S(1)}, s32[1,256]{1,0:T(1,128)}, u32[]{:S(2)}) copy-start(s32[1,256]{1,0:T(1,128)} %copy-done.7) | copy-start | bytes 3076

commit v4 on v3

--- a/solution.py
+++ b/solution.py
@@ -52,25 +52,29 @@
     return sum((r >= k * block).astype(I32) for k in range(1, count))
 
 
-def blocks_kernel(owners, rows, w_ref, ids_ref, mine_ref, send_ref, slot_ref):
+def blocks_kernel(owners, rows, chips, in_ref, out_ref, gain_ref, ids_ref, mine_ref, send_ref, gains_ref, slot_ref):
     owner, _, rank, _ = ranked(ids_ref[...], owners, rows)
     slot_ref[...] = owner * SLOTS + rank
     core = lax.axis_index("core")
-    n, m = mine_ref.shape[0], w_ref.shape[1]
-    row, lane = iota((n, m), 0), iota((n, m), 1)
-    block = n // lax.axis_size("x")
-    base = row + third(row, block, n // block) * block
-    w = w_ref[...]
-    mine_ref[...] = dot(hot(lane == base + core * block), w, 1, 1).astype(BF16)
-    send_ref[...] = dot(hot(lane == base + (1 - core) * block), w, 1, 1).astype(BF16)
-
-
-def order_kernel(*refs):
-    out_ref = refs[-1]
-    chips = out_ref.shape[0]
-    me = lax.axis_index("x")
-    for k, ref in enumerate(refs[:-1]):
-        out_ref[lax.rem(me - k + chips, chips)] = ref[...]
+    half, feats = in_ref.shape
+    n = feats // 2
+    block = n // chips
+    gain = gain_ref[...]
+    w_in, w_out = in_ref[...], out_ref[...]
+    row, lane = iota((n, feats), 0), iota((n, feats), 1)
+    base = row + third(row, block, chips) * block
+    for i, side in enumerate((core, 1 - core)):
+        mask = lane == base + side * block
+        gains_ref[i] = jnp.sum(jnp.where(mask, gain, 0.0), axis=1, keepdims=True)
+        pick = hot(mask)
+        part = dot(w_in, pick, 1, 1).astype(BF16)
+        mine_ref[i] = part
+        send_ref[1 - i] = part
+        rest = dot(pick, w_out, 1, 1).astype(BF16)
+        if i:
+            send_ref[2] = rest
+        else:
+            mine_ref[2] = rest
 
 
 def pick_kernel(block_ref, pick_ref):
@@ -87,34 +91,41 @@
     pick_ref[...] = hot(iota((rows, cols), 0) == local)
 
 
-def layer_kernel(pick, mine_ref, other_ref, gain_ref, in_a, in_b, out_a, out_b,
-                 part_ref, emb_ref, scaled, hidden, own):
-    core, chip = lax.axis_index("core"), lax.axis_index("x")
-    chips, step, rows = mine_ref.shape
-    feats = 2 * chips * step
-    cols = pick.shape[1]
-    squares = jnp.zeros((1, cols), F32)
-    for ref, side in ((mine_ref, core), (other_ref, 1 - core)):
-        x = dot(ref[...].reshape(chips * step, rows), pick[...], 1, 0)
-        squares += jnp.sum(x * x, axis=0, keepdims=True)
-        for i in range(chips):
-            part = x[i * step:(i + 1) * step]
-            at = pl.ds(pl.multiple_of((2 * i + side) * step, 16), step)
-            scaled[at, :] = (gain_ref[at, :] * part).astype(BF16)
-            if ref is mine_ref:
-                own[i] = part.astype(BF16)
-    emb_ref[...] = own[chip]
-    scale = lax.rsqrt(squares / feats + NORM_EPS)
-    half = in_a.shape[0]
-    for i, w in enumerate((in_a, in_b)):
-        pre = dot(w[...], scaled[...], 1, 0) * scale
-        hidden[pl.ds(i * half, half), :] = jax.nn.gelu(pre, approximate=True).astype(BF16)
-    total = dot(out_a[...], hidden[:half, :], 1, 0) + dot(out_b[...], hidden[half:, :], 1, 0)
-    part_ref[...] = total.astype(BF16).reshape(part_ref.shape)
-
-
-def finish_kernel(parts_ref, emb_ref, out_ref):
-    total = emb_ref[...].astype(F32)
+def select_kernel(pick_ref, *refs):
+    out_ref, table = refs[-2:]
+    chips, step = out_ref.shape[0], out_ref.shape[1]
+    me = lax.axis_index("x")
+    for k, ref in enumerate(refs[:-2]):
+        table[lax.rem(me - k + chips, chips)] = ref[...]
+    x = dot(table[...].reshape(chips * step, -1), pick_ref[...], 1, 0)
+    out_ref[...] = x.astype(BF16).reshape(out_ref.shape)
+
+
+def scaled_of(x_ref, gain):
+    chips, step, cols = x_ref.shape
+    x = x_ref[...].reshape(chips * step, cols).astype(F32)
+    return (gain * x).astype(BF16), jnp.sum(x * x, axis=0, keepdims=True)
+
+
+def first_kernel(x_ref, gains_ref, mine_ref, other_ref, pre_ref, square_ref):
+    scaled, square_ref[...] = scaled_of(x_ref, gains_ref[0])
+    for i, w in enumerate((mine_ref, other_ref)):
+        pre_ref[i] = dot(w[0], scaled, 1, 0)
+
+
+def second_kernel(x_ref, gains_ref, mine_ref, other_ref, pre_ref, square_ref, out_ref, hidden):
+    scaled, squares = scaled_of(x_ref, gains_ref[1])
+    squares += square_ref[...]
+    scale = lax.rsqrt(squares / (2 * scaled.shape[0]) + NORM_EPS)
+    for i, w in enumerate((mine_ref, other_ref)):
+        pre = (pre_ref[i] + dot(w[1], scaled, 1, 0)) * scale
+        hidden[i] = jax.nn.gelu(pre, approximate=True).astype(BF16)
+    total = dot(mine_ref[2], hidden[0], 1, 0) + dot(other_ref[2], hidden[1], 1, 0)
+    out_ref[...] = total.astype(BF16).reshape(out_ref.shape)
+
+
+def finish_kernel(parts_ref, x_ref, out_ref):
+    total = x_ref[lax.axis_index("x")].astype(F32)
     for i in range(parts_ref.shape[0]):
         total += parts_ref[i].astype(F32)
     encoded = total.astype(BF16)
@@ -155,36 +166,34 @@
     shape = jax.ShapeDtypeStruct
 
     ids = neighbour_ids.reshape(1, toks)
+    outgoing = call(functools.partial(request_kernel, rows), shape((owners, 1, SLOTS), I32))(ids)
+    block = lax.all_to_all(outgoing, seq, split_axis=0, concat_axis=0, tiled=True)
     behind = [
         lax.ppermute(table_cols, "x", [(i, (i + k) % chips) for i in range(chips)])
         for k in range(1, chips)
     ]
-    outgoing = call(functools.partial(request_kernel, rows), shape((owners, 1, SLOTS), I32))(ids)
-    block = lax.all_to_all(outgoing, seq, split_axis=0, concat_axis=0, tiled=True)
-
     swap = [(0, 1), (1, 0)]
-    w_in_t = w_in.T
-    out_mine, out_send, slot = call(
-        functools.partial(blocks_kernel, owners, rows),
-        (shape((chips * feat_local, half), BF16),) * 2 + (shape((1, toks), I32),),
-    )(w_out, ids)
-    in_other = lax.ppermute(w_in_t, "core", swap)
-    out_other = lax.ppermute(out_send, "core", swap)
-    mine = call(order_kernel, shape((chips, feat_local, rows), BF16))(table_cols, *behind)
-    other = lax.ppermute(mine, "core", swap)
-
-    pick = call(pick_kernel, shape((rows, cols), BF16), flops=30_000_000_000)(block)
-    parts, emb = call(
-        layer_kernel,
-        (shape((chips, feat_local, cols), BF16), shape((feat_local, cols), BF16)),
-        (
-            pltpu.VMEM((feats, cols), BF16),
-            pltpu.VMEM((2 * half, cols), BF16),
-            pltpu.VMEM((chips, feat_local, cols), BF16),
-        ),
-    )(pick, mine, other, gain.reshape(feats, 1), w_in_t, in_other, out_mine, out_other)
+    w_mine, w_send, gains, slot = call(
+        functools.partial(blocks_kernel, owners, rows, chips),
+        (shape((3, half, half), BF16),) * 2 + (shape((2, half, 1), F32), shape((1, toks), I32)),
+    )(w_in.T, w_out, gain.reshape(1, feats), ids)
+    w_other = lax.ppermute(w_send, "core", swap)
+
+    pick = call(pick_kernel, shape((rows, cols), BF16), flops=10_000_000_000)(block)
+    x_mine = call(
+        select_kernel,
+        shape((chips, feat_local, cols), BF16),
+        (pltpu.VMEM((chips, feat_local, rows), BF16),),
+    )(pick, table_cols, *behind)
+    x_other = lax.ppermute(x_mine, "core", swap)
+    pre, square = call(first_kernel, (shape((2, half, cols), F32), shape((1, cols), F32)))(
+        x_mine, gains, w_mine, w_other
+    )
+    parts = call(second_kernel, shape((chips, feat_local, cols), BF16), (pltpu.VMEM((2, half, cols), BF16),))(
+        x_other, gains, w_mine, w_other, pre, square
+    )
     parts = lax.all_to_all(parts, "x", split_axis=0, concat_axis=0, tiled=True)
-    encoded = call(finish_kernel, shape((owners, SLOTS, feat_local), BF16))(parts, emb)
+    encoded = call(finish_kernel, shape((owners, SLOTS, feat_local), BF16))(parts, x_mine)
     back = lax.all_to_all(encoded, seq, split_axis=0, concat_axis=0, tiled=True)
     return call(place_kernel, shape((feat_local, toks), BF16))(back, slot)
 

time: 102 us -> 101 us (level)
  blocking collectives: 42.8 us -> 45.3 us
  starting transfers between devices: 40.5 us -> 38.2 us
  waiting for transfers between devices: 2.2 us -> 0.6 us
    all_to_all x1, waiting for transfers between devices: 2.19 us -> 0.01 us  [on_device(): lax.all_to_all(outgoing, seq, split_axis=0, concat_axis=0, tiled=True)]
    ppermute x3 -> x2, starting transfers between devices: 6.37 us -> 4.44 us  [the longest x1 2.4 us: on_device(): x_other = lax.ppermute(x_mine, 'core', swap)]
    all_to_all x1, blocking collectives: 11.3 us -> 13.2 us  [on_device(): parts = lax.all_to_all(parts, 'x', split_axis=0, concat_axis=0, tiled=True)]
    unnamed x18 -> x10, local copies, waits for them, and re-layouts: 2.51 us -> 3.64 us
    pallas_call x5 -> x6, Pallas kernels: 10.6 us -> 10.5 us  [the longest x1 3.32 us: on_device(): call(functools.partial(blocks_kernel, owners, rows, chips), (shape((3, ha...]
  transfers between devices with their start and end apart: 7 -> 6, of which waited for: 1 -> 1; matrix products, arithmetic and copies ran while one was open for 1% -> 1% of each run, Pallas kernels for 5% -> 8%
where the time goes in v4:
time: 101 us
  blocking collectives  45.3 us (45%)
  starting transfers between devices  38.2 us (38%)
  Pallas kernels  12.4 us (12%)
  local copies, waits for them, and re-layouts  4.33 us (4%)
    all_to_all x1, blocking collectives, on_device(): back = lax.all_to_all(encoded, seq, split_axis=0, concat_axis=0, tiled=True)  32.1 us
    all_to_all x1, starting transfers between devices, on_device(): lax.all_to_all(outgoing, seq, split_axis=0, concat_axis=0, tiled=True)  21.8 us
    all_to_all x1, blocking collectives, on_device(): parts = lax.all_to_all(parts, 'x', split_axis=0, concat_axis=0, tiled=True)  13.2 us
    ppermute x3, starting transfers between devices, on_device(): lax.ppermute(table_cols, 'x', [(i, (i + k) % chips) for i in range(chips)])  12 us
    unnamed x10, local copies, waits for them, and re-layouts  3.64 us
    pallas_call x1, Pallas kernels, on_device(): call(functools.partial(blocks_kernel, owners, rows, chips), (shape((3, ha...  3.32 us
    ppermute x1, starting transfers between devices, on_device(): x_other = lax.ppermute(x_mine, 'core', swap)  2.4 us
    pallas_call x1, Pallas kernels, on_device(): call(select_kernel, shape((chips, feat_local, cols), BF16), (pltpu.VMEM((...  2.3 us
  transfers between devices with their start and end apart: 6, of which 1 were waited for; matrix products, arithmetic and copies ran while one was open for 1% of the time, Pallas kernels for 8%

profile of v4, /device:TPU:8, one launch (start us, length us, event | category | flops | bytes accessed | tf_op | source)
XLA Modules:
  0.0 100.9 jit_solution(391640885740646423)
XLA Ops:
  0.0 0.0 copy-start.3
  0.0 0.7 copy-done.3
  0.7 1.0 shard_map.55
  1.7 21.8 %all-to-all-start = ((s32[96,1,8]{2,1,0:T(1,128)}), s32[96,1,8]{2,1,0:T(1,128)S(1)}, u32[]{:S(2)}, u32[]{:S(2)}) async-start(s32[96,1,8]{2,1,0:T(1,128)} %shard_map.55), calls=%async_computation | async-start | bytes 98304 | tf_op jit(solution)/shard_map/all_to_all | solution.py:170
  23.4 4.9 %collective-permute-start.1 = (bf16[112,1280]{1,0:T(8,128)(2,1)}, bf16[112,1280]{1,0:T(8,128)(2,1)}, u32[]{:S(2)}, u32[]{:S(2)}) collective-permute-start(bf16[112,1280]{1,0:T(8,128)(2,1)} %refs_0_.1), channel_id=1, source_target_pairs={{0,4},{2,6},{4,0},{6,2},{1,5},{3,7},{5,1},{7,3},{8,12},{10,14},{12... | collective-permute-start | bytes 860168 | tf_op jit(solution)/shard_map/ppermute | solution.py:172
  28.4 2.5 %collective-permute-start = (bf16[112,1280]{1,0:T(8,128)(2,1)}, bf16[112,1280]{1,0:T(8,128)(2,1)}, u32[]{:S(2)}, u32[]{:S(2)}) collective-permute-start(bf16[112,1280]{1,0:T(8,128)(2,1)} %refs_0_.1), channel_id=1, source_target_pairs={{0,2},{2,4},{4,6},{6,0},{1,3},{3,5},{5,7},{7,1},{8,10},{10,12},{12... | collective-permute-start | bytes 860168 | tf_op jit(solution)/shard_map/ppermute | solution.py:172
  30.9 4.6 %collective-permute-start.2 = (bf16[112,1280]{1,0:T(8,128)(2,1)}, bf16[112,1280]{1,0:T(8,128)(2,1)}, u32[]{:S(2)}, u32[]{:S(2)}) collective-permute-start(bf16[112,1280]{1,0:T(8,128)(2,1)} %refs_0_.1), channel_id=1, source_target_pairs={{0,6},{2,0},{4,2},{6,4},{1,7},{3,1},{5,3},{7,5},{8,14},{10,8},{12,... | collective-permute-start | bytes 860168 | tf_op jit(solution)/shard_map/ppermute | solution.py:172
  35.5 0.7 reshape.7.gain_ref
  36.2 1.1 %copy-done = bf16[896,448]{0,1:T(8,128)(2,1)S(1)} copy-done((bf16[896,448]{0,1:T(8,128)(2,1)S(1)}, bf16[896,448]{0,1:T(8,128)(2,1)}, u32[]{:S(2)}) %copy-start) | copy-done | bytes 802840
  37.3 0.0 copy-start.1
  37.3 1.1 %copy-done.1 = bf16[448,896]{1,0:T(8,128)(2,1)S(1)} copy-done((bf16[448,896]{1,0:T(8,128)(2,1)S(1)}, bf16[448,896]{1,0:T(8,128)(2,1)}, u32[]{:S(2)}) %copy-start.1) | copy-done | bytes 802840
  38.4 0.0 copy-start.4
  38.4 0.7 copy-done.4
  39.1 3.3 %shard_map.58 = (bf16[3,448,448]{2,1,0:T(8,128)(2,1)S(1)}, bf16[3,448,448]{2,1,0:T(8,128)(2,1)}, f32[2,448,1]{2,1,0:T(8,128)S(1)}, s32[1,256]{1,0:T(1,128)S(1)}) custom-call(bf16[448,896]{1,0:T(8,128)(2,1)S(1)} %bitcast.2, bf16[448,896]{1,0:T(8,128)(2,1)S(1)} %copy-done.1, f32[1,896]{1,0:T(1,128)S(1)} %reshape.7.gain_ref, s32[1,256]{1,0:T(1,128)S(1)} %bitcast.4), custom_call_target="tpu_custom_call" | custom-call | tf_op jit(solution)/shard_map/pallas_call | solution.py:176
  42.4 0.0 copy-start.2
  42.4 2.0 %collective-permute-start.4 = (bf16[3,448,448]{2,1,0:T(8,128)(2,1)}, bf16[3,448,448]{2,1,0:T(8,128)(2,1)S(1)}, u32[]{:S(2)}, u32[]{:S(2)}) collective-permute-start(bf16[3,448,448]{2,1,0:T(8,128)(2,1)} %get-tuple-element.13), channel_id=1, source_target_pairs={{0,1},{1,0},{2,3},{3,2},{4,5},{5,4},{6,7},{7,6},{8,9},{9,8},{10,11... | collective-permute-start | bytes 3612680 | tf_op jit(solution)/shard_map/ppermute | solution.py:180
  44.5 0.0 all-to-all-done.block_ref
  44.5 1.4 %shard_map.56.pick_ref = bf16[1280,576]{1,0:T(8,128)(2,1)S(1)} custom-call(s32[96,1,8]{2,1,0:T(1,128)S(1)} %all-to-all-done.block_ref), custom_call_target="tpu_custom_call" | custom-call | flops 10000000000 | tf_op jit(solution)/shard_map/pallas_call | solution.py:182
  45.9 0.0 collective-permute-done.1.refs_2_
  45.9 0.0 collective-permute-done.refs_1_
  45.9 0.0 collective-permute-done.2.refs_3_
  45.9 0.0 copy-done.2
  45.9 2.3 %shard_map.57.x_ref = bf16[4,112,576]{2,1,0:T(8,128)(2,1)S(1)} custom-call(bf16[1280,576]{1,0:T(8,128)(2,1)S(1)} %shard_map.56.pick_ref, bf16[112,1280]{1,0:T(8,128)(2,1)S(1)} %copy-done.2, bf16[112,1280]{1,0:T(8,128)(2,1)} %collective-permute-done.refs_1_, bf16[112,1280]{1,0:T(8,128)(2,1)} %collective-permute-done.1.refs_2_, ...), custom_call_target="tpu_custom_call" | custom-call | tf_op jit(solution)/shard_map/pallas_call | solution.py:183
  48.2 2.4 %collective-permute-start.3 = (bf16[4,112,576]{2,1,0:T(8,128)(2,1)S(1)}, bf16[4,112,576]{2,1,0:T(8,128)(2,1)S(1)}, u32[]{:S(2)}, u32[]{:S(2)}) collective-permute-start(bf16[4,112,576]{2,1,0:T(8,128)(2,1)S(1)} %shard_map.57.x_ref), channel_id=1, source_target_pairs={{0,1},{1,0},{2,3},{3,2},{4,5},{5,4},{6,7},{7,6},{8,9},{9,8},{10,11... | collective-permute-start | bytes 1548296 | tf_op jit(solution)/shard_map/ppermute | solution.py:188
  50.6 0.0 collective-permute-done.4.other_ref
  50.7 1.0 shard_map.59
  51.6 0.6 collective-permute-done.3.x_ref
  52.2 2.0 %shard_map.60 = bf16[4,112,576]{2,1,0:T(8,128)(2,1)S(1)} custom-call(bf16[4,112,576]{2,1,0:T(8,128)(2,1)S(1)} %collective-permute-done.3.x_ref, f32[2,448,1]{2,1,0:T(8,128)S(1)} %get-tuple-element.11.gains_ref, bf16[3,448,448]{2,1,0:T(8,128)(2,1)S(1)} %get-tuple-element.12.mine_ref, bf16[3,448,448]{2,1,0:T(8,128)(2,1)S(1)} %collective-permute-done.4.other_ref, ...), custom_call_target="tpu_custom_call" | custom-call | tf_op jit(solution)/shard_map/pallas_call | solution.py:192
  54.2 13.2 %all_to_all.15.parts_ref = bf16[4,112,576]{2,1,0:T(8,128)(2,1)S(1)} all-to-all(bf16[4,112,576]{2,1,0:T(8,128)(2,1)S(1)} %shard_map.60), channel_id=1, replica_groups=mesh['y'=8,'z'=12,'x'=4,'core'=2] {'x'}, dimensions={0} | all-to-all | bytes 1032192 | tf_op jit(solution)/shard_map/all_to_all | solution.py:195
  67.4 0.6 shard_map.61
  68.0 32.1 %all_to_all.16.back_ref = bf16[96,8,112]{2,1,0:T(8,128)(2,1)S(1)} all-to-all(bf16[96,8,112]{2,1,0:T(8,128)(2,1)S(1)} %shard_map.61), channel_id=1, replica_groups=mesh['y'=8,'z'=12,'x'=4,'core'=2] {'y','z'}, dimensions={0} | all-to-all | bytes 344064 | tf_op jit(solution)/shard_map/all_to_all | solution.py:197
  100.1 0.9 shard_map.62
  (1 shorter events, 0.0 us)
Async XLA Ops:
  0.0 0.7 copy-start.3
  1.7 42.8 %all-to-all-start = ((s32[96,1,8]{2,1,0:T(1,128)}), s32[96,1,8]{2,1,0:T(1,128)S(1)}, u32[]{:S(2)}, u32[]{:S(2)}) async-start(s32[96,1,8]{2,1,0:T(1,128)} %shard_map.55), calls=%async_computation | async-start | bytes 98304 | tf_op jit(solution)/shard_map/all_to_all | solution.py:170
  23.4 22.4 %collective-permute-start.1 = (bf16[112,1280]{1,0:T(8,128)(2,1)}, bf16[112,1280]{1,0:T(8,128)(2,1)}, u32[]{:S(2)}, u32[]{:S(2)}) collective-permute-start(bf16[112,1280]{1,0:T(8,128)(2,1)} %refs_0_.1), channel_id=1, source_target_pairs={{0,4},{2,6},{4,0},{6,2},{1,5},{3,7},{5,1},{7,3},{8,12},{10,14},{12... | collective-permute-start | bytes 860168 | tf_op jit(solution)/shard_map/ppermute | solution.py:172
  28.4 17.5 %collective-permute-start = (bf16[112,1280]{1,0:T(8,128)(2,1)}, bf16[112,1280]{1,0:T(8,128)(2,1)}, u32[]{:S(2)}, u32[]{:S(2)}) collective-permute-start(bf16[112,1280]{1,0:T(8,128)(2,1)} %refs_0_.1), channel_id=1, source_target_pairs={{0,2},{2,4},{4,6},{6,0},{1,3},{3,5},{5,7},{7,1},{8,10},{10,12},{12... | collective-permute-start | bytes 860168 | tf_op jit(solution)/shard_map/ppermute | solution.py:172
  30.9 15.0 %collective-permute-start.2 = (bf16[112,1280]{1,0:T(8,128)(2,1)}, bf16[112,1280]{1,0:T(8,128)(2,1)}, u32[]{:S(2)}, u32[]{:S(2)}) collective-permute-start(bf16[112,1280]{1,0:T(8,128)(2,1)} %refs_0_.1), channel_id=1, source_target_pairs={{0,6},{2,0},{4,2},{6,4},{1,7},{3,1},{5,3},{7,5},{8,14},{10,8},{12,... | collective-permute-start | bytes 860168 | tf_op jit(solution)/shard_map/ppermute | solution.py:172
  36.2 1.1 %copy-start = (bf16[896,448]{0,1:T(8,128)(2,1)S(1)}, bf16[896,448]{0,1:T(8,128)(2,1)}, u32[]{:S(2)}) copy-start(bf16[896,448]{0,1:T(8,128)(2,1)} %param.8) | copy-start | bytes 2408452
  37.3 1.1 %copy-start.1 = (bf16[448,896]{1,0:T(8,128)(2,1)S(1)}, bf16[448,896]{1,0:T(8,128)(2,1)}, u32[]{:S(2)}) copy-start(bf16[448,896]{1,0:T(8,128)(2,1)} %out_ref.1) | copy-start | bytes 2408452
  38.4 0.7 copy-start.4
  42.4 3.5 %copy-start.2 = (bf16[112,1280]{1,0:T(8,128)(2,1)S(1)}, bf16[112,1280]{1,0:T(8,128)(2,1)}, u32[]{:S(2)}) copy-start(bf16[112,1280]{1,0:T(8,128)(2,1)} %refs_0_.1) | copy-start | bytes 860164
  42.4 8.2 %collective-permute-start.4 = (bf16[3,448,448]{2,1,0:T(8,128)(2,1)}, bf16[3,448,448]{2,1,0:T(8,128)(2,1)S(1)}, u32[]{:S(2)}, u32[]{:S(2)}) collective-permute-start(bf16[3,448,448]{2,1,0:T(8,128)(2,1)} %get-tuple-element.13), channel_id=1, source_target_pairs={{0,1},{1,0},{2,3},{3,2},{4,5},{5,4},{6,7},{7,6},{8,9},{9,8},{10,11... | collective-permute-start | bytes 3612680 | tf_op jit(solution)/shard_map/ppermute | solution.py:180
  48.2 4.0 %collective-permute-start.3 = (bf16[4,112,576]{2,1,0:T(8,128)(2,1)S(1)}, bf16[4,112,576]{2,1,0:T(8,128)(2,1)S(1)}, u32[]{:S(2)}, u32[]{:S(2)}) collective-permute-start(bf16[4,112,576]{2,1,0:T(8,128)(2,1)S(1)} %shard_map.57.x_ref), channel_id=1, source_target_pairs={{0,1},{1,0},{2,3},{3,2},{4,5},{5,4},{6,7},{7,6},{8,9},{9,8},{10,11... | collective-permute-start | bytes 1548296 | tf_op jit(solution)/shard_map/ppermute | solution.py:188

commit v5 on v4

--- a/solution.py
+++ b/solution.py
@@ -52,34 +52,38 @@
     return sum((r >= k * block).astype(I32) for k in range(1, count))
 
 
-def blocks_kernel(owners, rows, chips, in_ref, out_ref, gain_ref, ids_ref, mine_ref, send_ref, gains_ref, slot_ref):
+def blocks_kernel(owners, rows, chips, in_hbm, out_hbm, gain_ref, ids_ref, mine_ref, send_ref, gains_ref, slot_ref,
+                  w_in, w_out, sems):
+    load_in = pltpu.make_async_copy(in_hbm, w_in, sems.at[0])
+    load_out = pltpu.make_async_copy(out_hbm, w_out, sems.at[1])
+    load_in.start()
+    load_out.start()
     owner, _, rank, _ = ranked(ids_ref[...], owners, rows)
     slot_ref[...] = owner * SLOTS + rank
     core = lax.axis_index("core")
-    half, feats = in_ref.shape
+    half, feats = w_in.shape
     n = feats // 2
     block = n // chips
-    gain = gain_ref[...]
-    w_in, w_out = in_ref[...], out_ref[...]
+    gain = jnp.transpose(jnp.broadcast_to(gain_ref[...].reshape(1, feats), (8, feats)))[:, :1]
+    for i in range(chips):
+        for j in range(2):
+            at = (2 * i + j) * block
+            gains_ref[jnp.where(core == j, 0, 1), pl.ds(i * block, block), :] = gain[at:at + block]
     row, lane = iota((n, feats), 0), iota((n, feats), 1)
     base = row + third(row, block, chips) * block
-    for i, side in enumerate((core, 1 - core)):
-        mask = lane == base + side * block
-        gains_ref[i] = jnp.sum(jnp.where(mask, gain, 0.0), axis=1, keepdims=True)
-        pick = hot(mask)
-        part = dot(w_in, pick, 1, 1).astype(BF16)
+    picks = [hot(lane == base + side * block) for side in (core, 1 - core)]
+    load_in.wait()
+    for i, pick in enumerate(picks):
+        part = dot(w_in[...], pick, 1, 1).astype(BF16)
         mine_ref[i] = part
         send_ref[1 - i] = part
-        rest = dot(pick, w_out, 1, 1).astype(BF16)
-        if i:
-            send_ref[2] = rest
-        else:
-            mine_ref[2] = rest
-
-
-def pick_kernel(block_ref, pick_ref):
-    sources = block_ref.shape[0]
-    rows, cols = pick_ref.shape
+    load_out.wait()
+    mine_ref[2] = dot(picks[0], w_out[...], 1, 1).astype(BF16)
+    send_ref[2] = dot(picks[1], w_out[...], 1, 1).astype(BF16)
+
+
+def decode_kernel(block_ref, out_ref):
+    sources, cols = block_ref.shape[0], out_ref.shape[1]
     code = block_ref[:, 0, :]
     spread = hot(iota((sources, cols), 1) // CAP == iota((sources, cols), 0))
     high = (code // SPLIT).astype(F32).astype(BF16)
@@ -87,17 +91,24 @@
     wide = dot(high, spread, 0, 0) * SPLIT + dot(low, spread, 0, 0)
     lane = iota((SLOTS, cols), 1)
     local = jnp.sum(jnp.where(lane - (lane // CAP) * CAP == iota((SLOTS, cols), 0), wide, 0.0), axis=0, keepdims=True)
-    local = local.astype(I32) - 1
-    pick_ref[...] = hot(iota((rows, cols), 0) == local)
-
-
-def select_kernel(pick_ref, *refs):
-    out_ref, table = refs[-2:]
-    chips, step = out_ref.shape[0], out_ref.shape[1]
+    out_ref[...] = local.astype(I32) - 1
+
+
+def select_kernel(local_ref, *refs):
+    blocks, (out_ref, table, sems) = refs[:-3], refs[-3:]
+    chips, step, cols = out_ref.shape
+    rows = table.shape[2]
     me = lax.axis_index("x")
-    for k, ref in enumerate(refs[:-2]):
-        table[lax.rem(me - k + chips, chips)] = ref[...]
-    x = dot(table[...].reshape(chips * step, -1), pick_ref[...], 1, 0)
+    loads = [
+        pltpu.make_async_copy(ref, table.at[lax.rem(me - k + chips, chips)], sems.at[k])
+        for k, ref in enumerate(blocks)
+    ]
+    for load in loads:
+        load.start()
+    pick = hot(iota((rows, cols), 0) == local_ref[...])
+    for load in loads:
+        load.wait()
+    x = dot(table[...].reshape(chips * step, rows), pick, 1, 0)
     out_ref[...] = x.astype(BF16).reshape(out_ref.shape)
 
 
@@ -145,13 +156,14 @@
     out_ref[...] = dot(back, pick, 0, 0).astype(BF16)
 
 
-def call(kernel, out_shape, scratch=(), vmem=32 * 1024 * 1024, flops=None):
+def call(kernel, out_shape, scratch=(), vmem=32 * 1024 * 1024, flops=None, **more):
     return pl.pallas_call(
         kernel,
         out_shape=out_shape,
         scratch_shapes=list(scratch),
         cost_estimate=flops and pl.CostEstimate(flops=flops, bytes_accessed=0, transcendentals=0),
         compiler_params=pltpu.CompilerParams(vmem_limit_bytes=vmem),
+        **more,
     )
 
 
@@ -168,23 +180,32 @@
     ids = neighbour_ids.reshape(1, toks)
     outgoing = call(functools.partial(request_kernel, rows), shape((owners, 1, SLOTS), I32))(ids)
     block = lax.all_to_all(outgoing, seq, split_axis=0, concat_axis=0, tiled=True)
-    behind = [
-        lax.ppermute(table_cols, "x", [(i, (i + k) % chips) for i in range(chips)])
-        for k in range(1, chips)
-    ]
+    late_cols, _ = lax.optimization_barrier((table_cols, outgoing))
+
+    def shifted(cols, k):
+        return lax.ppermute(cols, "x", [(i, (i + k) % chips) for i in range(chips)])
+
+    far = shifted(table_cols, 2)
+    block, far = lax.optimization_barrier((block, far))
+    behind = shifted(late_cols, 1), far, shifted(late_cols, 3)
     swap = [(0, 1), (1, 0)]
+    anywhere, vmem = pl.BlockSpec(memory_space=pl.ANY), pl.BlockSpec(memory_space=pltpu.VMEM)
     w_mine, w_send, gains, slot = call(
         functools.partial(blocks_kernel, owners, rows, chips),
         (shape((3, half, half), BF16),) * 2 + (shape((2, half, 1), F32), shape((1, toks), I32)),
-    )(w_in.T, w_out, gain.reshape(1, feats), ids)
+        (pltpu.VMEM((half, feats), BF16), pltpu.VMEM((half, feats), BF16), pltpu.SemaphoreType.DMA((2,))),
+        in_specs=[anywhere, anywhere, vmem, vmem],
+        vmem=60_000_000,
+    )(w_in.T, w_out, gain, ids)
     w_other = lax.ppermute(w_send, "core", swap)
 
-    pick = call(pick_kernel, shape((rows, cols), BF16), flops=10_000_000_000)(block)
+    local = call(decode_kernel, shape((1, cols), I32), flops=10_000_000_000)(block)
     x_mine = call(
         select_kernel,
         shape((chips, feat_local, cols), BF16),
-        (pltpu.VMEM((chips, feat_local, rows), BF16),),
-    )(pick, table_cols, *behind)
+        (pltpu.VMEM((chips, feat_local, rows), BF16), pltpu.SemaphoreType.DMA((chips,))),
+        in_specs=[vmem] + [anywhere] * chips,
+    )(local, table_cols, *behind)
     x_other = lax.ppermute(x_mine, "core", swap)
     pre, square = call(first_kernel, (shape((2, half, cols), F32), shape((1, cols), F32)))(
         x_mine, gains, w_mine, w_other

time: 101 us -> 97.5 us (0.965)
  local copies, waits for them, and re-layouts: 4.33 us -> 0.69 us
  starting transfers between devices: 38.2 us -> 36.8 us
    unnamed x10, local copies, waits for them, and re-layouts: 3.64 us -> 0.69 us
    pallas_call x1, Pallas kernels: 3.32 us -> 5.34 us  [on_device(): call(functools.partial(blocks_kernel, owners, rows, chips), (shape((3, ha...]
    ppermute x3, starting transfers between devices: 12 us -> 10.8 us  [shifted(): return lax.ppermute(cols, 'x', [(i, (i + k) % chips) for i in range(chips)])]
  transfers between devices with their start and end apart: 6 -> 6, of which waited for: 1 -> 2; matrix products, arithmetic and copies ran while one was open for 1% -> 0% of each run, Pallas kernels for 8% -> 10%
where the time goes in v5:
time: 97.5 us; the launch traced here: 97.1 us
  blocking collectives  45.4 us (47%)
  starting transfers between devices  36.8 us (38%)
  Pallas kernels  13.1 us (13%)
    all_to_all x1, blocking collectives, on_device(): back = lax.all_to_all(encoded, seq, split_axis=0, concat_axis=0, tiled=True)  31.5 us
    all_to_all x1, starting transfers between devices, on_device(): lax.all_to_all(outgoing, seq, split_axis=0, concat_axis=0, tiled=True)  21.8 us
    all_to_all x1, blocking collectives, on_device(): parts = lax.all_to_all(parts, 'x', split_axis=0, concat_axis=0, tiled=True)  13.9 us
    ppermute x3, starting transfers between devices, shifted(): return lax.ppermute(cols, 'x', [(i, (i + k) % chips) for i in range(chips)])  10.8 us
    pallas_call x1, Pallas kernels, on_device(): call(functools.partial(blocks_kernel, owners, rows, chips), (shape((3, ha...  5.34 us
    ppermute x1, starting transfers between devices, on_device(): x_other = lax.ppermute(x_mine, 'core', swap)  2.21 us
    ppermute x1, starting transfers between devices, on_device(): w_other = lax.ppermute(w_send, 'core', swap)  2.05 us
    pallas_call x1, Pallas kernels, on_device(): call(second_kernel, shape((chips, feat_local, cols), BF16), (pltpu.VMEM((...  2.01 us
  transfers between devices with their start and end apart: 6, of which 2 were waited for; matrix products, arithmetic and copies ran while one was open for 0% of the time, Pallas kernels for 10%

profile of v5, /device:TPU:8, one launch (start us, length us, event | category | flops | bytes accessed | tf_op | source)
XLA Modules:
  0.0 97.1 jit_solution(11208925084902965921)
XLA Ops:
  0.0 4.9 %collective-permute-start = (bf16[112,1280]{1,0:T(8,128)(2,1)}, bf16[112,1280]{1,0:T(8,128)(2,1)S(1)}, u32[]{:S(2)}, u32[]{:S(2)}) collective-permute-start(bf16[112,1280]{1,0:T(8,128)(2,1)} %refs_0_.1), channel_id=1, source_target_pairs={{0,4},{2,6},{4,0},{6,2},{1,5},{3,7},{5,1},{7,3},{8,12},{10,14},{12... | collective-permute-start | bytes 860168 | tf_op jit(solution)/shard_map/ppermute | solution.py:186
  4.9 0.0 copy-start.3
  4.9 0.7 copy-done.3
  5.6 1.0 %shard_map.55 = s32[96,1,8]{2,1,0:T(1,128)} custom-call(s32[1,256]{1,0:T(1,128)S(1)} %bitcast.3), custom_call_target="tpu_custom_call" | custom-call | tf_op jit(solution)/shard_map/pallas_call | solution.py:181
  6.6 21.8 %all-to-all-start = ((s32[96,1,8]{2,1,0:T(1,128)}), s32[96,1,8]{2,1,0:T(1,128)S(1)}, u32[]{:S(2)}, u32[]{:S(2)}) async-start(s32[96,1,8]{2,1,0:T(1,128)} %shard_map.55), calls=%async_computation | async-start | bytes 98304 | tf_op jit(solution)/shard_map/all_to_all | solution.py:182
  28.4 3.1 %collective-permute-start.2 = (bf16[112,1280]{1,0:T(8,128)(2,1)}, bf16[112,1280]{1,0:T(8,128)(2,1)S(1)}, u32[]{:S(2)}, u32[]{:S(2)}) collective-permute-start(bf16[112,1280]{1,0:T(8,128)(2,1)} %refs_0_.1), channel_id=1, source_target_pairs={{0,6},{2,0},{4,2},{6,4},{1,7},{3,1},{5,3},{7,5},{8,14},{10,8},{12,... | collective-permute-start | bytes 860168 | tf_op jit(solution)/shard_map/ppermute | solution.py:186
  31.4 2.8 %collective-permute-start.1 = (bf16[112,1280]{1,0:T(8,128)(2,1)}, bf16[112,1280]{1,0:T(8,128)(2,1)S(1)}, u32[]{:S(2)}, u32[]{:S(2)}) collective-permute-start(bf16[112,1280]{1,0:T(8,128)(2,1)} %refs_0_.1), channel_id=1, source_target_pairs={{0,2},{2,4},{4,6},{6,0},{1,3},{3,5},{5,7},{7,1},{8,10},{10,12},{12... | collective-permute-start | bytes 860168 | tf_op jit(solution)/shard_map/ppermute | solution.py:186
  34.2 5.3 %shard_map.58 = (bf16[3,448,448]{2,1,0:T(8,128)(2,1)}, bf16[3,448,448]{2,1,0:T(8,128)(2,1)}, f32[2,448,1]{2,1,0:T(8,128)}, s32[1,256]{1,0:T(1,128)}) custom-call(bf16[448,896]{1,0:T(8,128)(2,1)} %bitcast.4, bf16[448,896]{1,0:T(8,128)(2,1)} %out_hbm.1, f32[896]{0:T(1024)} %gain_ref.1, s32[1,256]{1,0:T(1,128)} %bitcast.2), custom_call_target="tpu_custom_call" | custom-call | tf_op jit(solution)/shard_map/pallas_call | solution.py:193
  39.6 0.0 copy-start.2
  39.6 2.1 %collective-permute-start.4 = (bf16[3,448,448]{2,1,0:T(8,128)(2,1)}, bf16[3,448,448]{2,1,0:T(8,128)(2,1)S(1)}, u32[]{:S(2)}, u32[]{:S(2)}) collective-permute-start(bf16[3,448,448]{2,1,0:T(8,128)(2,1)} %get-tuple-element.19), channel_id=1, source_target_pairs={{0,1},{1,0},{2,3},{3,2},{4,5},{5,4},{6,7},{7,6},{8,9},{9,8},{10,11... | collective-permute-start | bytes 3612680 | tf_op jit(solution)/shard_map/ppermute | solution.py:200
  41.7 0.2 all-to-all-done.block_ref
  41.9 0.0 collective-permute-done.refs_2_
  41.9 0.0 copy-start.1
  41.9 0.6 shard_map.56.local_ref
  42.5 0.0 copy-start
  42.6 0.0 collective-permute-done.2.refs_3_
  42.6 0.0 collective-permute-done.1.refs_1_
  42.6 0.0 copy-done.2
  42.6 1.7 %shard_map.57.x_ref = bf16[4,112,576]{2,1,0:T(8,128)(2,1)S(1)} custom-call(s32[1,576]{1,0:T(1,128)S(1)} %shard_map.56.local_ref, bf16[112,1280]{1,0:T(8,128)(2,1)S(1)} %copy-done.2, bf16[112,1280]{1,0:T(8,128)(2,1)S(1)} %collective-permute-done.1.refs_1_, bf16[112,1280]{1,0:T(8,128)(2,1)S(1)} %collective-permute-done.refs_2_, ...), custom_call_target="tpu_custom_call" | custom-call | tf_op jit(solution)/shard_map/pallas_call | solution.py:203
  44.3 2.2 %collective-permute-start.3 = (bf16[4,112,576]{2,1,0:T(8,128)(2,1)S(1)}, bf16[4,112,576]{2,1,0:T(8,128)(2,1)S(1)}, u32[]{:S(2)}, u32[]{:S(2)}) collective-permute-start(bf16[4,112,576]{2,1,0:T(8,128)(2,1)S(1)} %shard_map.57.x_ref), channel_id=1, source_target_pairs={{0,1},{1,0},{2,3},{3,2},{4,5},{5,4},{6,7},{7,6},{8,9},{9,8},{10,11... | collective-permute-start | bytes 1548296 | tf_op jit(solution)/shard_map/ppermute | solution.py:209
  46.5 0.0 collective-permute-done.4.other_ref
  46.6 0.0 copy-done.1
  46.6 0.0 copy-done
  46.6 1.0 %shard_map.59 = (f32[2,448,576]{2,1,0:T(8,128)S(1)}, f32[1,576]{1,0:T(1,128)S(1)}) custom-call(bf16[4,112,576]{2,1,0:T(8,128)(2,1)S(1)} %shard_map.57.x_ref, f32[2,448,1]{2,1,0:T(8,128)S(1)} %copy-done.1, bf16[3,448,448]{2,1,0:T(8,128)(2,1)S(1)} %copy-done, bf16[3,448,448]{2,1,0:T(8,128)(2,1)S(1)} %collective-permute-done.4.other_ref), custom_call_target="tpu_custom_call" | custom-call | tf_op jit(solution)/shard_map/pallas_call | solution.py:210
  47.6 0.6 collective-permute-done.3.x_ref
  48.2 2.0 %shard_map.60 = bf16[4,112,576]{2,1,0:T(8,128)(2,1)S(1)} custom-call(bf16[4,112,576]{2,1,0:T(8,128)(2,1)S(1)} %collective-permute-done.3.x_ref, f32[2,448,1]{2,1,0:T(8,128)S(1)} %copy-done.1, bf16[3,448,448]{2,1,0:T(8,128)(2,1)S(1)} %copy-done, bf16[3,448,448]{2,1,0:T(8,128)(2,1)S(1)} %collective-permute-done.4.other_ref, ...), custom_call_target="tpu_custom_call" | custom-call | tf_op jit(solution)/shard_map/pallas_call | solution.py:213
  50.2 0.0 copy-start.4
  50.2 13.9 %all_to_all.15.parts_ref = bf16[4,112,576]{2,1,0:T(8,128)(2,1)S(1)} all-to-all(bf16[4,112,576]{2,1,0:T(8,128)(2,1)S(1)} %shard_map.60), channel_id=1, replica_groups=mesh['y'=8,'z'=12,'x'=4,'core'=2] {'x'}, dimensions={0} | all-to-all | bytes 1032192 | tf_op jit(solution)/shard_map/all_to_all | solution.py:216
  64.1 0.6 shard_map.61
  64.7 31.5 %all_to_all.16.back_ref = bf16[96,8,112]{2,1,0:T(8,128)(2,1)S(1)} all-to-all(bf16[96,8,112]{2,1,0:T(8,128)(2,1)S(1)} %shard_map.61), channel_id=1, replica_groups=mesh['y'=8,'z'=12,'x'=4,'core'=2] {'y','z'}, dimensions={0} | all-to-all | bytes 344064 | tf_op jit(solution)/shard_map/all_to_all | solution.py:218
  96.2 0.0 copy-done.4
  96.2 0.9 shard_map.62
Async XLA Ops:
  0.0 41.9 %collective-permute-start = (bf16[112,1280]{1,0:T(8,128)(2,1)}, bf16[112,1280]{1,0:T(8,128)(2,1)S(1)}, u32[]{:S(2)}, u32[]{:S(2)}) collective-permute-start(bf16[112,1280]{1,0:T(8,128)(2,1)} %refs_0_.1), channel_id=1, source_target_pairs={{0,4},{2,6},{4,0},{6,2},{1,5},{3,7},{5,1},{7,3},{8,12},{10,14},{12... | collective-permute-start | bytes 860168 | tf_op jit(solution)/shard_map/ppermute | solution.py:186
  4.9 0.7 copy-start.3
  6.6 35.3 %all-to-all-start = ((s32[96,1,8]{2,1,0:T(1,128)}), s32[96,1,8]{2,1,0:T(1,128)S(1)}, u32[]{:S(2)}, u32[]{:S(2)}) async-start(s32[96,1,8]{2,1,0:T(1,128)} %shard_map.55), calls=%async_computation | async-start | bytes 98304 | tf_op jit(solution)/shard_map/all_to_all | solution.py:182
  28.4 14.2 %collective-permute-start.2 = (bf16[112,1280]{1,0:T(8,128)(2,1)}, bf16[112,1280]{1,0:T(8,128)(2,1)S(1)}, u32[]{:S(2)}, u32[]{:S(2)}) collective-permute-start(bf16[112,1280]{1,0:T(8,128)(2,1)} %refs_0_.1), channel_id=1, source_target_pairs={{0,6},{2,0},{4,2},{6,4},{1,7},{3,1},{5,3},{7,5},{8,14},{10,8},{12,... | collective-permute-start | bytes 860168 | tf_op jit(solution)/shard_map/ppermute | solution.py:186
  31.4 11.1 %collective-permute-start.1 = (bf16[112,1280]{1,0:T(8,128)(2,1)}, bf16[112,1280]{1,0:T(8,128)(2,1)S(1)}, u32[]{:S(2)}, u32[]{:S(2)}) collective-permute-start(bf16[112,1280]{1,0:T(8,128)(2,1)} %refs_0_.1), channel_id=1, source_target_pairs={{0,2},{2,4},{4,6},{6,0},{1,3},{3,5},{5,7},{7,1},{8,10},{10,12},{12... | collective-permute-start | bytes 860168 | tf_op jit(solution)/shard_map/ppermute | solution.py:186
  39.6 3.0 %copy-start.2 = (bf16[112,1280]{1,0:T(8,128)(2,1)S(1)}, bf16[112,1280]{1,0:T(8,128)(2,1)}, u32[]{:S(2)}) copy-start(bf16[112,1280]{1,0:T(8,128)(2,1)} %refs_0_.1) | copy-start | bytes 860164
  39.6 6.9 %collective-permute-start.4 = (bf16[3,448,448]{2,1,0:T(8,128)(2,1)}, bf16[3,448,448]{2,1,0:T(8,128)(2,1)S(1)}, u32[]{:S(2)}, u32[]{:S(2)}) collective-permute-start(bf16[3,448,448]{2,1,0:T(8,128)(2,1)} %get-tuple-element.19), channel_id=1, source_target_pairs={{0,1},{1,0},{2,3},{3,2},{4,5},{5,4},{6,7},{7,6},{8,9},{9,8},{10,11... | collective-permute-start | bytes 3612680 | tf_op jit(solution)/shard_map/ppermute | solution.py:200
  41.9 4.7 %copy-start.1 = (f32[2,448,1]{2,1,0:T(8,128)S(1)}, f32[2,448,1]{2,1,0:T(8,128)}, u32[]{:S(2)}) copy-start(f32[2,448,1]{2,1,0:T(8,128)} %get-tuple-element.17.gains_ref) | copy-start | bytes 10756
  42.5 4.0 %copy-start = (bf16[3,448,448]{2,1,0:T(8,128)(2,1)S(1)}, bf16[3,448,448]{2,1,0:T(8,128)(2,1)}, u32[]{:S(2)}) copy-start(bf16[3,448,448]{2,1,0:T(8,128)(2,1)} %get-tuple-element.18.mine_ref) | copy-start | bytes 3612676
  44.3 3.9 %collective-permute-start.3 = (bf16[4,112,576]{2,1,0:T(8,128)(2,1)S(1)}, bf16[4,112,576]{2,1,0:T(8,128)(2,1)S(1)}, u32[]{:S(2)}, u32[]{:S(2)}) collective-permute-start(bf16[4,112,576]{2,1,0:T(8,128)(2,1)S(1)} %shard_map.57.x_ref), channel_id=1, source_target_pairs={{0,1},{1,0},{2,3},{3,2},{4,5},{5,4},{6,7},{7,6},{8,9},{9,8},{10,11... | collective-permute-start | bytes 1548296 | tf_op jit(solution)/shard_map/ppermute | solution.py:209
  50.2 46.0 %copy-start.4 = (s32[1,256]{1,0:T(1,128)S(1)}, s32[1,256]{1,0:T(1,128)}, u32[]{:S(2)}) copy-start(s32[1,256]{1,0:T(1,128)} %get-tuple-element.22.slot_ref) | copy-start | bytes 3076

commit v6 on v5

--- a/solution.py
+++ b/solution.py
@@ -82,34 +82,18 @@
     send_ref[2] = dot(picks[1], w_out[...], 1, 1).astype(BF16)
 
 
-def decode_kernel(block_ref, out_ref):
-    sources, cols = block_ref.shape[0], out_ref.shape[1]
+def rows_kernel(block_ref, table_ref, out_ref):
+    sources, rows = block_ref.shape[0], table_ref.shape[1]
+    n = sources * SLOTS
     code = block_ref[:, 0, :]
-    spread = hot(iota((sources, cols), 1) // CAP == iota((sources, cols), 0))
+    spread = hot(iota((n, sources), 0) // SLOTS == iota((n, sources), 1))
     high = (code // SPLIT).astype(F32).astype(BF16)
     low = (code % SPLIT).astype(F32).astype(BF16)
-    wide = dot(high, spread, 0, 0) * SPLIT + dot(low, spread, 0, 0)
-    lane = iota((SLOTS, cols), 1)
-    local = jnp.sum(jnp.where(lane - (lane // CAP) * CAP == iota((SLOTS, cols), 0), wide, 0.0), axis=0, keepdims=True)
-    out_ref[...] = local.astype(I32) - 1
-
-
-def select_kernel(local_ref, *refs):
-    blocks, (out_ref, table, sems) = refs[:-3], refs[-3:]
-    chips, step, cols = out_ref.shape
-    rows = table.shape[2]
-    me = lax.axis_index("x")
-    loads = [
-        pltpu.make_async_copy(ref, table.at[lax.rem(me - k + chips, chips)], sems.at[k])
-        for k, ref in enumerate(blocks)
-    ]
-    for load in loads:
-        load.start()
-    pick = hot(iota((rows, cols), 0) == local_ref[...])
-    for load in loads:
-        load.wait()
-    x = dot(table[...].reshape(chips * step, rows), pick, 1, 0)
-    out_ref[...] = x.astype(BF16).reshape(out_ref.shape)
+    wide = dot(spread, high, 1, 0) * SPLIT + dot(spread, low, 1, 0)
+    row = iota((n, SLOTS), 0)
+    local = jnp.sum(jnp.where(row % SLOTS == iota((n, SLOTS), 1), wide, 0.0), axis=1, keepdims=True)
+    pick = hot(iota((n, rows), 1) == local.astype(I32) - 1)
+    out_ref[...] = dot(pick, table_ref[...], 1, 1).astype(BF16).reshape(out_ref.shape)
 
 
 def scaled_of(x_ref, gain):
@@ -135,25 +119,20 @@
     out_ref[...] = total.astype(BF16).reshape(out_ref.shape)
 
 
+def place_kernel(back_ref, slot_ref, x_ref):
+    back = back_ref[...].reshape(-1, back_ref.shape[2])
+    n, toks = back.shape[0], slot_ref.shape[1]
+    pick = hot(iota((n, toks), 0) == slot_ref[...])
+    x = dot(back, pick, 0, 0).astype(BF16)
+    for i in range(x_ref.shape[0]):
+        x_ref[i] = x
+
+
 def finish_kernel(parts_ref, x_ref, out_ref):
     total = x_ref[lax.axis_index("x")].astype(F32)
     for i in range(parts_ref.shape[0]):
         total += parts_ref[i].astype(F32)
-    encoded = total.astype(BF16)
-    cols = encoded.shape[1]
-    sources = out_ref.shape[0]
-    n = sources * SLOTS
-    row, col = iota((n, cols), 0), iota((n, cols), 1)
-    place = hot((row // SLOTS) * CAP + row % SLOTS == col)
-    place = jnp.where(row % SLOTS < CAP, place, jnp.zeros_like(place))
-    out_ref[...] = dot(place, encoded, 1, 1).astype(BF16).reshape(out_ref.shape)
-
-
-def place_kernel(back_ref, slot_ref, out_ref):
-    back = back_ref[...].reshape(-1, back_ref.shape[2])
-    n, toks = back.shape[0], slot_ref.shape[1]
-    pick = hot(iota((n, toks), 0) == slot_ref[...])
-    out_ref[...] = dot(back, pick, 0, 0).astype(BF16)
+    out_ref[...] = total.astype(BF16)
 
 
 def call(kernel, out_shape, scratch=(), vmem=32 * 1024 * 1024, flops=None, **more):
@@ -174,20 +153,11 @@
     feat_local, rows = table_cols.shape
     feats, half = w_in.shape
     toks = neighbour_ids.shape[0]
-    cols = owners * CAP
     shape = jax.ShapeDtypeStruct
 
     ids = neighbour_ids.reshape(1, toks)
     outgoing = call(functools.partial(request_kernel, rows), shape((owners, 1, SLOTS), I32))(ids)
     block = lax.all_to_all(outgoing, seq, split_axis=0, concat_axis=0, tiled=True)
-    late_cols, _ = lax.optimization_barrier((table_cols, outgoing))
-
-    def shifted(cols, k):
-        return lax.ppermute(cols, "x", [(i, (i + k) % chips) for i in range(chips)])
-
-    far = shifted(table_cols, 2)
-    block, far = lax.optimization_barrier((block, far))
-    behind = shifted(late_cols, 1), far, shifted(late_cols, 3)
     swap = [(0, 1), (1, 0)]
     anywhere, vmem = pl.BlockSpec(memory_space=pl.ANY), pl.BlockSpec(memory_space=pltpu.VMEM)
     w_mine, w_send, gains, slot = call(
@@ -199,24 +169,19 @@
     )(w_in.T, w_out, gain, ids)
     w_other = lax.ppermute(w_send, "core", swap)
 
-    local = call(decode_kernel, shape((1, cols), I32), flops=10_000_000_000)(block)
-    x_mine = call(
-        select_kernel,
-        shape((chips, feat_local, cols), BF16),
-        (pltpu.VMEM((chips, feat_local, rows), BF16), pltpu.SemaphoreType.DMA((chips,))),
-        in_specs=[vmem] + [anywhere] * chips,
-    )(local, table_cols, *behind)
+    asked = call(rows_kernel, shape((owners, SLOTS, feat_local), BF16), flops=10_000_000_000)(block, table_cols)
+    back = lax.all_to_all(asked, seq, split_axis=0, concat_axis=0, tiled=True)
+    spread = call(place_kernel, shape((chips, feat_local, toks), BF16))(back, slot)
+    x_mine = lax.all_to_all(spread, "x", split_axis=0, concat_axis=0, tiled=True)
     x_other = lax.ppermute(x_mine, "core", swap)
-    pre, square = call(first_kernel, (shape((2, half, cols), F32), shape((1, cols), F32)))(
+    pre, square = call(first_kernel, (shape((2, half, toks), F32), shape((1, toks), F32)))(
         x_mine, gains, w_mine, w_other
     )
-    parts = call(second_kernel, shape((chips, feat_local, cols), BF16), (pltpu.VMEM((2, half, cols), BF16),))(
+    parts = call(second_kernel, shape((chips, feat_local, toks), BF16), (pltpu.VMEM((2, half, toks), BF16),))(
         x_other, gains, w_mine, w_other, pre, square
     )
     parts = lax.all_to_all(parts, "x", split_axis=0, concat_axis=0, tiled=True)
-    encoded = call(finish_kernel, shape((owners, SLOTS, feat_local), BF16))(parts, x_mine)
-    back = lax.all_to_all(encoded, seq, split_axis=0, concat_axis=0, tiled=True)
-    return call(place_kernel, shape((feat_local, toks), BF16))(back, slot)
+    return call(finish_kernel, shape((feat_local, toks), BF16))(parts, x_mine)
 
 
 def solution(mesh):

time: 97.5 us -> 91.4 us (0.937)
  the two profiles are of different devices: /device:TPU:8 before, /device:TPU:1 now
where the time goes in v6:
time: 91.4 us; the launch traced here: 91 us
  blocking collectives  43.3 us (47%)
  starting transfers between devices  31.5 us (34%)
  Pallas kernels  10.1 us (11%)
  waiting for transfers between devices  5.35 us (6%)
    all_to_all x1, blocking collectives, on_device(): back = lax.all_to_all(asked, seq, split_axis=0, concat_axis=0, tiled=True)  25.7 us
    all_to_all x1, starting transfers between devices, on_device(): lax.all_to_all(outgoing, seq, split_axis=0, concat_axis=0, tiled=True)  22.5 us
    all_to_all x1, blocking collectives, on_device(): lax.all_to_all(spread, 'x', split_axis=0, concat_axis=0, tiled=True)  9.17 us
    all_to_all x1, blocking collectives, on_device(): parts = lax.all_to_all(parts, 'x', split_axis=0, concat_axis=0, tiled=True)  8.44 us
    ppermute x1, starting transfers between devices, on_device(): x_other = lax.ppermute(x_mine, 'core', swap)  6.09 us
    pallas_call x1, Pallas kernels, on_device(): call(functools.partial(blocks_kernel, owners, rows, chips), (shape((3, ha...  5.34 us
    all_to_all x1, waiting for transfers between devices, on_device(): lax.all_to_all(outgoing, seq, split_axis=0, concat_axis=0, tiled=True)  4.76 us
    ppermute x1, starting transfers between devices, on_device(): w_other = lax.ppermute(w_send, 'core', swap)  2.86 us
  transfers between devices with their start and end apart: 3, of which 2 were waited for; matrix products, arithmetic and copies ran while one was open for 0% of the time, Pallas kernels for 8%

profile of v6, /device:TPU:1, one launch (start us, length us, event | category | flops | bytes accessed | tf_op | source)
XLA Modules:
  0.0 91.0 jit_solution(7906325431076333677)
XLA Ops:
  0.0 0.0 copy-start.2
  0.0 0.7 copy-done.2
  0.7 0.0 copy-start.4
  0.7 1.0 %shard_map.55 = s32[96,1,8]{2,1,0:T(1,128)} custom-call(s32[1,256]{1,0:T(1,128)S(1)} %bitcast.3), custom_call_target="tpu_custom_call" | custom-call | tf_op jit(solution)/shard_map/pallas_call | solution.py:159
  1.7 22.5 %all-to-all-start = ((s32[96,1,8]{2,1,0:T(1,128)}), s32[96,1,8]{2,1,0:T(1,128)S(1)}, u32[]{:S(2)}, u32[]{:S(2)}) async-start(s32[96,1,8]{2,1,0:T(1,128)} %shard_map.55), calls=%async_computation | async-start | bytes 98304 | tf_op jit(solution)/shard_map/all_to_all | solution.py:160
  24.2 5.3 %shard_map.57 = (bf16[3,448,448]{2,1,0:T(8,128)(2,1)}, bf16[3,448,448]{2,1,0:T(8,128)(2,1)}, f32[2,448,1]{2,1,0:T(8,128)}, s32[1,256]{1,0:T(1,128)}) custom-call(bf16[448,896]{1,0:T(8,128)(2,1)} %bitcast.4, bf16[448,896]{1,0:T(8,128)(2,1)} %out_hbm.1, f32[896]{0:T(1024)} %gain_ref.1, s32[1,256]{1,0:T(1,128)} %bitcast.2), custom_call_target="tpu_custom_call" | custom-call | tf_op jit(solution)/shard_map/pallas_call | solution.py:163
  29.6 0.0 copy-start.3
  29.6 2.9 %collective-permute-start.1 = (bf16[3,448,448]{2,1,0:T(8,128)(2,1)}, bf16[3,448,448]{2,1,0:T(8,128)(2,1)S(1)}, u32[]{:S(2)}, u32[]{:S(2)}) collective-permute-start(bf16[3,448,448]{2,1,0:T(8,128)(2,1)} %get-tuple-element.14), channel_id=1, source_target_pairs={{0,1},{1,0},{2,3},{3,2},{4,5},{5,4},{6,7},{7,6},{8,9},{9,8},{10,11... | collective-permute-start | bytes 3612680 | tf_op jit(solution)/shard_map/ppermute | solution.py:170
  32.4 4.8 %all-to-all-done.block_ref = s32[96,1,8]{2,1,0:T(1,128)S(1)} async-done(((s32[96,1,8]{2,1,0:T(1,128)}), s32[96,1,8]{2,1,0:T(1,128)S(1)}, u32[]{:S(2)}, u32[]{:S(2)}) %all-to-all-start) | async-done | bytes 3104 | tf_op jit(solution)/shard_map/all_to_all | solution.py:160
  37.2 0.0 copy-done.4
  37.2 0.0 copy-start
  37.2 1.3 %shard_map.56 = bf16[96,8,112]{2,1,0:T(8,128)(2,1)S(1)} custom-call(s32[96,1,8]{2,1,0:T(1,128)S(1)} %all-to-all-done.block_ref, bf16[112,1280]{1,0:T(8,128)(2,1)S(1)} %copy-done.4), custom_call_target="tpu_custom_call" | custom-call | flops 10000000000 | tf_op jit(solution)/shard_map/pallas_call | solution.py:172
  38.6 0.0 copy-start.1
  38.6 25.7 %all_to_all.20.back_ref = bf16[96,8,112]{2,1,0:T(8,128)(2,1)S(1)} all-to-all(bf16[96,8,112]{2,1,0:T(8,128)(2,1)S(1)} %shard_map.56), channel_id=1, replica_groups=mesh['y'=8,'z'=12,'x'=4,'core'=2] {'y','z'}, dimensions={0} | all-to-all | bytes 344064 | tf_op jit(solution)/shard_map/all_to_all | solution.py:173
  64.2 0.0 copy-done.3
  64.2 0.2 shard_map.58
  64.5 9.2 %all_to_all.21.x_ref = bf16[4,112,256]{2,1,0:T(8,128)(2,1)S(1)} all-to-all(bf16[4,112,256]{2,1,0:T(8,128)(2,1)S(1)} %shard_map.58), channel_id=1, replica_groups=mesh['y'=8,'z'=12,'x'=4,'core'=2] {'x'}, dimensions={0} | all-to-all | bytes 458752 | tf_op jit(solution)/shard_map/all_to_all | solution.py:175
  73.7 6.1 %collective-permute-start = (bf16[4,112,256]{2,1,0:T(8,128)(2,1)S(1)}, bf16[4,112,256]{2,1,0:T(8,128)(2,1)S(1)}, u32[]{:S(2)}, u32[]{:S(2)}) collective-permute-start(bf16[4,112,256]{2,1,0:T(8,128)(2,1)S(1)} %all_to_all.21.x_ref), channel_id=1, source_target_pairs={{0,1},{1,0},{2,3},{3,2},{4,5},{5,4},{6,7},{7,6},{8,9},{9,8},{10,11... | collective-permute-start | bytes 688136 | tf_op jit(solution)/shard_map/ppermute | solution.py:176
  79.8 0.0 collective-permute-done.1.other_ref
  79.8 0.0 copy-done
  79.8 0.0 copy-done.1
  79.8 0.5 shard_map.59
  80.3 0.6 collective-permute-done.x_ref
  80.8 1.1 %shard_map.60 = bf16[4,112,256]{2,1,0:T(8,128)(2,1)S(1)} custom-call(bf16[4,112,256]{2,1,0:T(8,128)(2,1)S(1)} %collective-permute-done.x_ref, f32[2,448,1]{2,1,0:T(8,128)S(1)} %copy-done.1, bf16[3,448,448]{2,1,0:T(8,128)(2,1)S(1)} %copy-done, bf16[3,448,448]{2,1,0:T(8,128)(2,1)S(1)} %collective-permute-done.1.other_ref, ...), custom_call_target="tpu_custom_call" | custom-call | tf_op jit(solution)/shard_map/pallas_call | solution.py:180
  81.9 8.4 %all_to_all.22.parts_ref = bf16[4,112,256]{2,1,0:T(8,128)(2,1)S(1)} all-to-all(bf16[4,112,256]{2,1,0:T(8,128)(2,1)S(1)} %shard_map.60), channel_id=1, replica_groups=mesh['y'=8,'z'=12,'x'=4,'core'=2] {'x'}, dimensions={0} | all-to-all | bytes 458752 | tf_op jit(solution)/shard_map/all_to_all | solution.py:183
  90.4 0.7 shard_map.61
Async XLA Ops:
  0.0 0.7 copy-start.2
  0.7 36.5 %copy-start.4 = (bf16[112,1280]{1,0:T(8,128)(2,1)S(1)}, bf16[112,1280]{1,0:T(8,128)(2,1)}, u32[]{:S(2)}) copy-start(bf16[112,1280]{1,0:T(8,128)(2,1)} %table_ref.1) | copy-start | bytes 860164
  1.7 35.5 %all-to-all-start = ((s32[96,1,8]{2,1,0:T(1,128)}), s32[96,1,8]{2,1,0:T(1,128)S(1)}, u32[]{:S(2)}, u32[]{:S(2)}) async-start(s32[96,1,8]{2,1,0:T(1,128)} %shard_map.55), calls=%async_computation | async-start | bytes 98304 | tf_op jit(solution)/shard_map/all_to_all | solution.py:160
  29.6 34.7 %copy-start.3 = (s32[1,256]{1,0:T(1,128)S(1)}, s32[1,256]{1,0:T(1,128)}, u32[]{:S(2)}) copy-start(s32[1,256]{1,0:T(1,128)} %get-tuple-element.11.slot_ref) | copy-start | bytes 3076
  29.6 50.2 %collective-permute-start.1 = (bf16[3,448,448]{2,1,0:T(8,128)(2,1)}, bf16[3,448,448]{2,1,0:T(8,128)(2,1)S(1)}, u32[]{:S(2)}, u32[]{:S(2)}) collective-permute-start(bf16[3,448,448]{2,1,0:T(8,128)(2,1)} %get-tuple-element.14), channel_id=1, source_target_pairs={{0,1},{1,0},{2,3},{3,2},{4,5},{5,4},{6,7},{7,6},{8,9},{9,8},{10,11... | collective-permute-start | bytes 3612680 | tf_op jit(solution)/shard_map/ppermute | solution.py:170
  37.2 42.6 %copy-start = (bf16[3,448,448]{2,1,0:T(8,128)(2,1)S(1)}, bf16[3,448,448]{2,1,0:T(8,128)(2,1)}, u32[]{:S(2)}) copy-start(bf16[3,448,448]{2,1,0:T(8,128)(2,1)} %get-tuple-element.13.mine_ref) | copy-start | bytes 3612676
  38.6 41.2 %copy-start.1 = (f32[2,448,1]{2,1,0:T(8,128)S(1)}, f32[2,448,1]{2,1,0:T(8,128)}, u32[]{:S(2)}) copy-start(f32[2,448,1]{2,1,0:T(8,128)} %get-tuple-element.12.gains_ref) | copy-start | bytes 10756
  73.7 7.2 %collective-permute-start = (bf16[4,112,256]{2,1,0:T(8,128)(2,1)S(1)}, bf16[4,112,256]{2,1,0:T(8,128)(2,1)S(1)}, u32[]{:S(2)}, u32[]{:S(2)}) collective-permute-start(bf16[4,112,256]{2,1,0:T(8,128)(2,1)S(1)} %all_to_all.21.x_ref), channel_id=1, source_target_pairs={{0,1},{1,0},{2,3},{3,2},{4,5},{5,4},{6,7},{7,6},{8,9},{9,8},{10,11... | collective-permute-start | bytes 688136 | tf_op jit(solution)/shard_map/ppermute | solution.py:176

commit v7 on v6

--- a/solution.py
+++ b/solution.py
@@ -7,7 +7,7 @@
 from jax.experimental.pallas import tpu as pltpu
 from jax.sharding import Mesh, PartitionSpec as P
 
-CAP = 6
+TALL, WIDE, LANES = 2, 3, 128
 SLOTS = 8
 SPLIT = 64
 NORM_EPS = 1e-05
@@ -52,48 +52,67 @@
     return sum((r >= k * block).astype(I32) for k in range(1, count))
 
 
-def blocks_kernel(owners, rows, chips, in_hbm, out_hbm, gain_ref, ids_ref, mine_ref, send_ref, gains_ref, slot_ref,
-                  w_in, w_out, sems):
+def side_of(side, chips, n):
+    row, lane = iota((n, 2 * n), 0), iota((n, 2 * n), 1)
+    return hot(lane == row + third(row, n // chips, chips) * (n // chips) + side * (n // chips))
+
+
+def send_kernel(chips, in_hbm, out_hbm, send_ref, mark_ref, w_in, w_out, sems):
     load_in = pltpu.make_async_copy(in_hbm, w_in, sems.at[0])
     load_out = pltpu.make_async_copy(out_hbm, w_out, sems.at[1])
     load_in.start()
     load_out.start()
+    mark_ref[...] = jnp.zeros_like(mark_ref)
+    core = lax.axis_index("core")
+    n = w_in.shape[1] // 2
+    other, own = side_of(1 - core, chips, n), side_of(core, chips, n)
+    load_in.wait()
+    send_ref[0] = dot(w_in[...], other, 1, 1).astype(BF16)
+    send_ref[1] = dot(w_in[...], own, 1, 1).astype(BF16)
+    load_out.wait()
+    send_ref[2] = dot(other, w_out[...], 1, 1).astype(BF16)
+
+
+def keep_kernel(owners, rows, chips, out_hbm, gain_ref, ids_ref, keep_ref, gains_ref, slot_ref, w_out, sems):
+    load = pltpu.make_async_copy(out_hbm, w_out, sems.at[0])
+    load.start()
     owner, _, rank, _ = ranked(ids_ref[...], owners, rows)
     slot_ref[...] = owner * SLOTS + rank
     core = lax.axis_index("core")
-    half, feats = w_in.shape
-    n = feats // 2
-    block = n // chips
+    feats = w_out.shape[1]
+    block = feats // (2 * chips)
     gain = jnp.transpose(jnp.broadcast_to(gain_ref[...].reshape(1, feats), (8, feats)))[:, :1]
     for i in range(chips):
         for j in range(2):
             at = (2 * i + j) * block
             gains_ref[jnp.where(core == j, 0, 1), pl.ds(i * block, block), :] = gain[at:at + block]
-    row, lane = iota((n, feats), 0), iota((n, feats), 1)
-    base = row + third(row, block, chips) * block
-    picks = [hot(lane == base + side * block) for side in (core, 1 - core)]
-    load_in.wait()
-    for i, pick in enumerate(picks):
-        part = dot(w_in[...], pick, 1, 1).astype(BF16)
-        mine_ref[i] = part
-        send_ref[1 - i] = part
-    load_out.wait()
-    mine_ref[2] = dot(picks[0], w_out[...], 1, 1).astype(BF16)
-    send_ref[2] = dot(picks[1], w_out[...], 1, 1).astype(BF16)
-
-
-def rows_kernel(block_ref, table_ref, out_ref):
-    sources, rows = block_ref.shape[0], table_ref.shape[1]
-    n = sources * SLOTS
+    pick = side_of(core, chips, feats // 2)
+    load.wait()
+    keep_ref[...] = dot(pick, w_out[...], 1, 1).astype(BF16)
+
+
+def rows_kernel(block_ref, table_hbm, _, out_ref, table, sems):
+    load = pltpu.make_async_copy(table_hbm, table, sems.at[0])
+    load.start()
+    sources = block_ref.shape[0]
+    feats, rows = table.shape
+    n = sources * TALL
     code = block_ref[:, 0, :]
-    spread = hot(iota((n, sources), 0) // SLOTS == iota((n, sources), 1))
+    spread = hot(iota((n, sources), 0) // TALL == iota((n, sources), 1))
     high = (code // SPLIT).astype(F32).astype(BF16)
     low = (code % SPLIT).astype(F32).astype(BF16)
     wide = dot(spread, high, 1, 0) * SPLIT + dot(spread, low, 1, 0)
-    row = iota((n, SLOTS), 0)
-    local = jnp.sum(jnp.where(row % SLOTS == iota((n, SLOTS), 1), wide, 0.0), axis=1, keepdims=True)
-    pick = hot(iota((n, rows), 1) == local.astype(I32) - 1)
-    out_ref[...] = dot(pick, table_ref[...], 1, 1).astype(BF16).reshape(out_ref.shape)
+    row, slot = iota((n, SLOTS), 0) % TALL, iota((n, SLOTS), 1)
+    lane = iota((n, rows), 1)
+    picks = []
+    for j in range(WIDE):
+        local = jnp.sum(jnp.where(slot == row * WIDE + j, wide, 0.0), axis=1, keepdims=True).astype(I32) - 1
+        picks.append(hot(lane == local))
+    out_ref[...] = jnp.zeros_like(out_ref)
+    load.wait()
+    for j, pick in enumerate(picks):
+        x = dot(pick, table[...], 1, 1)
+        out_ref[:, :, j * LANES:j * LANES + feats] = x.reshape(sources, TALL, feats).astype(BF16)
 
 
 def scaled_of(x_ref, gain):
@@ -104,27 +123,33 @@
 
 def first_kernel(x_ref, gains_ref, mine_ref, other_ref, pre_ref, square_ref):
     scaled, square_ref[...] = scaled_of(x_ref, gains_ref[0])
-    for i, w in enumerate((mine_ref, other_ref)):
-        pre_ref[i] = dot(w[0], scaled, 1, 0)
-
-
-def second_kernel(x_ref, gains_ref, mine_ref, other_ref, pre_ref, square_ref, out_ref, hidden):
+    pre_ref[0] = dot(mine_ref[1], scaled, 1, 0)
+    pre_ref[1] = dot(other_ref[0], scaled, 1, 0)
+
+
+def second_kernel(x_ref, gains_ref, mine_ref, other_ref, keep_ref, pre_ref, square_ref, out_ref, hidden):
     scaled, squares = scaled_of(x_ref, gains_ref[1])
     squares += square_ref[...]
     scale = lax.rsqrt(squares / (2 * scaled.shape[0]) + NORM_EPS)
-    for i, w in enumerate((mine_ref, other_ref)):
-        pre = (pre_ref[i] + dot(w[1], scaled, 1, 0)) * scale
+    for i, w in enumerate((mine_ref[0], other_ref[1])):
+        pre = (pre_ref[i] + dot(w, scaled, 1, 0)) * scale
         hidden[i] = jax.nn.gelu(pre, approximate=True).astype(BF16)
-    total = dot(mine_ref[2], hidden[0], 1, 0) + dot(other_ref[2], hidden[1], 1, 0)
+    total = dot(keep_ref[...], hidden[0], 1, 0) + dot(other_ref[2], hidden[1], 1, 0)
     out_ref[...] = total.astype(BF16).reshape(out_ref.shape)
 
 
 def place_kernel(back_ref, slot_ref, x_ref):
-    back = back_ref[...].reshape(-1, back_ref.shape[2])
-    n, toks = back.shape[0], slot_ref.shape[1]
-    pick = hot(iota((n, toks), 0) == slot_ref[...])
-    x = dot(back, pick, 0, 0).astype(BF16)
-    for i in range(x_ref.shape[0]):
+    chips, feats, toks = x_ref.shape
+    n = back_ref.shape[0] * TALL
+    slot = slot_ref[...]
+    owner, rank = slot // SLOTS, slot % SLOTS
+    x = jnp.zeros((feats, toks), F32)
+    for j in range(WIDE):
+        back = back_ref[:, :, j * LANES:j * LANES + feats].astype(F32).reshape(n, feats).astype(BF16)
+        at = jnp.where(rank % WIDE == j, owner * TALL + rank // WIDE, -1)
+        x += dot(back, hot(iota((n, toks), 0) == at), 0, 0)
+    x = x.astype(BF16)
+    for i in range(chips):
         x_ref[i] = x
 
 
@@ -160,25 +185,39 @@
     block = lax.all_to_all(outgoing, seq, split_axis=0, concat_axis=0, tiled=True)
     swap = [(0, 1), (1, 0)]
     anywhere, vmem = pl.BlockSpec(memory_space=pl.ANY), pl.BlockSpec(memory_space=pltpu.VMEM)
-    w_mine, w_send, gains, slot = call(
-        functools.partial(blocks_kernel, owners, rows, chips),
-        (shape((3, half, half), BF16),) * 2 + (shape((2, half, 1), F32), shape((1, toks), I32)),
+    w_in_t = w_in.T
+    w_send, mark = call(
+        functools.partial(send_kernel, chips),
+        (shape((3, half, half), BF16), shape((8, 128), I32)),
         (pltpu.VMEM((half, feats), BF16), pltpu.VMEM((half, feats), BF16), pltpu.SemaphoreType.DMA((2,))),
-        in_specs=[anywhere, anywhere, vmem, vmem],
+        in_specs=[anywhere, anywhere],
         vmem=60_000_000,
-    )(w_in.T, w_out, gain, ids)
-    w_other = lax.ppermute(w_send, "core", swap)
-
-    asked = call(rows_kernel, shape((owners, SLOTS, feat_local), BF16), flops=10_000_000_000)(block, table_cols)
+    )(w_in_t, w_out)
+    asked = call(
+        rows_kernel,
+        shape((owners, TALL, WIDE * LANES), BF16),
+        (pltpu.VMEM((feat_local, rows), BF16), pltpu.SemaphoreType.DMA((1,))),
+        in_specs=[vmem, anywhere, anywhere],
+        flops=10_000_000_000,
+    )(block, table_cols, mark)
     back = lax.all_to_all(asked, seq, split_axis=0, concat_axis=0, tiled=True)
-    spread = call(place_kernel, shape((chips, feat_local, toks), BF16))(back, slot)
+    w_later, gain_later, _ = lax.optimization_barrier((w_send, gain, block))
+    w_other = lax.ppermute(w_later, "core", swap)
+    w_keep, gains, slot = call(
+        functools.partial(keep_kernel, owners, rows, chips),
+        (shape((half, half), BF16), shape((2, half, 1), F32), shape((1, toks), I32)),
+        (pltpu.VMEM((half, feats), BF16), pltpu.SemaphoreType.DMA((1,))),
+        in_specs=[anywhere, vmem, vmem],
+        vmem=32_000_000,
+    )(w_out, gain_later, ids)
+    spread = call(place_kernel, shape((chips, feat_local, toks), BF16), flops=10_000_000_000)(back, slot)
     x_mine = lax.all_to_all(spread, "x", split_axis=0, concat_axis=0, tiled=True)
     x_other = lax.ppermute(x_mine, "core", swap)
     pre, square = call(first_kernel, (shape((2, half, toks), F32), shape((1, toks), F32)))(
-        x_mine, gains, w_mine, w_other
+        x_mine, gains, w_send, w_other
     )
     parts = call(second_kernel, shape((chips, feat_local, toks), BF16), (pltpu.VMEM((2, half, toks), BF16),))(
-        x_other, gains, w_mine, w_other, pre, square
+        x_other, gains, w_send, w_other, w_keep, pre, square
     )
     parts = lax.all_to_all(parts, "x", split_axis=0, concat_axis=0, tiled=True)
     return call(finish_kernel, shape((feat_local, toks), BF16))(parts, x_mine)

time: 91.4 us -> 88.2 us (0.965)
  blocking collectives: 43.3 us -> 17.6 us
  waiting for transfers between devices: 5.35 us -> 17.5 us
  starting transfers between devices: 31.5 us -> 39.4 us
  local copies, waits for them, and re-layouts: 0.69 us -> 2.15 us
    all_to_all x1 -> x0, blocking collectives: 25.7 us -> none  [on_device(): back = lax.all_to_all(asked, seq, split_axis=0, concat_axis=0, tiled=True)]
    all_to_all x0 -> x1, waiting for transfers between devices: none -> 8.02 us  [on_device(): back = lax.all_to_all(asked, seq, split_axis=0, concat_axis=0, tiled=True)]
    all_to_all x0 -> x1, starting transfers between devices: none -> 6.15 us  [on_device(): back = lax.all_to_all(asked, seq, split_axis=0, concat_axis=0, tiled=True)]
    all_to_all x1, waiting for transfers between devices: 4.76 us -> 8.92 us  [on_device(): lax.all_to_all(outgoing, seq, split_axis=0, concat_axis=0, tiled=True)]
    unnamed x10 -> x18, local copies, waits for them, and re-layouts: 0.69 us -> 2.15 us
    ppermute x1, starting transfers between devices: 2.86 us -> 3.81 us  [on_device(): w_other = lax.ppermute(w_later, 'core', swap)]
    pallas_call x3 -> x4, Pallas kernels: 6.93 us -> 7.8 us  [the longest x1 4.06 us: on_device(): call(functools.partial(send_kernel, chips), (shape((3, half, half), BF16)...]
  transfers between devices with their start and end apart: 3 -> 4, of which waited for: 2 -> 3; matrix products, arithmetic and copies ran while one was open for 0% -> 0% of each run, Pallas kernels for 8% -> 7%
where the time goes in v7:
time: 88.2 us; the launch traced here: 87.8 us
  starting transfers between devices  39.4 us (45%)
  blocking collectives  17.6 us (20%)
  waiting for transfers between devices  17.5 us (20%)
  Pallas kernels  11 us (12%)
  local copies, waits for them, and re-layouts  2.15 us (2%)
    all_to_all x1, starting transfers between devices, on_device(): lax.all_to_all(outgoing, seq, split_axis=0, concat_axis=0, tiled=True)  22.5 us
    all_to_all x1, blocking collectives, on_device(): lax.all_to_all(spread, 'x', split_axis=0, concat_axis=0, tiled=True)  9.17 us
    all_to_all x1, waiting for transfers between devices, on_device(): lax.all_to_all(outgoing, seq, split_axis=0, concat_axis=0, tiled=True)  8.92 us
    all_to_all x1, blocking collectives, on_device(): parts = lax.all_to_all(parts, 'x', split_axis=0, concat_axis=0, tiled=True)  8.45 us
    all_to_all x1, waiting for transfers between devices, on_device(): back = lax.all_to_all(asked, seq, split_axis=0, concat_axis=0, tiled=True)  8.02 us
    ppermute x1, starting transfers between devices, on_device(): x_other = lax.ppermute(x_mine, 'core', swap)  6.86 us
    all_to_all x1, starting transfers between devices, on_device(): back = lax.all_to_all(asked, seq, split_axis=0, concat_axis=0, tiled=True)  6.15 us
    pallas_call x1, Pallas kernels, on_device(): call(functools.partial(send_kernel, chips), (shape((3, half, half), BF16)...  4.06 us
  transfers between devices with their start and end apart: 4, of which 3 were waited for; matrix products, arithmetic and copies ran while one was open for 0% of the time, Pallas kernels for 7%

profile of v7, /device:TPU:1, one launch (start us, length us, event | category | flops | bytes accessed | tf_op | source)
XLA Modules:
  0.0 87.8 jit_solution(16096297892261436776)
XLA Ops:
  0.0 0.0 copy-start.5
  0.0 0.7 copy-done.5
  0.7 0.0 copy-start.7
  0.7 1.0 %shard_map.55 = s32[96,1,8]{2,1,0:T(1,128)} custom-call(s32[1,256]{1,0:T(1,128)S(1)} %bitcast.2), custom_call_target="tpu_custom_call" | custom-call | tf_op jit(solution)/shard_map/pallas_call | solution.py:184
  1.7 22.5 %all-to-all-start = ((s32[96,1,8]{2,1,0:T(1,128)}), s32[96,1,8]{2,1,0:T(1,128)S(1)}, u32[]{:S(2)}, u32[]{:S(2)}) async-start(s32[96,1,8]{2,1,0:T(1,128)} %shard_map.55), calls=%async_computation | async-start | bytes 98304 | tf_op jit(solution)/shard_map/all_to_all | solution.py:185
  24.2 4.1 %shard_map.56 = (bf16[3,448,448]{2,1,0:T(8,128)(2,1)}, s32[8,128]{1,0:T(8,128)}) custom-call(bf16[448,896]{1,0:T(8,128)(2,1)} %bitcast.4, bf16[448,896]{1,0:T(8,128)(2,1)} %out_hbm.3), custom_call_target="tpu_custom_call" | custom-call | tf_op jit(solution)/shard_map/pallas_call | solution.py:189
  28.3 8.9 %all-to-all-done.block_ref = s32[96,1,8]{2,1,0:T(1,128)S(1)} async-done(((s32[96,1,8]{2,1,0:T(1,128)}), s32[96,1,8]{2,1,0:T(1,128)S(1)}, u32[]{:S(2)}, u32[]{:S(2)}) %all-to-all-start) | async-done | bytes 3104 | tf_op jit(solution)/shard_map/all_to_all | solution.py:185
  37.2 0.0 copy-done.7
  37.2 0.0 copy-start.8
  37.2 0.7 copy-done.8
  37.9 2.4 %shard_map.57 = bf16[96,2,384]{2,1,0:T(2,128)(2,1)} custom-call(s32[96,1,8]{2,1,0:T(1,128)S(1)} %all-to-all-done.block_ref, bf16[112,1280]{1,0:T(8,128)(2,1)S(1)} %copy-done.7, s32[8,128]{1,0:T(8,128)S(1)} %copy-done.8), custom_call_target="tpu_custom_call" | custom-call | flops 10000000000 | tf_op jit(solution)/shard_map/pallas_call | solution.py:196
  40.3 6.2 %all-to-all-start.1 = ((bf16[96,2,384]{2,1,0:T(2,128)(2,1)}), bf16[96,2,384]{2,1,0:T(2,128)(2,1)S(1)}, u32[]{:S(2)}, u32[]{:S(2)}) async-start(bf16[96,2,384]{2,1,0:T(2,128)(2,1)} %shard_map.57), calls=%async_computation.1 | async-start | bytes 294912 | tf_op jit(solution)/shard_map/all_to_all | solution.py:203
  46.4 0.0 copy-done.1
  46.4 0.0 copy-done.4
  46.5 0.0 copy-done.6
  46.5 1.1 %shard_map.58 = (bf16[448,448]{1,0:T(8,128)(2,1)S(1)}, f32[2,448,1]{2,1,0:T(8,128)S(1)}, s32[1,256]{1,0:T(1,128)S(1)}) custom-call(bf16[448,896]{1,0:T(8,128)(2,1)S(1)} %copy-done.1, f32[896]{0:T(1024)S(1)} %copy-done.4, s32[1,256]{1,0:T(1,128)S(1)} %bitcast.3), custom_call_target="tpu_custom_call" | custom-call | tf_op jit(solution)/shard_map/pallas_call | solution.py:206
  47.6 0.0 copy-start.2
  47.6 0.8 copy-done.2
  48.3 0.0 copy-done
  48.3 3.8 %collective-permute-start.1 = (bf16[3,448,448]{2,1,0:T(8,128)(2,1)S(1)}, bf16[3,448,448]{2,1,0:T(8,128)(2,1)S(1)}, u32[]{:S(2)}, u32[]{:S(2)}) collective-permute-start(bf16[3,448,448]{2,1,0:T(8,128)(2,1)S(1)} %copy-done), channel_id=1, source_target_pairs={{0,1},{1,0},{2,3},{3,2},{4,5},{5,4},{6,7},{7,6},{8,9},{9,8},{10,11... | collective-permute-start | bytes 3612680 | tf_op jit(solution)/shard_map/ppermute | solution.py:205
  52.1 8.0 %all-to-all-done.1.back_ref = bf16[96,2,384]{2,1,0:T(2,128)(2,1)S(1)} async-done(((bf16[96,2,384]{2,1,0:T(2,128)(2,1)}), bf16[96,2,384]{2,1,0:T(2,128)(2,1)S(1)}, u32[]{:S(2)}, u32[]{:S(2)}) %all-to-all-start.1) | async-done | bytes 147488 | tf_op jit(solution)/shard_map/all_to_all | solution.py:203
  60.2 0.3 shard_map.59
  60.5 9.2 %all_to_all.20.x_ref = bf16[4,112,256]{2,1,0:T(8,128)(2,1)S(1)} all-to-all(bf16[4,112,256]{2,1,0:T(8,128)(2,1)S(1)} %shard_map.59), channel_id=1, replica_groups=mesh['y'=8,'z'=12,'x'=4,'core'=2] {'x'}, dimensions={0} | all-to-all | bytes 458752 | tf_op jit(solution)/shard_map/all_to_all | solution.py:214
  69.6 6.9 %collective-permute-start = (bf16[4,112,256]{2,1,0:T(8,128)(2,1)S(1)}, bf16[4,112,256]{2,1,0:T(8,128)(2,1)S(1)}, u32[]{:S(2)}, u32[]{:S(2)}) collective-permute-start(bf16[4,112,256]{2,1,0:T(8,128)(2,1)S(1)} %all_to_all.20.x_ref), channel_id=1, source_target_pairs={{0,1},{1,0},{2,3},{3,2},{4,5},{5,4},{6,7},{7,6},{8,9},{9,8},{10,11... | collective-permute-start | bytes 688136 | tf_op jit(solution)/shard_map/ppermute | solution.py:215
  76.5 0.0 collective-permute-done.1.other_ref
  76.5 0.0 copy-start.3
  76.5 0.5 shard_map.60
  77.0 0.6 collective-permute-done.x_ref
  77.6 0.0 copy-done.3
  77.6 1.1 %shard_map.61 = bf16[4,112,256]{2,1,0:T(8,128)(2,1)S(1)} custom-call(bf16[4,112,256]{2,1,0:T(8,128)(2,1)S(1)} %collective-permute-done.x_ref, f32[2,448,1]{2,1,0:T(8,128)S(1)} %get-tuple-element.18.gains_ref, bf16[3,448,448]{2,1,0:T(8,128)(2,1)S(1)} %copy-done, bf16[3,448,448]{2,1,0:T(8,128)(2,1)S(1)} %collective-permute-done.1.other_ref, ...), custom_call_target="tpu_custom_call" | custom-call | tf_op jit(solution)/shard_map/pallas_call | solution.py:219
  78.7 8.4 %all_to_all.21.parts_ref = bf16[4,112,256]{2,1,0:T(8,128)(2,1)S(1)} all-to-all(bf16[4,112,256]{2,1,0:T(8,128)(2,1)S(1)} %shard_map.61), channel_id=1, replica_groups=mesh['y'=8,'z'=12,'x'=4,'core'=2] {'x'}, dimensions={0} | all-to-all | bytes 458752 | tf_op jit(solution)/shard_map/all_to_all | solution.py:222
  87.1 0.7 shard_map.62
  (4 shorter events, 0.0 us)
Async XLA Ops:
  0.0 0.7 copy-start.5
  0.7 36.5 %copy-start.7 = (bf16[112,1280]{1,0:T(8,128)(2,1)S(1)}, bf16[112,1280]{1,0:T(8,128)(2,1)}, u32[]{:S(2)}) copy-start(bf16[112,1280]{1,0:T(8,128)(2,1)} %table_hbm.1) | copy-start | bytes 860164
  1.7 35.5 %all-to-all-start = ((s32[96,1,8]{2,1,0:T(1,128)}), s32[96,1,8]{2,1,0:T(1,128)S(1)}, u32[]{:S(2)}, u32[]{:S(2)}) async-start(s32[96,1,8]{2,1,0:T(1,128)} %shard_map.55), calls=%async_computation | async-start | bytes 98304 | tf_op jit(solution)/shard_map/all_to_all | solution.py:185
  37.2 0.7 copy-start.8
  37.9 8.5 %copy-start.1 = (bf16[448,896]{1,0:T(8,128)(2,1)S(1)}, bf16[448,896]{1,0:T(8,128)(2,1)}, u32[]{:S(2)}) copy-start(bf16[448,896]{1,0:T(8,128)(2,1)} %out_hbm.3) | copy-start | bytes 2408452
  37.9 8.6 %copy-start.4 = (f32[896]{0:T(1024)S(1)}, f32[896]{0:T(1024)}, u32[]{:S(2)}) copy-start(f32[896]{0:T(1024)} %gain_ref) | copy-start | bytes 10756
  37.9 8.6 %copy-start.6 = (s32[256]{0:T(256)S(1)}, s32[256]{0:T(256)}, u32[]{:S(2)}) copy-start(s32[256]{0:T(256)} %param.5) | copy-start | bytes 3076
  37.9 10.4 %copy-start = (bf16[3,448,448]{2,1,0:T(8,128)(2,1)S(1)}, bf16[3,448,448]{2,1,0:T(8,128)(2,1)}, u32[]{:S(2)}) copy-start(bf16[3,448,448]{2,1,0:T(8,128)(2,1)} %get-tuple-element.19.mine_ref) | copy-start | bytes 3612676
  40.3 19.9 %all-to-all-start.1 = ((bf16[96,2,384]{2,1,0:T(2,128)(2,1)}), bf16[96,2,384]{2,1,0:T(2,128)(2,1)S(1)}, u32[]{:S(2)}, u32[]{:S(2)}) async-start(bf16[96,2,384]{2,1,0:T(2,128)(2,1)} %shard_map.57), calls=%async_computation.1 | async-start | bytes 294912 | tf_op jit(solution)/shard_map/all_to_all | solution.py:203
  47.6 0.8 copy-start.2
  48.3 28.2 %collective-permute-start.1 = (bf16[3,448,448]{2,1,0:T(8,128)(2,1)S(1)}, bf16[3,448,448]{2,1,0:T(8,128)(2,1)S(1)}, u32[]{:S(2)}, u32[]{:S(2)}) collective-permute-start(bf16[3,448,448]{2,1,0:T(8,128)(2,1)S(1)} %copy-done), channel_id=1, source_target_pairs={{0,1},{1,0},{2,3},{3,2},{4,5},{5,4},{6,7},{7,6},{8,9},{9,8},{10,11... | collective-permute-start | bytes 3612680 | tf_op jit(solution)/shard_map/ppermute | solution.py:205
  69.6 8.0 %collective-permute-start = (bf16[4,112,256]{2,1,0:T(8,128)(2,1)S(1)}, bf16[4,112,256]{2,1,0:T(8,128)(2,1)S(1)}, u32[]{:S(2)}, u32[]{:S(2)}) collective-permute-start(bf16[4,112,256]{2,1,0:T(8,128)(2,1)S(1)} %all_to_all.20.x_ref), channel_id=1, source_target_pairs={{0,1},{1,0},{2,3},{3,2},{4,5},{5,4},{6,7},{7,6},{8,9},{9,8},{10,11... | collective-permute-start | bytes 688136 | tf_op jit(solution)/shard_map/ppermute | solution.py:215
  76.5 1.1 %copy-start.3 = (bf16[448,448]{1,0:T(8,128)(2,1)S(1)}, bf16[448,448]{1,0:T(8,128)(2,1)}, u32[]{:S(2)}) copy-start(bf16[448,448]{1,0:T(8,128)(2,1)} %copy-done.2) | copy-start | bytes 1204228

commit v8 on v6

v8 whole, which is shorter than its diff:
```python
import functools

import jax
import jax.numpy as jnp
from jax import lax
from jax.experimental import pallas as pl
from jax.experimental.pallas import tpu as pltpu
from jax.sharding import Mesh, PartitionSpec as P

TALL, WIDE, LANES = 2, 3, 128
SLOTS = 8
SPLIT = 64
NORM_EPS = 1e-05
F32 = jnp.float32
BF16 = jnp.bfloat16
I32 = jnp.int32


def iota(shape, dim):
    return lax.broadcasted_iota(I32, shape, dim)


def hot(mask):
    return jnp.where(mask, 1.0, 0.0).astype(BF16)


def dot(a, b, ca, cb):
    return lax.dot_general(a, b, (((ca,), (cb,)), ((), ())), preferred_element_type=F32)


def ranked(ids, owners, rows):
    toks = ids.shape[1]
    owner = ids // rows
    mine = iota((owners, toks), 0) == owner
    mine_hot = hot(mine)
    earlier = hot(iota((toks, toks), 0) < iota((toks, toks), 1))
    count = dot(mine_hot, earlier, 1, 0)
    rank = jnp.sum(jnp.where(mine, count, 0.0), axis=0, keepdims=True).astype(I32)
    return owner, ids - owner * rows + 1, rank, mine_hot


def request_kernel(rows, ids_ref, out_ref):
    owner, code, rank, mine_hot = ranked(ids_ref[...], out_ref.shape[0], rows)
    at = iota((SLOTS, ids_ref.shape[1]), 0) == rank
    high = jnp.where(at, code // SPLIT, 0).astype(F32).astype(BF16)
    low = jnp.where(at, code % SPLIT, 0).astype(F32).astype(BF16)
    out = dot(mine_hot, high, 1, 1) * SPLIT + dot(mine_hot, low, 1, 1)
    out_ref[:, 0, :] = out.astype(I32)


def third(r, block, count):
    return sum((r >= k * block).astype(I32) for k in range(1, count))


def blocks_kernel(owners, rows, chips, w_ref, ids_ref, keep_ref, send_ref, slot_ref, mark_ref):
    mark_ref[...] = jnp.zeros_like(mark_ref)
    owner, _, rank, _ = ranked(ids_ref[...], owners, rows)
    slot_ref[...] = owner * SLOTS + rank
    feats = w_ref.shape[1]
    n = feats // 2
    block = n // chips
    core = lax.axis_index("core")
    row, lane = iota((n, feats), 0), iota((n, feats), 1)
    base = row + third(row, block, chips) * block
    send_ref[...] = dot(hot(lane == base + (1 - core) * block), w_ref[...], 1, 1).astype(BF16)
    keep_ref[...] = dot(hot(lane == base + core * block), w_ref[...], 1, 1).astype(BF16)


def rows_kernel(block_ref, table_ref, _, out_ref, pick):
    sources = block_ref.shape[0]
    feats, rows = table_ref.shape
    n = sources * TALL
    code = block_ref[:, 0, :]
    spread = hot(iota((n, sources), 0) // TALL == iota((n, sources), 1))
    high = (code // SPLIT).astype(F32).astype(BF16)
    low = (code % SPLIT).astype(F32).astype(BF16)
    wide = dot(spread, high, 1, 0) * SPLIT + dot(spread, low, 1, 0)
    row, slot = iota((n, SLOTS), 0) % TALL, iota((n, SLOTS), 1)
    lane = iota((n, rows), 1)
    for j in range(WIDE):
        local = jnp.sum(jnp.where(slot == row * WIDE + j, wide, 0.0), axis=1, keepdims=True).astype(I32) - 1
        pick[j * n:(j + 1) * n] = hot(lane == local)
    out_ref[...] = jnp.zeros_like(out_ref)
    x = dot(pick[...], table_ref[...], 1, 1)
    for j in range(WIDE):
        out_ref[:, :, j * LANES:j * LANES + feats] = x[j * n:(j + 1) * n].reshape(sources, TALL, feats).astype(BF16)


def layer_kernel(x_ref, gain_ref, in_a, in_b, out_a, out_b, part_ref):
    feats = gain_ref.shape[0]
    x = x_ref[...].reshape(feats, x_ref.shape[2]).astype(F32)
    gain = jnp.transpose(jnp.broadcast_to(gain_ref[...].reshape(1, feats), (8, feats)))[:, :1]
    scaled = (gain * x).astype(BF16)
    scale = lax.rsqrt(jnp.sum(x * x, axis=0, keepdims=True) / feats + NORM_EPS)
    total = 0.0
    for w_in, w_out in ((in_a, out_a), (in_b, out_b)):
        pre = dot(w_in[...], scaled, 1, 0) * scale
        hidden = jax.nn.gelu(pre, approximate=True).astype(BF16)
        total += dot(w_out[...], hidden, 1, 0)
    part_ref[...] = total.astype(BF16).reshape(part_ref.shape)


def place_kernel(back_ref, slot_ref, x_ref):
    copies, feats, toks = x_ref.shape
    n = back_ref.shape[0] * TALL
    slot = slot_ref[...]
    owner, rank = slot // SLOTS, slot % SLOTS
    x = jnp.zeros((feats, toks), F32)
    for j in range(WIDE):
        back = back_ref[:, :, j * LANES:j * LANES + feats].astype(F32).reshape(n, feats).astype(BF16)
        at = jnp.where(rank % WIDE == j, owner * TALL + rank // WIDE, -1)
        x += dot(back, hot(iota((n, toks), 0) == at), 0, 0)
    x = x.astype(BF16)
    for i in range(copies):
        x_ref[i] = x


def finish_kernel(parts_ref, x_ref, out_ref):
    total = x_ref[2 * lax.axis_index("x") + lax.axis_index("core")].astype(F32)
    for i in range(parts_ref.shape[0]):
        total += parts_ref[i].astype(F32)
    out_ref[...] = total.astype(BF16)


def call(kernel, out_shape, scratch=(), vmem=32 * 1024 * 1024, flops=None, **more):
    return pl.pallas_call(
        kernel,
        out_shape=out_shape,
        scratch_shapes=list(scratch),
        cost_estimate=flops and pl.CostEstimate(flops=flops, bytes_accessed=0, transcendentals=0),
        compiler_params=pltpu.CompilerParams(vmem_limit_bytes=vmem),
        **more,
    )


def on_device(neighbour_ids, table_cols, gain, w_in, w_out):
    seq = ("y", "z")
    owners = lax.axis_size(seq)
    chips = lax.axis_size("x")
    feat_local, rows = table_cols.shape
    feats, half = w_in.shape
    toks = neighbour_ids.shape[0]
    shape = jax.ShapeDtypeStruct

    ids = neighbour_ids.reshape(1, toks)
    outgoing = call(functools.partial(request_kernel, rows), shape((owners, 1, SLOTS), I32))(ids)
    block = lax.all_to_all(outgoing, seq, split_axis=0, concat_axis=0, tiled=True)
    swap = [(0, 1), (1, 0)]
    anywhere, vmem = pl.BlockSpec(memory_space=pl.ANY), pl.BlockSpec(memory_space=pltpu.VMEM)
    out_own, out_send, slot, mark = call(
        functools.partial(blocks_kernel, owners, rows, chips),
        (shape((feats // 2, half), BF16),) * 2 + (shape((1, toks), I32), shape((8, 128), I32)),
    )(w_out, ids)
    asked = call(
        rows_kernel,
        shape((owners, TALL, WIDE * LANES), BF16),
        (pltpu.VMEM((owners * TALL * WIDE, rows), BF16),),
        in_specs=[vmem, vmem, anywhere],
        flops=10_000_000_000,
    )(block, table_cols, mark)
    back = lax.all_to_all(asked, seq, split_axis=0, concat_axis=0, tiled=True)
    in_own = w_in.T
    in_later, out_later, _ = lax.optimization_barrier((in_own, out_send, block))
    in_other = lax.ppermute(in_later, "core", swap)
    out_other = lax.ppermute(out_later, "core", swap)
    spread = call(place_kernel, shape((2 * chips, feat_local, toks), BF16), flops=10_000_000_000)(back, slot)
    spread, in_other, out_other = lax.optimization_barrier((spread, in_other, out_other))
    x = lax.all_to_all(spread, ("x", "core"), split_axis=0, concat_axis=0, tiled=True)
    parts = call(layer_kernel, shape((chips, feat_local, toks), BF16))(
        x, gain, in_own, in_other, out_own, out_other
    )
    parts = lax.all_to_all(parts, "x", split_axis=0, concat_axis=0, tiled=True)
    return call(finish_kernel, shape((feat_local, toks), BF16))(parts, x)


def solution(mesh):
    fine = Mesh(mesh.devices.reshape(8, 12, 4, 2), ("y", "z", "x", "core"))
    seq, vocab = ("y", "z"), ("x", "core")
    in_specs = (P(seq), P(vocab, seq), P(), P(None, vocab), P(vocab, None))
    return jax.shard_map(
        on_device, mesh=fine, in_specs=in_specs, out_specs=P(vocab, seq), check_vma=False
    )
```

time: 91.4 us -> 85.9 us (0.940)
  the two profiles are of different devices: /device:TPU:1 before, /device:TPU:8 now
where the time goes in v8:
time: 85.9 us; the launch traced here: 85.5 us
  starting transfers between devices  32.6 us (38%)
  blocking collectives  22.7 us (26%)
  waiting for transfers between devices  21.6 us (25%)
  Pallas kernels  6.69 us (8%)
  local copies, waits for them, and re-layouts  1.83 us (2%)
    all_to_all x1, starting transfers between devices, on_device(): lax.all_to_all(outgoing, seq, split_axis=0, concat_axis=0, tiled=True)  21.8 us
    all_to_all x1, blocking collectives, on_device(): lax.all_to_all(spread, ('x', 'core'), split_axis=0, concat_axis=0, tiled=...  13.8 us
    all_to_all x1, waiting for transfers between devices, on_device(): lax.all_to_all(outgoing, seq, split_axis=0, concat_axis=0, tiled=True)  11.2 us
    all_to_all x1, waiting for transfers between devices, on_device(): back = lax.all_to_all(asked, seq, split_axis=0, concat_axis=0, tiled=True)  10.4 us
    all_to_all x1, blocking collectives, on_device(): parts = lax.all_to_all(parts, 'x', split_axis=0, concat_axis=0, tiled=True)  8.88 us
    all_to_all x1, starting transfers between devices, on_device(): back = lax.all_to_all(asked, seq, split_axis=0, concat_axis=0, tiled=True)  6.52 us
    ppermute x1, starting transfers between devices, on_device(): in_other = lax.ppermute(in_later, 'core', swap)  2.41 us
    ppermute x1, starting transfers between devices, on_device(): out_other = lax.ppermute(out_later, 'core', swap)  1.92 us
  transfers between devices with their start and end apart: 4, of which 2 were waited for; matrix products, arithmetic and copies ran while one was open for 0% of the time, Pallas kernels for 2%

profile of v8, /device:TPU:8, one launch (start us, length us, event | category | flops | bytes accessed | tf_op | source)
XLA Modules:
  0.0 85.5 jit_solution(16402110080092502642)
XLA Ops:
  0.0 0.0 copy-start.3
  0.0 0.7 copy-done.3
  0.7 1.0 %shard_map.55 = s32[96,1,8]{2,1,0:T(1,128)} custom-call(s32[1,256]{1,0:T(1,128)S(1)} %bitcast.4), custom_call_target="tpu_custom_call" | custom-call | tf_op jit(solution)/shard_map/pallas_call | solution.py:146
  1.7 21.8 %all-to-all-start = ((s32[96,1,8]{2,1,0:T(1,128)}), s32[96,1,8]{2,1,0:T(1,128)S(1)}, u32[]{:S(2)}, u32[]{:S(2)}) async-start(s32[96,1,8]{2,1,0:T(1,128)} %shard_map.55), calls=%async_computation | async-start | bytes 98304 | tf_op jit(solution)/shard_map/all_to_all | solution.py:147
  23.4 0.0 copy-start
  23.5 1.1 %copy-done = bf16[448,896]{1,0:T(8,128)(2,1)S(1)} copy-done((bf16[448,896]{1,0:T(8,128)(2,1)S(1)}, bf16[448,896]{1,0:T(8,128)(2,1)}, u32[]{:S(2)}) %copy-start) | copy-done | bytes 802840
  24.6 0.0 copy-start.4
  24.6 1.1 %shard_map.56 = (bf16[448,448]{1,0:T(8,128)(2,1)S(1)}, bf16[448,448]{1,0:T(8,128)(2,1)S(1)}, s32[1,256]{1,0:T(1,128)S(1)}, s32[8,128]{1,0:T(8,128)S(1)}) custom-call(bf16[448,896]{1,0:T(8,128)(2,1)S(1)} %copy-done, s32[1,256]{1,0:T(1,128)S(1)} %bitcast.5), custom_call_target="tpu_custom_call" | custom-call | tf_op jit(solution)/shard_map/pallas_call | solution.py:150
  25.8 11.2 %all-to-all-done.block_ref = s32[96,1,8]{2,1,0:T(1,128)S(1)} async-done(((s32[96,1,8]{2,1,0:T(1,128)}), s32[96,1,8]{2,1,0:T(1,128)S(1)}, u32[]{:S(2)}, u32[]{:S(2)}) %all-to-all-start) | async-done | bytes 3104 | tf_op jit(solution)/shard_map/all_to_all | solution.py:147
  37.0 0.0 copy-done.4
  37.0 0.0 copy-start.1
  37.0 1.9 %shard_map.57 = bf16[96,2,384]{2,1,0:T(2,128)(2,1)} custom-call(s32[96,1,8]{2,1,0:T(1,128)S(1)} %all-to-all-done.block_ref, bf16[112,1280]{1,0:T(8,128)(2,1)S(1)} %copy-done.4, s32[8,128]{1,0:T(8,128)S(1)} %get-tuple-element.14._), custom_call_target="tpu_custom_call" | custom-call | flops 10000000000 | tf_op jit(solution)/shard_map/pallas_call | solution.py:154
  38.8 6.5 %all-to-all-start.1 = ((bf16[96,2,384]{2,1,0:T(2,128)(2,1)}), bf16[96,2,384]{2,1,0:T(2,128)(2,1)S(1)}, u32[]{:S(2)}, u32[]{:S(2)}) async-start(bf16[96,2,384]{2,1,0:T(2,128)(2,1)} %shard_map.57), calls=%async_computation.1 | async-start | bytes 294912 | tf_op jit(solution)/shard_map/all_to_all | solution.py:161
  45.4 1.9 %collective-permute-start.1 = (bf16[448,448]{1,0:T(8,128)(2,1)S(1)}, bf16[448,448]{1,0:T(8,128)(2,1)S(1)}, u32[]{:S(2)}, u32[]{:S(2)}) collective-permute-start(bf16[448,448]{1,0:T(8,128)(2,1)S(1)} %get-tuple-element.18), channel_id=1, source_target_pairs={{0,1},{1,0},{2,3},{3,2},{4,5},{5,4},{6,7},{7,6},{8,9},{9,8},{10,11... | collective-permute-start | bytes 1204232 | tf_op jit(solution)/shard_map/ppermute | solution.py:165
  47.3 0.0 copy-done.1
  47.3 2.4 %collective-permute-start = (bf16[448,896]{1,0:T(8,128)(2,1)S(1)}, bf16[448,896]{1,0:T(8,128)(2,1)S(1)}, u32[]{:S(2)}, u32[]{:S(2)}) collective-permute-start(bf16[448,896]{1,0:T(8,128)(2,1)S(1)} %bitcast.2), channel_id=1, source_target_pairs={{0,1},{1,0},{2,3},{3,2},{4,5},{5,4},{6,7},{7,6},{8,9},{9,8},{10,11... | collective-permute-start | bytes 2408456 | tf_op jit(solution)/shard_map/ppermute | solution.py:164
  49.7 10.4 %all-to-all-done.1.back_ref = bf16[96,2,384]{2,1,0:T(2,128)(2,1)S(1)} async-done(((bf16[96,2,384]{2,1,0:T(2,128)(2,1)}), bf16[96,2,384]{2,1,0:T(2,128)(2,1)S(1)}, u32[]{:S(2)}, u32[]{:S(2)}) %all-to-all-start.1) | async-done | bytes 147488 | tf_op jit(solution)/shard_map/all_to_all | solution.py:161
  60.1 0.3 shard_map.58
  60.4 0.0 collective-permute-done.1.out_b
  60.4 0.0 collective-permute-done.in_b
  60.5 0.0 copy-start.2
  60.5 13.8 %all_to_all.20.x_ref = bf16[8,112,256]{2,1,0:T(8,128)(2,1)S(1)} all-to-all(bf16[8,112,256]{2,1,0:T(8,128)(2,1)S(1)} %shard_map.58), channel_id=1, replica_groups=mesh['y'=8,'z'=12,'x'=4,'core'=2] {'x','core'}, dimensions={0} | all-to-all | bytes 917504 | tf_op jit(solution)/shard_map/all_to_all | solution.py:168
  74.3 0.0 copy-done.2
  74.3 1.7 %shard_map.59 = bf16[4,112,256]{2,1,0:T(8,128)(2,1)S(1)} custom-call(bf16[8,112,256]{2,1,0:T(8,128)(2,1)S(1)} %all_to_all.20.x_ref, f32[896]{0:T(1024)S(1)} %copy-done.2, bf16[448,896]{1,0:T(8,128)(2,1)S(1)} %bitcast.3, bf16[448,896]{1,0:T(8,128)(2,1)S(1)} %collective-permute-done.in_b, bf16[448,448]{1,0:T(8,128)(2,1)S(1)} %get-tuple-element.21.out_a, ...), custom_call_target="tpu_custom_call" | custom-call | tf_op jit(solution)/shard_map/pallas_call | solution.py:169
  76.0 8.9 %all_to_all.21.parts_ref = bf16[4,112,256]{2,1,0:T(8,128)(2,1)S(1)} all-to-all(bf16[4,112,256]{2,1,0:T(8,128)(2,1)S(1)} %shard_map.59), channel_id=1, replica_groups=mesh['y'=8,'z'=12,'x'=4,'core'=2] {'x'}, dimensions={0} | all-to-all | bytes 458752 | tf_op jit(solution)/shard_map/all_to_all | solution.py:172
  84.9 0.7 shard_map.60
Async XLA Ops:
  0.0 0.7 copy-start.3
  1.7 35.3 %all-to-all-start = ((s32[96,1,8]{2,1,0:T(1,128)}), s32[96,1,8]{2,1,0:T(1,128)S(1)}, u32[]{:S(2)}, u32[]{:S(2)}) async-start(s32[96,1,8]{2,1,0:T(1,128)} %shard_map.55), calls=%async_computation | async-start | bytes 98304 | tf_op jit(solution)/shard_map/all_to_all | solution.py:147
  23.4 1.1 %copy-start = (bf16[448,896]{1,0:T(8,128)(2,1)S(1)}, bf16[448,896]{1,0:T(8,128)(2,1)}, u32[]{:S(2)}) copy-start(bf16[448,896]{1,0:T(8,128)(2,1)} %w_ref.1) | copy-start | bytes 2408452
  24.6 12.4 %copy-start.4 = (bf16[112,1280]{1,0:T(8,128)(2,1)S(1)}, bf16[112,1280]{1,0:T(8,128)(2,1)}, u32[]{:S(2)}) copy-start(bf16[112,1280]{1,0:T(8,128)(2,1)} %table_ref.1) | copy-start | bytes 860164
  37.0 10.3 %copy-start.1 = (bf16[896,448]{0,1:T(8,128)(2,1)S(1)}, bf16[896,448]{0,1:T(8,128)(2,1)}, u32[]{:S(2)}) copy-start(bf16[896,448]{0,1:T(8,128)(2,1)} %param.8) | copy-start | bytes 2408452
  38.8 21.3 %all-to-all-start.1 = ((bf16[96,2,384]{2,1,0:T(2,128)(2,1)}), bf16[96,2,384]{2,1,0:T(2,128)(2,1)S(1)}, u32[]{:S(2)}, u32[]{:S(2)}) async-start(bf16[96,2,384]{2,1,0:T(2,128)(2,1)} %shard_map.57), calls=%async_computation.1 | async-start | bytes 294912 | tf_op jit(solution)/shard_map/all_to_all | solution.py:161
  45.4 15.1 %collective-permute-start.1 = (bf16[448,448]{1,0:T(8,128)(2,1)S(1)}, bf16[448,448]{1,0:T(8,128)(2,1)S(1)}, u32[]{:S(2)}, u32[]{:S(2)}) collective-permute-start(bf16[448,448]{1,0:T(8,128)(2,1)S(1)} %get-tuple-element.18), channel_id=1, source_target_pairs={{0,1},{1,0},{2,3},{3,2},{4,5},{5,4},{6,7},{7,6},{8,9},{9,8},{10,11... | collective-permute-start | bytes 1204232 | tf_op jit(solution)/shard_map/ppermute | solution.py:165
  47.3 13.2 %collective-permute-start = (bf16[448,896]{1,0:T(8,128)(2,1)S(1)}, bf16[448,896]{1,0:T(8,128)(2,1)S(1)}, u32[]{:S(2)}, u32[]{:S(2)}) collective-permute-start(bf16[448,896]{1,0:T(8,128)(2,1)S(1)} %bitcast.2), channel_id=1, source_target_pairs={{0,1},{1,0},{2,3},{3,2},{4,5},{5,4},{6,7},{7,6},{8,9},{9,8},{10,11... | collective-permute-start | bytes 2408456 | tf_op jit(solution)/shard_map/ppermute | solution.py:164
  60.5 13.8 %copy-start.2 = (f32[896]{0:T(1024)S(1)}, f32[896]{0:T(1024)}, u32[]{:S(2)}) copy-start(f32[896]{0:T(1024)} %gain_ref.1) | copy-start | bytes 10756

commit v9 on v8

--- a/solution.py
+++ b/solution.py
@@ -48,25 +48,12 @@
     out_ref[:, 0, :] = out.astype(I32)
 
 
-def third(r, block, count):
-    return sum((r >= k * block).astype(I32) for k in range(1, count))
+def slot_kernel(owners, rows, ids_ref, slot_ref):
+    owner, _, rank, _ = ranked(ids_ref[...], owners, rows)
+    slot_ref[...] = owner * SLOTS + rank
 
 
-def blocks_kernel(owners, rows, chips, w_ref, ids_ref, keep_ref, send_ref, slot_ref, mark_ref):
-    mark_ref[...] = jnp.zeros_like(mark_ref)
-    owner, _, rank, _ = ranked(ids_ref[...], owners, rows)
-    slot_ref[...] = owner * SLOTS + rank
-    feats = w_ref.shape[1]
-    n = feats // 2
-    block = n // chips
-    core = lax.axis_index("core")
-    row, lane = iota((n, feats), 0), iota((n, feats), 1)
-    base = row + third(row, block, chips) * block
-    send_ref[...] = dot(hot(lane == base + (1 - core) * block), w_ref[...], 1, 1).astype(BF16)
-    keep_ref[...] = dot(hot(lane == base + core * block), w_ref[...], 1, 1).astype(BF16)
-
-
-def rows_kernel(block_ref, table_ref, _, out_ref, pick):
+def rows_kernel(block_ref, table_ref, out_ref, pick):
     sources = block_ref.shape[0]
     feats, rows = table_ref.shape
     n = sources * TALL
@@ -86,8 +73,8 @@
         out_ref[:, :, j * LANES:j * LANES + feats] = x[j * n:(j + 1) * n].reshape(sources, TALL, feats).astype(BF16)
 
 
-def layer_kernel(x_ref, gain_ref, in_a, in_b, out_a, out_b, part_ref):
-    feats = gain_ref.shape[0]
+def layer_kernel(x_ref, gain_ref, in_a, out_a, in_b, out_b, part_ref):
+    feats = in_a.shape[1]
     x = x_ref[...].reshape(feats, x_ref.shape[2]).astype(F32)
     gain = jnp.transpose(jnp.broadcast_to(gain_ref[...].reshape(1, feats), (8, feats)))[:, :1]
     scaled = (gain * x).astype(BF16)
@@ -96,12 +83,12 @@
     for w_in, w_out in ((in_a, out_a), (in_b, out_b)):
         pre = dot(w_in[...], scaled, 1, 0) * scale
         hidden = jax.nn.gelu(pre, approximate=True).astype(BF16)
-        total += dot(w_out[...], hidden, 1, 0)
-    part_ref[...] = total.astype(BF16).reshape(part_ref.shape)
+        total += dot(hidden, w_out[...], 0, 0)
+    part_ref[...] = jnp.transpose(total).astype(BF16).reshape(part_ref.shape)
 
 
-def place_kernel(back_ref, slot_ref, x_ref):
-    copies, feats, toks = x_ref.shape
+def place_kernel(back_ref, slot_ref, x_ref, own_ref):
+    feats, toks = own_ref.shape
     n = back_ref.shape[0] * TALL
     slot = slot_ref[...]
     owner, rank = slot // SLOTS, slot % SLOTS
@@ -111,15 +98,20 @@
         at = jnp.where(rank % WIDE == j, owner * TALL + rank // WIDE, -1)
         x += dot(back, hot(iota((n, toks), 0) == at), 0, 0)
     x = x.astype(BF16)
-    for i in range(copies):
-        x_ref[i] = x
+    own_ref[...] = x
+    part = toks // 2
+    for i in range(x_ref.shape[0]):
+        x_ref[i] = x[:, i % 2 * part:(i % 2 + 1) * part]
 
 
-def finish_kernel(parts_ref, x_ref, out_ref):
-    total = x_ref[2 * lax.axis_index("x") + lax.axis_index("core")].astype(F32)
-    for i in range(parts_ref.shape[0]):
-        total += parts_ref[i].astype(F32)
-    out_ref[...] = total.astype(BF16)
+def finish_kernel(parts_ref, own_ref, out_ref):
+    part = parts_ref.shape[2]
+    for core in range(2):
+        at = slice(core * part, (core + 1) * part)
+        total = own_ref[:, at].astype(F32)
+        for i in range(core, parts_ref.shape[0], 2):
+            total += parts_ref[i].astype(F32)
+        out_ref[:, at] = total.astype(BF16)
 
 
 def call(kernel, out_shape, scratch=(), vmem=32 * 1024 * 1024, flops=None, **more):
@@ -136,7 +128,7 @@
 def on_device(neighbour_ids, table_cols, gain, w_in, w_out):
     seq = ("y", "z")
     owners = lax.axis_size(seq)
-    chips = lax.axis_size("x")
+    vocab = 2 * lax.axis_size("x")
     feat_local, rows = table_cols.shape
     feats, half = w_in.shape
     toks = neighbour_ids.shape[0]
@@ -146,31 +138,28 @@
     outgoing = call(functools.partial(request_kernel, rows), shape((owners, 1, SLOTS), I32))(ids)
     block = lax.all_to_all(outgoing, seq, split_axis=0, concat_axis=0, tiled=True)
     swap = [(0, 1), (1, 0)]
-    anywhere, vmem = pl.BlockSpec(memory_space=pl.ANY), pl.BlockSpec(memory_space=pltpu.VMEM)
-    out_own, out_send, slot, mark = call(
-        functools.partial(blocks_kernel, owners, rows, chips),
-        (shape((feats // 2, half), BF16),) * 2 + (shape((1, toks), I32), shape((8, 128), I32)),
-    )(w_out, ids)
+    slot = call(functools.partial(slot_kernel, owners, rows), shape((1, toks), I32))(ids)
     asked = call(
         rows_kernel,
         shape((owners, TALL, WIDE * LANES), BF16),
         (pltpu.VMEM((owners * TALL * WIDE, rows), BF16),),
-        in_specs=[vmem, vmem, anywhere],
         flops=10_000_000_000,
-    )(block, table_cols, mark)
+    )(block, table_cols)
     back = lax.all_to_all(asked, seq, split_axis=0, concat_axis=0, tiled=True)
-    in_own = w_in.T
-    in_later, out_later, _ = lax.optimization_barrier((in_own, out_send, block))
-    in_other = lax.ppermute(in_later, "core", swap)
-    out_other = lax.ppermute(out_later, "core", swap)
-    spread = call(place_kernel, shape((2 * chips, feat_local, toks), BF16), flops=10_000_000_000)(back, slot)
-    spread, in_other, out_other = lax.optimization_barrier((spread, in_other, out_other))
+    weights = w_in.T, w_out
+    others = [lax.ppermute(w, "core", swap) for w in weights]
+    spread, own = call(
+        place_kernel,
+        (shape((vocab, feat_local, toks // 2), BF16), shape((feat_local, toks), BF16)),
+        flops=10_000_000_000,
+    )(back, slot)
+    spread, others = lax.optimization_barrier((spread, others))
     x = lax.all_to_all(spread, ("x", "core"), split_axis=0, concat_axis=0, tiled=True)
-    parts = call(layer_kernel, shape((chips, feat_local, toks), BF16))(
-        x, gain, in_own, in_other, out_own, out_other
+    parts = call(layer_kernel, shape((vocab, feat_local, toks // 2), BF16))(
+        x, gain, *weights, *others
     )
-    parts = lax.all_to_all(parts, "x", split_axis=0, concat_axis=0, tiled=True)
-    return call(finish_kernel, shape((feat_local, toks), BF16))(parts, x)
+    parts = lax.all_to_all(parts, ("x", "core"), split_axis=0, concat_axis=0, tiled=True)
+    return call(finish_kernel, shape((feat_local, toks), BF16))(parts, own)
 
 
 def solution(mesh):

time: 85.9 us -> 85.1 us (level)
  the two profiles are of different devices: /device:TPU:8 before, /device:TPU:1 now
where the time goes in v9:
time: 85.1 us; the launch traced here: 84.7 us
  blocking collectives  58.8 us (69%)
  starting transfers between devices  11.8 us (14%)
  waiting for transfers between devices  7.58 us (9%)
  Pallas kernels  4.74 us (6%)
  local copies, waits for them, and re-layouts  1.65 us (2%)
    all_to_all x1, blocking collectives, on_device(): lax.all_to_all(outgoing, seq, split_axis=0, concat_axis=0, tiled=True)  35.4 us
    all_to_all x1, blocking collectives, on_device(): lax.all_to_all(spread, ('x', 'core'), split_axis=0, concat_axis=0, tiled=...  13.8 us
    all_to_all x1, blocking collectives, on_device(): lax.all_to_all(parts, ('x', 'core'), split_axis=0, concat_axis=0, tiled=T...  9.6 us
    all_to_all x1, waiting for transfers between devices, on_device(): back = lax.all_to_all(asked, seq, split_axis=0, concat_axis=0, tiled=True)  7.57 us
    ppermute x2, starting transfers between devices, on_device(): others = [lax.ppermute(w, 'core', swap) for w in weights]  5.94 us
    all_to_all x1, starting transfers between devices, on_device(): back = lax.all_to_all(asked, seq, split_axis=0, concat_axis=0, tiled=True)  5.91 us
    pallas_call x1, Pallas kernels, on_device(): call(rows_kernel, shape((owners, TALL, WIDE * LANES), BF16), (pltpu.VMEM(...  1.87 us
  transfers between devices with their start and end apart: 3, of which 1 were waited for; matrix products, arithmetic and copies ran while one was open for 0% of the time, Pallas kernels for 1%

profile of v9, /device:TPU:1, one launch (start us, length us, event | category | flops | bytes accessed | tf_op | source)
XLA Modules:
  0.0 84.7 jit_solution(18055618473124662297)
XLA Ops:
  0.0 0.0 copy-start.2
  0.0 0.7 copy-done.2
  0.7 0.4 shard_map.55
  1.1 35.4 %all_to_all.20.block_ref = s32[96,1,8]{2,1,0:T(1,128)S(1)} all-to-all(s32[96,1,8]{2,1,0:T(1,128)S(1)} %shard_map.55), channel_id=1, replica_groups=mesh['y'=8,'z'=12,'x'=4,'core'=2] {'y','z'}, dimensions={0} | all-to-all | bytes 6144 | tf_op jit(solution)/shard_map/all_to_all | solution.py:139
  36.5 0.0 copy-start.4
  36.5 1.0 %copy-done.4 = bf16[112,1280]{1,0:T(8,128)(2,1)S(1)} copy-done((bf16[112,1280]{1,0:T(8,128)(2,1)S(1)}, bf16[112,1280]{1,0:T(8,128)(2,1)}, u32[]{:S(2)}) %copy-start.4) | copy-done | bytes 286744
  37.4 0.0 copy-start
  37.4 0.0 copy-start.1
  37.4 1.9 %shard_map.56 = bf16[96,2,384]{2,1,0:T(2,128)(2,1)} custom-call(s32[96,1,8]{2,1,0:T(1,128)S(1)} %all_to_all.20.block_ref, bf16[112,1280]{1,0:T(8,128)(2,1)S(1)} %copy-done.4), custom_call_target="tpu_custom_call" | custom-call | flops 10000000000 | tf_op jit(solution)/shard_map/pallas_call | solution.py:142
  39.3 5.9 %all-to-all-start.1 = ((bf16[96,2,384]{2,1,0:T(2,128)(2,1)}), bf16[96,2,384]{2,1,0:T(2,128)(2,1)S(1)}, u32[]{:S(2)}, u32[]{:S(2)}) async-start(bf16[96,2,384]{2,1,0:T(2,128)(2,1)} %shard_map.56), calls=%async_computation.1 | async-start | bytes 294912 | tf_op jit(solution)/shard_map/all_to_all | solution.py:148
  45.2 0.0 copy-done
  45.2 4.0 %collective-permute-start = (bf16[448,896]{1,0:T(8,128)(2,1)S(1)}, bf16[448,896]{1,0:T(8,128)(2,1)S(1)}, u32[]{:S(2)}, u32[]{:S(2)}) collective-permute-start(bf16[448,896]{1,0:T(8,128)(2,1)S(1)} %bitcast.2), channel_id=1, source_target_pairs={{0,1},{1,0},{2,3},{3,2},{4,5},{5,4},{6,7},{7,6},{8,9},{9,8},{10,11... | collective-permute-start | bytes 2408456 | tf_op jit(solution)/shard_map/ppermute | solution.py:150
  49.2 0.0 copy-done.1
  49.3 1.9 %collective-permute-start.1 = (bf16[448,896]{1,0:T(8,128)(2,1)S(1)}, bf16[448,896]{1,0:T(8,128)(2,1)S(1)}, u32[]{:S(2)}, u32[]{:S(2)}) collective-permute-start(bf16[448,896]{1,0:T(8,128)(2,1)S(1)} %copy-done.1), channel_id=1, source_target_pairs={{0,1},{1,0},{2,3},{3,2},{4,5},{5,4},{6,7},{7,6},{8,9},{9,8},{10,11... | collective-permute-start | bytes 2408456 | tf_op jit(solution)/shard_map/ppermute | solution.py:150
  51.2 0.2 shard_map.57.slot_ref
  51.4 7.6 %all-to-all-done.1.back_ref = bf16[96,2,384]{2,1,0:T(2,128)(2,1)S(1)} async-done(((bf16[96,2,384]{2,1,0:T(2,128)(2,1)}), bf16[96,2,384]{2,1,0:T(2,128)(2,1)S(1)}, u32[]{:S(2)}, u32[]{:S(2)}) %all-to-all-start.1) | async-done | bytes 147488 | tf_op jit(solution)/shard_map/all_to_all | solution.py:148
  58.9 0.3 shard_map.58
  59.2 0.0 collective-permute-done.in_b
  59.3 0.0 collective-permute-done.1.out_b
  59.3 0.0 copy-start.3
  59.3 13.8 %all_to_all.21.x_ref = bf16[8,112,128]{2,1,0:T(8,128)(2,1)S(1)} all-to-all(bf16[8,112,128]{2,1,0:T(8,128)(2,1)S(1)} %get-tuple-element.11), channel_id=1, replica_groups=mesh['y'=8,'z'=12,'x'=4,'core'=2] {'x','core'}, dimensions={0} | all-to-all | bytes 458752 | tf_op jit(solution)/shard_map/all_to_all | solution.py:157
  73.0 0.0 copy-done.3
  73.0 1.4 %shard_map.59 = bf16[8,112,128]{2,1,0:T(8,128)(2,1)S(1)} custom-call(bf16[8,112,128]{2,1,0:T(8,128)(2,1)S(1)} %all_to_all.21.x_ref, f32[896]{0:T(1024)S(1)} %copy-done.3, bf16[448,896]{1,0:T(8,128)(2,1)S(1)} %bitcast.3, bf16[448,896]{1,0:T(8,128)(2,1)S(1)} %copy-done.1, bf16[448,896]{1,0:T(8,128)(2,1)S(1)} %collective-permute-done.in_b, ...), custom_call_target="tpu_custom_call" | custom-call | tf_op jit(solution)/shard_map/pallas_call | solution.py:158
  74.4 9.6 %all_to_all.22.parts_ref = bf16[8,112,128]{2,1,0:T(8,128)(2,1)S(1)} all-to-all(bf16[8,112,128]{2,1,0:T(8,128)(2,1)S(1)} %shard_map.59), channel_id=1, replica_groups=mesh['y'=8,'z'=12,'x'=4,'core'=2] {'x','core'}, dimensions={0} | all-to-all | bytes 458752 | tf_op jit(solution)/shard_map/all_to_all | solution.py:161
  84.0 0.7 shard_map.60
Async XLA Ops:
  0.0 0.7 copy-start.2
  36.5 1.0 %copy-start.4 = (bf16[112,1280]{1,0:T(8,128)(2,1)S(1)}, bf16[112,1280]{1,0:T(8,128)(2,1)}, u32[]{:S(2)}) copy-start(bf16[112,1280]{1,0:T(8,128)(2,1)} %table_ref.1) | copy-start | bytes 860164
  37.4 7.8 %copy-start = (bf16[896,448]{0,1:T(8,128)(2,1)S(1)}, bf16[896,448]{0,1:T(8,128)(2,1)}, u32[]{:S(2)}) copy-start(bf16[896,448]{0,1:T(8,128)(2,1)} %param.8) | copy-start | bytes 2408452
  37.4 11.8 %copy-start.1 = (bf16[448,896]{1,0:T(8,128)(2,1)S(1)}, bf16[448,896]{1,0:T(8,128)(2,1)}, u32[]{:S(2)}) copy-start(bf16[448,896]{1,0:T(8,128)(2,1)} %out_a.1) | copy-start | bytes 2408452
  39.3 19.6 %all-to-all-start.1 = ((bf16[96,2,384]{2,1,0:T(2,128)(2,1)}), bf16[96,2,384]{2,1,0:T(2,128)(2,1)S(1)}, u32[]{:S(2)}, u32[]{:S(2)}) async-start(bf16[96,2,384]{2,1,0:T(2,128)(2,1)} %shard_map.56), calls=%async_computation.1 | async-start | bytes 294912 | tf_op jit(solution)/shard_map/all_to_all | solution.py:148
  45.2 14.0 %collective-permute-start = (bf16[448,896]{1,0:T(8,128)(2,1)S(1)}, bf16[448,896]{1,0:T(8,128)(2,1)S(1)}, u32[]{:S(2)}, u32[]{:S(2)}) collective-permute-start(bf16[448,896]{1,0:T(8,128)(2,1)S(1)} %bitcast.2), channel_id=1, source_target_pairs={{0,1},{1,0},{2,3},{3,2},{4,5},{5,4},{6,7},{7,6},{8,9},{9,8},{10,11... | collective-permute-start | bytes 2408456 | tf_op jit(solution)/shard_map/ppermute | solution.py:150
  49.3 10.0 %collective-permute-start.1 = (bf16[448,896]{1,0:T(8,128)(2,1)S(1)}, bf16[448,896]{1,0:T(8,128)(2,1)S(1)}, u32[]{:S(2)}, u32[]{:S(2)}) collective-permute-start(bf16[448,896]{1,0:T(8,128)(2,1)S(1)} %copy-done.1), channel_id=1, source_target_pairs={{0,1},{1,0},{2,3},{3,2},{4,5},{5,4},{6,7},{7,6},{8,9},{9,8},{10,11... | collective-permute-start | bytes 2408456 | tf_op jit(solution)/shard_map/ppermute | solution.py:150
  59.3 13.8 %copy-start.3 = (f32[896]{0:T(1024)S(1)}, f32[896]{0:T(1024)}, u32[]{:S(2)}) copy-start(f32[896]{0:T(1024)} %gain_ref.1) | copy-start | bytes 10756

commit v10 on v9

--- a/solution.py
+++ b/solution.py
@@ -53,24 +53,32 @@
     slot_ref[...] = owner * SLOTS + rank
 
 
-def rows_kernel(block_ref, table_ref, out_ref, pick):
+def rows_kernel(block_ref, table_ref, out_ref, pick, sides):
     sources = block_ref.shape[0]
     feats, rows = table_ref.shape
+    part = rows // 2
     n = sources * TALL
+    sides[...] = jnp.zeros_like(sides)
+    for i in range(2):
+        sides[i * LANES:i * LANES + feats] = table_ref[:, i * part:(i + 1) * part]
     code = block_ref[:, 0, :]
     spread = hot(iota((n, sources), 0) // TALL == iota((n, sources), 1))
     high = (code // SPLIT).astype(F32).astype(BF16)
     low = (code % SPLIT).astype(F32).astype(BF16)
     wide = dot(spread, high, 1, 0) * SPLIT + dot(spread, low, 1, 0)
     row, slot = iota((n, SLOTS), 0) % TALL, iota((n, SLOTS), 1)
-    lane = iota((n, rows), 1)
+    lane = iota((n, part), 1)
+    later = []
     for j in range(WIDE):
         local = jnp.sum(jnp.where(slot == row * WIDE + j, wide, 0.0), axis=1, keepdims=True).astype(I32) - 1
-        pick[j * n:(j + 1) * n] = hot(lane == local)
+        later.append(local >= part)
+        pick[j * n:(j + 1) * n] = hot(lane == jnp.where(later[j], local - part, local))
     out_ref[...] = jnp.zeros_like(out_ref)
-    x = dot(pick[...], table_ref[...], 1, 1)
+    x = dot(pick[...], sides[...], 1, 1)
     for j in range(WIDE):
-        out_ref[:, :, j * LANES:j * LANES + feats] = x[j * n:(j + 1) * n].reshape(sources, TALL, feats).astype(BF16)
+        mine = x[j * n:(j + 1) * n]
+        mine = jnp.where(later[j], mine[:, LANES:LANES + feats], mine[:, :feats])
+        out_ref[:, :, j * LANES:j * LANES + feats] = mine.reshape(sources, TALL, feats).astype(BF16)
 
 
 def layer_kernel(x_ref, gain_ref, in_a, out_a, in_b, out_b, part_ref):
@@ -142,7 +150,7 @@
     asked = call(
         rows_kernel,
         shape((owners, TALL, WIDE * LANES), BF16),
-        (pltpu.VMEM((owners * TALL * WIDE, rows), BF16),),
+        (pltpu.VMEM((owners * TALL * WIDE, rows // 2), BF16), pltpu.VMEM((2 * LANES, rows // 2), BF16)),
         flops=10_000_000_000,
     )(block, table_cols)
     back = lax.all_to_all(asked, seq, split_axis=0, concat_axis=0, tiled=True)

time: 85.1 us -> 85 us (level)
  no operation moved by 1% of the time
where the time goes in v10:
time: 85 us; the launch traced here: 84.6 us
  blocking collectives  58.8 us (69%)
  starting transfers between devices  11.8 us (14%)
  waiting for transfers between devices  7.58 us (9%)
  Pallas kernels  4.68 us (6%)
  local copies, waits for them, and re-layouts  1.65 us (2%)
    all_to_all x1, blocking collectives, on_device(): lax.all_to_all(outgoing, seq, split_axis=0, concat_axis=0, tiled=True)  35.4 us
    all_to_all x1, blocking collectives, on_device(): lax.all_to_all(spread, ('x', 'core'), split_axis=0, concat_axis=0, tiled=...  13.8 us
    all_to_all x1, blocking collectives, on_device(): lax.all_to_all(parts, ('x', 'core'), split_axis=0, concat_axis=0, tiled=T...  9.59 us
    all_to_all x1, waiting for transfers between devices, on_device(): back = lax.all_to_all(asked, seq, split_axis=0, concat_axis=0, tiled=True)  7.57 us
    ppermute x2, starting transfers between devices, on_device(): others = [lax.ppermute(w, 'core', swap) for w in weights]  5.93 us
    all_to_all x1, starting transfers between devices, on_device(): back = lax.all_to_all(asked, seq, split_axis=0, concat_axis=0, tiled=True)  5.91 us
    pallas_call x1, Pallas kernels, on_device(): call(rows_kernel, shape((owners, TALL, WIDE * LANES), BF16), (pltpu.VMEM(...  1.81 us
  transfers between devices with their start and end apart: 3, of which 1 were waited for; matrix products, arithmetic and copies ran while one was open for 0% of the time, Pallas kernels for 1%

profile of v10, /device:TPU:1, one launch (start us, length us, event | category | flops | bytes accessed | tf_op | source)
XLA Modules:
  0.0 84.6 jit_solution(16548979862007120591)
XLA Ops:
  0.0 0.0 copy-start.2
  0.0 0.7 copy-done.2
  0.7 0.4 shard_map.55
  1.1 35.4 %all_to_all.20.block_ref = s32[96,1,8]{2,1,0:T(1,128)S(1)} all-to-all(s32[96,1,8]{2,1,0:T(1,128)S(1)} %shard_map.55), channel_id=1, replica_groups=mesh['y'=8,'z'=12,'x'=4,'core'=2] {'y','z'}, dimensions={0} | all-to-all | bytes 6144 | tf_op jit(solution)/shard_map/all_to_all | solution.py:147
  36.5 0.0 copy-start.4
  36.5 1.0 %copy-done.4 = bf16[112,1280]{1,0:T(8,128)(2,1)S(1)} copy-done((bf16[112,1280]{1,0:T(8,128)(2,1)S(1)}, bf16[112,1280]{1,0:T(8,128)(2,1)}, u32[]{:S(2)}) %copy-start.4) | copy-done | bytes 286744
  37.4 0.0 copy-start
  37.4 0.0 copy-start.1
  37.4 1.8 %shard_map.56 = bf16[96,2,384]{2,1,0:T(2,128)(2,1)} custom-call(s32[96,1,8]{2,1,0:T(1,128)S(1)} %all_to_all.20.block_ref, bf16[112,1280]{1,0:T(8,128)(2,1)S(1)} %copy-done.4), custom_call_target="tpu_custom_call" | custom-call | flops 10000000000 | tf_op jit(solution)/shard_map/pallas_call | solution.py:150
  39.2 5.9 %all-to-all-start.1 = ((bf16[96,2,384]{2,1,0:T(2,128)(2,1)}), bf16[96,2,384]{2,1,0:T(2,128)(2,1)S(1)}, u32[]{:S(2)}, u32[]{:S(2)}) async-start(bf16[96,2,384]{2,1,0:T(2,128)(2,1)} %shard_map.56), calls=%async_computation.1 | async-start | bytes 294912 | tf_op jit(solution)/shard_map/all_to_all | solution.py:156
  45.2 0.0 copy-done
  45.2 4.0 %collective-permute-start = (bf16[448,896]{1,0:T(8,128)(2,1)S(1)}, bf16[448,896]{1,0:T(8,128)(2,1)S(1)}, u32[]{:S(2)}, u32[]{:S(2)}) collective-permute-start(bf16[448,896]{1,0:T(8,128)(2,1)S(1)} %bitcast.2), channel_id=1, source_target_pairs={{0,1},{1,0},{2,3},{3,2},{4,5},{5,4},{6,7},{7,6},{8,9},{9,8},{10,11... | collective-permute-start | bytes 2408456 | tf_op jit(solution)/shard_map/ppermute | solution.py:158
  49.2 0.0 copy-done.1
  49.2 1.9 %collective-permute-start.1 = (bf16[448,896]{1,0:T(8,128)(2,1)S(1)}, bf16[448,896]{1,0:T(8,128)(2,1)S(1)}, u32[]{:S(2)}, u32[]{:S(2)}) collective-permute-start(bf16[448,896]{1,0:T(8,128)(2,1)S(1)} %copy-done.1), channel_id=1, source_target_pairs={{0,1},{1,0},{2,3},{3,2},{4,5},{5,4},{6,7},{7,6},{8,9},{9,8},{10,11... | collective-permute-start | bytes 2408456 | tf_op jit(solution)/shard_map/ppermute | solution.py:158
  51.1 0.2 shard_map.57.slot_ref
  51.3 7.6 %all-to-all-done.1.back_ref = bf16[96,2,384]{2,1,0:T(2,128)(2,1)S(1)} async-done(((bf16[96,2,384]{2,1,0:T(2,128)(2,1)}), bf16[96,2,384]{2,1,0:T(2,128)(2,1)S(1)}, u32[]{:S(2)}, u32[]{:S(2)}) %all-to-all-start.1) | async-done | bytes 147488 | tf_op jit(solution)/shard_map/all_to_all | solution.py:156
  58.9 0.3 shard_map.58
  59.2 0.0 collective-permute-done.in_b
  59.2 0.0 collective-permute-done.1.out_b
  59.2 0.0 copy-start.3
  59.2 13.8 %all_to_all.21.x_ref = bf16[8,112,128]{2,1,0:T(8,128)(2,1)S(1)} all-to-all(bf16[8,112,128]{2,1,0:T(8,128)(2,1)S(1)} %get-tuple-element.11), channel_id=1, replica_groups=mesh['y'=8,'z'=12,'x'=4,'core'=2] {'x','core'}, dimensions={0} | all-to-all | bytes 458752 | tf_op jit(solution)/shard_map/all_to_all | solution.py:165
  73.0 0.0 copy-done.3
  73.0 1.4 %shard_map.59 = bf16[8,112,128]{2,1,0:T(8,128)(2,1)S(1)} custom-call(bf16[8,112,128]{2,1,0:T(8,128)(2,1)S(1)} %all_to_all.21.x_ref, f32[896]{0:T(1024)S(1)} %copy-done.3, bf16[448,896]{1,0:T(8,128)(2,1)S(1)} %bitcast.3, bf16[448,896]{1,0:T(8,128)(2,1)S(1)} %copy-done.1, bf16[448,896]{1,0:T(8,128)(2,1)S(1)} %collective-permute-done.in_b, ...), custom_call_target="tpu_custom_call" | custom-call | tf_op jit(solution)/shard_map/pallas_call | solution.py:166
  74.4 9.6 %all_to_all.22.parts_ref = bf16[8,112,128]{2,1,0:T(8,128)(2,1)S(1)} all-to-all(bf16[8,112,128]{2,1,0:T(8,128)(2,1)S(1)} %shard_map.59), channel_id=1, replica_groups=mesh['y'=8,'z'=12,'x'=4,'core'=2] {'x','core'}, dimensions={0} | all-to-all | bytes 458752 | tf_op jit(solution)/shard_map/all_to_all | solution.py:169
  83.9 0.7 shard_map.60
Async XLA Ops:
  0.0 0.7 copy-start.2
  36.5 1.0 %copy-start.4 = (bf16[112,1280]{1,0:T(8,128)(2,1)S(1)}, bf16[112,1280]{1,0:T(8,128)(2,1)}, u32[]{:S(2)}) copy-start(bf16[112,1280]{1,0:T(8,128)(2,1)} %table_ref.1) | copy-start | bytes 860164
  37.4 7.7 %copy-start = (bf16[896,448]{0,1:T(8,128)(2,1)S(1)}, bf16[896,448]{0,1:T(8,128)(2,1)}, u32[]{:S(2)}) copy-start(bf16[896,448]{0,1:T(8,128)(2,1)} %param.8) | copy-start | bytes 2408452
  37.4 11.8 %copy-start.1 = (bf16[448,896]{1,0:T(8,128)(2,1)S(1)}, bf16[448,896]{1,0:T(8,128)(2,1)}, u32[]{:S(2)}) copy-start(bf16[448,896]{1,0:T(8,128)(2,1)} %out_a.1) | copy-start | bytes 2408452
  39.2 19.6 %all-to-all-start.1 = ((bf16[96,2,384]{2,1,0:T(2,128)(2,1)}), bf16[96,2,384]{2,1,0:T(2,128)(2,1)S(1)}, u32[]{:S(2)}, u32[]{:S(2)}) async-start(bf16[96,2,384]{2,1,0:T(2,128)(2,1)} %shard_map.56), calls=%async_computation.1 | async-start | bytes 294912 | tf_op jit(solution)/shard_map/all_to_all | solution.py:156
  45.2 14.0 %collective-permute-start = (bf16[448,896]{1,0:T(8,128)(2,1)S(1)}, bf16[448,896]{1,0:T(8,128)(2,1)S(1)}, u32[]{:S(2)}, u32[]{:S(2)}) collective-permute-start(bf16[448,896]{1,0:T(8,128)(2,1)S(1)} %bitcast.2), channel_id=1, source_target_pairs={{0,1},{1,0},{2,3},{3,2},{4,5},{5,4},{6,7},{7,6},{8,9},{9,8},{10,11... | collective-permute-start | bytes 2408456 | tf_op jit(solution)/shard_map/ppermute | solution.py:158
  49.2 10.0 %collective-permute-start.1 = (bf16[448,896]{1,0:T(8,128)(2,1)S(1)}, bf16[448,896]{1,0:T(8,128)(2,1)S(1)}, u32[]{:S(2)}, u32[]{:S(2)}) collective-permute-start(bf16[448,896]{1,0:T(8,128)(2,1)S(1)} %copy-done.1), channel_id=1, source_target_pairs={{0,1},{1,0},{2,3},{3,2},{4,5},{5,4},{6,7},{7,6},{8,9},{9,8},{10,11... | collective-permute-start | bytes 2408456 | tf_op jit(solution)/shard_map/ppermute | solution.py:158
  59.2 13.8 %copy-start.3 = (f32[896]{0:T(1024)S(1)}, f32[896]{0:T(1024)}, u32[]{:S(2)}) copy-start(f32[896]{0:T(1024)} %gain_ref.1) | copy-start | bytes 10756
